TPU v7x, 32 devices: a whole 2x2x4 slice. The times are simulated.
32 devices in a mesh: dp: 8 (over y, x, core), head: 4 (over z).
Axes of the slice: x: 2, y: 2, z: 4, core: 2. Of those that a mesh axis runs over, the one named last changes fastest.
Arguments:
- tokens: bfloat16 [8192, 768], P('dp'), may hold values from -6 to 6
- memory: bfloat16 [16, 2048, 768], P(None, ('dp', 'head')), may hold values from -6 to 6
- cotangent: bfloat16 [8192, 768], P('dp'), may hold values from -6 to 6
- lengths: int32 [64], P('dp'), may hold values from 0 to 1024, as said below
- groups: int32 [64], P('dp'), may hold values from 0 to 2
- image_map: int32 [64], P('dp'), may hold values from 0 to 15, as said below
- entry_weights: float32 [6, 768, 768], P(None, 'dp', 'head'), may hold values from -0.21875 to 0.21875
- exit_weights: float32 [2, 768, 768], P(None, 'head', 'dp'), may hold values from -1 to 1
- expand_weights: float32 [2, 768, 2048], P(None, 'dp', 'head'), may hold values from -0.21875 to 0.21875
- contract_weights: float32 [2048, 768], P('head', 'dp'), may hold values from -0.125 to 0.125
- norm_gains: float32 [3, 768], P(None, 'dp'), may hold values from 0.4 to 2.4
- entry_first: float32 [6, 768, 768], P(None, 'dp', 'head'), may hold values from -112 to 112
- entry_second: float32 [6, 768, 768], P(None, 'dp', 'head'), may hold values from 24.576 to 98.304
- exit_first: float32 [2, 768, 768], P(None, 'head', 'dp'), may hold values from -14 to 14
- exit_second: float32 [2, 768, 768], P(None, 'head', 'dp'), may hold values from 0.385024 to 1.55648
- expand_first: float32 [2, 768, 2048], P(None, 'dp', 'head'), may hold values from -32 to 32
- expand_second: float32 [2, 768, 2048], P(None, 'dp', 'head'), may hold values from 2.21184 to 8.84736
- contract_first: float32 [2048, 768], P('head', 'dp'), may hold values from -40 to 40
- contract_second: float32 [2048, 768], P('head', 'dp'), may hold values from 4.42368 to 18.0224
- gains_first: float32 [3, 768], P(None, 'dp'), may hold values from -160 to 160
- gains_second: float32 [3, 768], P(None, 'dp'), may hold values from 55.296 to 221.184
Outputs:
- output: float32 [8192, 768], P('dp')
- token_grads: float32 [8192, 768], P('dp')
- memory_grads: float32 [16, 2048, 768], P(None, ('dp', 'head'))
- entry_grads: float32 [6, 768, 768], P(None, 'dp', 'head')
- exit_grads: float32 [2, 768, 768], P(None, 'head', 'dp')
- expand_grads: float32 [2, 768, 2048], P(None, 'dp', 'head')
- contract_grads: float32 [2048, 768], P('head', 'dp')
- gain_grads: float32 [3, 768], P(None, 'dp')
- entry_mean: float32 [6, 768, 768], P(None, 'dp', 'head')
- exit_mean: float32 [2, 768, 768], P(None, 'head', 'dp')
- expand_mean: float32 [2, 768, 2048], P(None, 'dp', 'head')
- contract_mean: float32 [2048, 768], P('head', 'dp')
- gains_mean: float32 [3, 768], P(None, 'dp')
- entry_square: float32 [6, 768, 768], P(None, 'dp', 'head')
- exit_square: float32 [2, 768, 768], P(None, 'head', 'dp')
- expand_square: float32 [2, 768, 2048], P(None, 'dp', 'head')
- contract_square: float32 [2048, 768], P('head', 'dp')
- gains_square: float32 [3, 768], P(None, 'dp')
- entry_new: float32 [6, 768, 768], P(None, 'dp', 'head')
- exit_new: float32 [2, 768, 768], P(None, 'head', 'dp')
- expand_new: float32 [2, 768, 2048], P(None, 'dp', 'head')
- contract_new: float32 [2048, 768], P('head', 'dp')
- gains_new: float32 [3, 768], P(None, 'dp')
- entry_copy: bfloat16 [6, 768, 768], P(None, 'dp', 'head')
- exit_copy: bfloat16 [2, 768, 768], P(None, 'head', 'dp')
- expand_copy: bfloat16 [2, 768, 2048], P(None, 'dp', 'head')
- contract_copy: bfloat16 [2048, 768], P('head', 'dp')
- trust_norms: float32 [2, 14], replicated
Inputs may be any that keep to these rules, and one draw needn't show every extreme that they name: Each dp group's 8 lengths sum to at most 1024; entries may be 0; in every draw some group holds a single text of 1024 tokens. `image_map`: A text of dp group i reads one of images i * 2 to (i + 1) * 2 - 1, and each of these is read by exactly 4 texts of the group.
All inputs are finite; a program needn't handle non-finite values.
Results may differ from a plain program's by a relative error of at most 0.025.
The roundings to bfloat16 on the way count: a program that leaves them out, or rounds other values in their place, can miss the bound.
Values may be sent and summed in bfloat16 or wider, within the bound.
No kernel may reach another device: no remote copies, remote signals or barrier semaphores. Data moves between devices by JAX's collectives and lax.ppermute only.
A program may use at most 192 MiB of HBM per device.

v0:
```python
import jax
import jax.numpy as jnp
from jax import lax
from jax.sharding import PartitionSpec as P

HEAD_DIM = 64
IMG_DEV = 2
STEPS_DONE = 10


group_scale = (1.0, 0.5, 2.0)
first_decay = 0.9
second_decay = 0.999
learn_rate = 0.5
weight_decay = 0.01
adam_eps = 1e-06
norm_eps = 1e-06
masked_score = -1e30


def token_layout(lengths, groups, image_map, tok_rows, img_count):
    text_count = lengths.shape[1]
    text_ends = jnp.cumsum(lengths, axis=1)
    position = jnp.arange(tok_rows, dtype=jnp.int32)
    segment = jnp.sum((position[None, :, None] >= text_ends[:, None, :]).astype(jnp.int32), axis=2)
    chosen = (segment[:, :, None] == jnp.arange(text_count, dtype=jnp.int32)[None, None, :]).astype(
        jnp.int32
    )
    group_tok = jnp.sum(chosen * groups[:, None, :], axis=2)
    image_tok = jnp.sum(chosen * (image_map % img_count)[:, None, :], axis=2)
    scale_table = jnp.array(group_scale, dtype=jnp.float32)
    picked = (group_tok[:, :, None] == jnp.arange(3, dtype=jnp.int32)[None, None, :]).astype(
        jnp.float32
    )
    weight_tok = jnp.sum(picked * scale_table, axis=2) * (segment < text_count).astype(jnp.float32)
    return (segment, image_tok, weight_tok)


def rms_norm(values, gain):
    return values * lax.rsqrt(jnp.mean(values * values, axis=-1, keepdims=True) + norm_eps) * gain


def gated_hidden(gate, upward):
    return jax.nn.gelu(gate, approximate=True) * upward


def head_total(partial_value):
    return lax.psum(partial_value, "head")


def split_items(array, block_rows):
    row_count, head_count, head_width = array.shape
    block_count = row_count // block_rows
    return (
        array.reshape(block_count, block_rows, head_count, head_width)
        .transpose(2, 0, 1, 3)
        .reshape(head_count * block_count, block_rows, head_width)
    )


def join_items(items, head_count, row_count):
    block_rows = items.shape[1]
    head_width = items.shape[2]
    block_count = row_count // block_rows
    return (
        items.reshape(head_count, block_count, block_rows, head_width)
        .transpose(1, 2, 0, 3)
        .reshape(row_count, head_count, head_width)
    )


def attend_forward(queries, key_rows, value_rows, mask_rule, block_rows):
    row_count, head_count, head_width = queries.shape
    block_count = row_count // block_rows
    score_scale = head_width ** (-0.5)
    query_items = split_items(queries, block_rows)
    key_heads = key_rows.transpose(1, 0, 2)
    value_heads = value_rows.transpose(1, 0, 2)

    def single(item_index):
        head_index = item_index // block_count
        row_start = item_index % block_count * block_rows
        scores = (
            jnp.einsum(
                "re,ke->rk",
                query_items[item_index],
                key_heads[head_index],
                preferred_element_type=jnp.float32,
            )
            * score_scale
        )
        scores = jnp.where(mask_rule(row_start, block_rows), scores, masked_score)
        largest = jnp.max(scores, axis=1, keepdims=True)
        exponent = jnp.exp(scores - largest)
        row_total = jnp.sum(exponent, axis=1, keepdims=True)
        weights = (exponent / row_total).astype(jnp.bfloat16)
        result = jnp.einsum(
            "rk,ke->re", weights, value_heads[head_index], preferred_element_type=jnp.float32
        )
        return (result, largest[:, 0] + jnp.log(row_total[:, 0]))

    results, log_sums = lax.map(single, jnp.arange(head_count * block_count))
    return (join_items(results, head_count, row_count), log_sums)


def attend_backward(queries, key_rows, value_rows, mask_rule, block_rows, log_sums, grad_out):
    row_count, head_count, head_width = queries.shape
    block_count = row_count // block_rows
    key_count = key_rows.shape[0]
    score_scale = head_width ** (-0.5)
    query_items = split_items(queries, block_rows)
    grad_items = split_items(grad_out, block_rows)
    key_heads = key_rows.transpose(1, 0, 2)
    value_heads = value_rows.transpose(1, 0, 2)

    def single(item_index):
        head_index = item_index // block_count
        row_start = item_index % block_count * block_rows
        query_set = query_items[item_index]
        grad_set = grad_items[item_index]
        key_set = key_heads[head_index]
        scores = (
            jnp.einsum("re,ke->rk", query_set, key_set, preferred_element_type=jnp.float32)
            * score_scale
        )
        scores = jnp.where(mask_rule(row_start, block_rows), scores, masked_score)
        probs = jnp.exp(scores - log_sums[item_index][:, None])
        grad_probs = jnp.einsum(
            "re,ke->rk", grad_set, value_heads[head_index], preferred_element_type=jnp.float32
        )
        inner = jnp.sum(grad_probs * probs, axis=1, keepdims=True)
        grad_scores = (probs * (grad_probs - inner)).astype(jnp.bfloat16)
        grad_query = (
            jnp.einsum("rk,ke->re", grad_scores, key_set, preferred_element_type=jnp.float32)
            * score_scale
        )
        grad_key = (
            jnp.einsum("rk,re->ke", grad_scores, query_set, preferred_element_type=jnp.float32)
            * score_scale
        )
        grad_value = jnp.einsum(
            "rk,re->ke", probs.astype(jnp.bfloat16), grad_set, preferred_element_type=jnp.float32
        )
        return (grad_query, grad_key, grad_value)

    query_parts, key_parts, value_parts = lax.map(single, jnp.arange(head_count * block_count))
    grad_queries = join_items(query_parts, head_count, row_count)
    grad_keys = jnp.sum(
        key_parts.reshape(head_count, block_count, key_count, head_width), axis=1
    ).transpose(1, 0, 2)
    grad_values = jnp.sum(
        value_parts.reshape(head_count, block_count, key_count, head_width), axis=1
    ).transpose(1, 0, 2)
    return (grad_queries, grad_keys, grad_values)


def lamb_step(weight, grad, first, second, decay):
    mean = first_decay * first + (1.0 - first_decay) * grad
    square = second_decay * second + (1.0 - second_decay) * grad * grad
    step = (
        mean
        / (1.0 - first_decay**STEPS_DONE)
        / (jnp.sqrt(square / (1.0 - second_decay**STEPS_DONE)) + adam_eps)
        + decay * weight
    )
    return (mean, square, step)


def per_device(
    tokens,
    memory,
    cotangent,
    lengths,
    groups,
    image_map,
    entry_weights,
    exit_weights,
    expand_weights,
    contract_weights,
    norm_gains,
    entry_first,
    entry_second,
    exit_first,
    exit_second,
    expand_first,
    expand_second,
    contract_first,
    contract_second,
    gains_first,
    gains_second,
):
    dp_count = lax.axis_size("dp")
    head_count = lax.axis_size("head")
    entry_full, exit_full, expand_full, contract_full, gains_full = (
        lax.all_gather(entry_weights.astype(jnp.bfloat16), "dp", axis=1, tiled=True),
        lax.all_gather(exit_weights.astype(jnp.bfloat16), "dp", axis=2, tiled=True),
        lax.all_gather(expand_weights.astype(jnp.bfloat16), "dp", axis=1, tiled=True),
        lax.all_gather(contract_weights.astype(jnp.bfloat16), "dp", axis=1, tiled=True),
        lax.all_gather(norm_gains.astype(jnp.bfloat16), "dp", axis=1, tiled=True),
    )
    gain_values = gains_full.astype(jnp.float32)
    tok_rows = tokens.shape[0]
    model_width = tokens.shape[1]
    local_width = entry_full.shape[2]
    local_heads = local_width // HEAD_DIM
    block_rows = min(512, tok_rows)
    segments, images, weights = token_layout(
        lengths.reshape(1, -1), groups.reshape(1, -1), image_map.reshape(1, -1), tok_rows, IMG_DEV
    )
    segment = segments[0]
    image_tok = images[0]
    weight_tok = weights[0]
    position = jnp.arange(tok_rows, dtype=jnp.int32)

    def self_mask(row_start, row_span):
        row_segment = lax.dynamic_slice_in_dim(segment, row_start, row_span)
        row_position = lax.dynamic_slice_in_dim(position, row_start, row_span)
        return (row_segment[:, None] == segment[None, :]) & (
            position[None, :] <= row_position[:, None]
        )

    stream = tokens.astype(jnp.float32)
    normed_one, pull_one = jax.vjp(rms_norm, stream, gain_values[0])
    hidden_one = normed_one.astype(jnp.bfloat16)
    projected = jnp.einsum(
        "td,sdc->tsc", hidden_one, entry_full[0:3], preferred_element_type=jnp.float32
    ).astype(jnp.bfloat16)
    heads_view = projected.reshape(tok_rows, 3, local_heads, HEAD_DIM)
    queries = heads_view[:, 0]
    key_rows = heads_view[:, 1]
    value_rows = heads_view[:, 2]
    self_out, self_sums = attend_forward(queries, key_rows, value_rows, self_mask, block_rows)
    self_flat = self_out.reshape(tok_rows, local_width).astype(jnp.bfloat16)
    stream_one = stream + head_total(
        jnp.dot(self_flat, exit_full[0], preferred_element_type=jnp.float32)
    )
    normed_two, pull_two = jax.vjp(rms_norm, stream_one, gain_values[1])
    hidden_two = normed_two.astype(jnp.bfloat16)
    cross_queries = (
        jnp.dot(hidden_two, entry_full[3], preferred_element_type=jnp.float32)
        .astype(jnp.bfloat16)
        .reshape(tok_rows, local_heads, HEAD_DIM)
    )
    image_total = memory.shape[0]
    patch_local = memory.shape[1]
    key_weights = lax.all_gather(entry_full[4:6], "head", axis=2, tiled=True)
    projected_pairs = jnp.einsum(
        "npd,sdc->npsc", memory, key_weights, preferred_element_type=jnp.float32
    ).astype(jnp.bfloat16)
    arranged = projected_pairs.reshape(
        dp_count, IMG_DEV, patch_local, 2, head_count, local_width
    ).transpose(0, 4, 1, 2, 3, 5)
    arranged = arranged.reshape(dp_count * head_count, IMG_DEV, patch_local, 2 * local_width)
    received = lax.all_to_all(arranged, ("dp", "head"), split_axis=0, concat_axis=2, tiled=True)
    key_pairs = received.reshape(-1, 2, local_width)
    key_count = key_pairs.shape[0]
    patch_total = key_count // IMG_DEV
    key_image = jnp.arange(key_count, dtype=jnp.int32) // patch_total

    def cross_mask(row_start, row_span):
        row_image = lax.dynamic_slice_in_dim(image_tok, row_start, row_span)
        return row_image[:, None] == key_image[None, :]

    cross_keys = key_pairs[:, 0].reshape(key_count, local_heads, HEAD_DIM)
    cross_values = key_pairs[:, 1].reshape(key_count, local_heads, HEAD_DIM)
    cross_out, cross_sums = attend_forward(
        cross_queries, cross_keys, cross_values, cross_mask, block_rows
    )
    cross_flat = cross_out.reshape(tok_rows, local_width).astype(jnp.bfloat16)
    stream_two = stream_one + head_total(
        jnp.dot(cross_flat, exit_full[1], preferred_element_type=jnp.float32)
    )
    normed_three, pull_three = jax.vjp(rms_norm, stream_two, gain_values[2])
    hidden_three = normed_three.astype(jnp.bfloat16)
    gate_up = jnp.einsum(
        "td,sdf->tsf", hidden_three, expand_full, preferred_element_type=jnp.float32
    )
    activated, pull_gate = jax.vjp(gated_hidden, gate_up[:, 0], gate_up[:, 1])
    activated_low = activated.astype(jnp.bfloat16)
    output = stream_two + head_total(
        jnp.dot(activated_low, contract_full, preferred_element_type=jnp.float32)
    )
    grad_stream = cotangent.astype(jnp.float32) * weight_tok[:, None]
    grad_branch = grad_stream.astype(jnp.bfloat16)
    contract_part = jnp.einsum(
        "tf,td->fd", activated_low, grad_branch, preferred_element_type=jnp.float32
    )
    grad_act = jnp.einsum(
        "td,fd->tf", grad_branch, contract_full, preferred_element_type=jnp.float32
    )
    grad_gate, grad_up = pull_gate(grad_act)
    grad_pair = jnp.stack([grad_gate, grad_up], axis=1).astype(jnp.bfloat16)
    expand_part = jnp.einsum(
        "td,tsf->sdf", hidden_three, grad_pair, preferred_element_type=jnp.float32
    )
    grad_normed = head_total(
        jnp.einsum("tsf,sdf->td", grad_pair, expand_full, preferred_element_type=jnp.float32)
    )
    grad_input, gain_three = pull_three(grad_normed)
    grad_stream = grad_stream + grad_input
    grad_branch = grad_stream.astype(jnp.bfloat16)
    exit_cross = jnp.einsum(
        "tc,td->cd", cross_flat, grad_branch, preferred_element_type=jnp.float32
    )
    grad_cross_out = (
        jnp.einsum("td,cd->tc", grad_branch, exit_full[1], preferred_element_type=jnp.float32)
        .astype(jnp.bfloat16)
        .reshape(tok_rows, local_heads, HEAD_DIM)
    )
    grad_cq, grad_ck, grad_cv = attend_backward(
        cross_queries, cross_keys, cross_values, cross_mask, block_rows, cross_sums, grad_cross_out
    )
    grad_cq_low = grad_cq.reshape(tok_rows, local_width).astype(jnp.bfloat16)
    query_part = jnp.einsum(
        "td,tc->dc", hidden_two, grad_cq_low, preferred_element_type=jnp.float32
    )
    grad_normed = head_total(
        jnp.einsum("tc,dc->td", grad_cq_low, entry_full[3], preferred_element_type=jnp.float32)
    )
    grad_input, gain_two = pull_two(grad_normed)
    grad_stream = grad_stream + grad_input
    grad_kv = jnp.stack(
        [grad_ck.reshape(key_count, local_width), grad_cv.reshape(key_count, local_width)], axis=1
    ).astype(jnp.bfloat16)
    sending = grad_kv.reshape(1, IMG_DEV, patch_total, 2 * local_width)
    returned = lax.all_to_all(sending, ("dp", "head"), split_axis=2, concat_axis=0, tiled=True)
    grad_full = returned.reshape(
        dp_count, head_count, IMG_DEV, patch_local, 2, local_width
    ).transpose(0, 2, 3, 4, 1, 5)
    grad_full = grad_full.reshape(image_total, patch_local, 2, model_width)
    memory_grads = jnp.einsum(
        "npsc,sdc->npd", grad_full, key_weights, preferred_element_type=jnp.float32
    )
    weight_part = jnp.einsum("npd,npsc->sdc", memory, grad_full, preferred_element_type=jnp.float32)
    spread_part = weight_part.reshape(
        2, dp_count, model_width // dp_count, head_count, local_width
    ).transpose(1, 3, 0, 2, 4)
    spread_part = spread_part.reshape(
        dp_count * head_count, 2, model_width // dp_count, local_width
    )
    key_grads = lax.psum_scatter(spread_part, ("dp", "head"), scatter_dimension=0, tiled=True)[0]
    grad_branch = grad_stream.astype(jnp.bfloat16)
    exit_self = jnp.einsum("tc,td->cd", self_flat, grad_branch, preferred_element_type=jnp.float32)
    grad_self_out = (
        jnp.einsum("td,cd->tc", grad_branch, exit_full[0], preferred_element_type=jnp.float32)
        .astype(jnp.bfloat16)
        .reshape(tok_rows, local_heads, HEAD_DIM)
    )
    grad_q, grad_k, grad_v = attend_backward(
        queries, key_rows, value_rows, self_mask, block_rows, self_sums, grad_self_out
    )
    grad_triple = jnp.stack(
        [
            grad_q.reshape(tok_rows, local_width),
            grad_k.reshape(tok_rows, local_width),
            grad_v.reshape(tok_rows, local_width),
        ],
        axis=1,
    ).astype(jnp.bfloat16)
    self_part = jnp.einsum(
        "td,tsc->sdc", hidden_one, grad_triple, preferred_element_type=jnp.float32
    )
    grad_normed = head_total(
        jnp.einsum("tsc,sdc->td", grad_triple, entry_full[0:3], preferred_element_type=jnp.float32)
    )
    grad_input, gain_one = pull_one(grad_normed)
    token_grads = grad_stream + grad_input
    entry_four = jnp.concatenate([self_part, query_part[None]], axis=0)
    exit_part = jnp.stack([exit_self, exit_cross])
    gain_part = jnp.stack([gain_one, gain_two, gain_three])
    entry_four_grads, exit_grads, expand_grads, contract_grads, gain_grads = (
        lax.psum_scatter(entry_four, "dp", scatter_dimension=1, tiled=True),
        lax.psum_scatter(exit_part, "dp", scatter_dimension=2, tiled=True),
        lax.psum_scatter(expand_part, "dp", scatter_dimension=1, tiled=True),
        lax.psum_scatter(contract_part, "dp", scatter_dimension=1, tiled=True),
        lax.psum_scatter(gain_part, "dp", scatter_dimension=1, tiled=True),
    )
    entry_grads = jnp.concatenate([entry_four_grads, key_grads], axis=0)
    entry_mean, entry_square, entry_step = lamb_step(
        entry_weights, entry_grads, entry_first, entry_second, weight_decay
    )
    exit_mean, exit_square, exit_step = lamb_step(
        exit_weights, exit_grads, exit_first, exit_second, weight_decay
    )
    expand_mean, expand_square, expand_step = lamb_step(
        expand_weights, expand_grads, expand_first, expand_second, weight_decay
    )
    contract_mean, contract_square, contract_step = lamb_step(
        contract_weights, contract_grads, contract_first, contract_second, weight_decay
    )
    gains_mean, gains_square, gains_step = lamb_step(
        norm_gains, gain_grads, gains_first, gains_second, 0.0
    )
    weight_local = jnp.concatenate(
        [
            jnp.sum(entry_weights * entry_weights, axis=(1, 2)),
            jnp.sum(exit_weights * exit_weights, axis=(1, 2)),
            jnp.sum(expand_weights * expand_weights, axis=(1, 2)),
            jnp.sum(contract_weights * contract_weights).reshape(1),
            jnp.sum(norm_gains * norm_gains, axis=1) / head_count,
        ]
    )
    step_local = jnp.concatenate(
        [
            jnp.sum(entry_step * entry_step, axis=(1, 2)),
            jnp.sum(exit_step * exit_step, axis=(1, 2)),
            jnp.sum(expand_step * expand_step, axis=(1, 2)),
            jnp.sum(contract_step * contract_step).reshape(1),
            jnp.sum(gains_step * gains_step, axis=1) / head_count,
        ]
    )
    weight_squares, step_squares = lax.psum((weight_local, step_local), ("dp", "head"))
    weight_norm = jnp.sqrt(weight_squares)
    step_norm = jnp.sqrt(step_squares)
    ratio = learn_rate * weight_norm / (step_norm + adam_eps)
    entry_new = entry_weights - ratio[0:6][:, None, None] * entry_step
    exit_new = exit_weights - ratio[6:8][:, None, None] * exit_step
    expand_new = expand_weights - ratio[8:10][:, None, None] * expand_step
    contract_new = contract_weights - ratio[10] * contract_step
    gains_new = norm_gains - ratio[11:14][:, None] * gains_step
    trust_norms = jnp.stack([weight_norm, step_norm])
    return (
        output,
        token_grads,
        memory_grads,
        entry_grads,
        exit_grads,
        expand_grads,
        contract_grads,
        gain_grads,
        entry_mean,
        exit_mean,
        expand_mean,
        contract_mean,
        gains_mean,
        entry_square,
        exit_square,
        expand_square,
        contract_square,
        gains_square,
        entry_new,
        exit_new,
        expand_new,
        contract_new,
        gains_new,
        entry_new.astype(jnp.bfloat16),
        exit_new.astype(jnp.bfloat16),
        expand_new.astype(jnp.bfloat16),
        contract_new.astype(jnp.bfloat16),
        trust_norms,
    )


def solution(mesh):
    in_specs = (
        P("dp", None),
        P(None, ("dp", "head"), None),
        P("dp", None),
        P("dp"),
        P("dp"),
        P("dp"),
        P(None, "dp", "head"),
        P(None, "head", "dp"),
        P(None, "dp", "head"),
        P("head", "dp"),
        P(None, "dp"),
        P(None, "dp", "head"),
        P(None, "dp", "head"),
        P(None, "head", "dp"),
        P(None, "head", "dp"),
        P(None, "dp", "head"),
        P(None, "dp", "head"),
        P("head", "dp"),
        P("head", "dp"),
        P(None, "dp"),
        P(None, "dp"),
    )
    out_specs = (
        P("dp", None),
        P("dp", None),
        P(None, ("dp", "head"), None),
        P(None, "dp", "head"),
        P(None, "head", "dp"),
        P(None, "dp", "head"),
        P("head", "dp"),
        P(None, "dp"),
        P(None, "dp", "head"),
        P(None, "head", "dp"),
        P(None, "dp", "head"),
        P("head", "dp"),
        P(None, "dp"),
        P(None, "dp", "head"),
        P(None, "head", "dp"),
        P(None, "dp", "head"),
        P("head", "dp"),
        P(None, "dp"),
        P(None, "dp", "head"),
        P(None, "head", "dp"),
        P(None, "dp", "head"),
        P("head", "dp"),
        P(None, "dp"),
        P(None, "dp", "head"),
        P(None, "head", "dp"),
        P(None, "dp", "head"),
        P("head", "dp"),
        P(),
    )
    return jax.shard_map(
        per_device, mesh=mesh, in_specs=in_specs, out_specs=out_specs, check_vma=False
    )
```

profile of v0, /device:TPU:18, one launch (start us, length us, event | category | flops | bytes accessed | tf_op | source)
XLA Modules:
  0.0 1915.3 jit_solution(4496052431067974165)
XLA Ops:
  10.3 33.6 %all-gather.5.cloned.1.call-done = bf16[6,768,192]{2,0,1:T(8,128)(2,1)} async-done(((bf16[6,96,192]{2,0,1:T(8,128)(2,1)}), bf16[6,768,192]{2,0,1:T(8,128)(2,1)}) %all-gather.5.cloned.1.call-update) | async-done | bytes 1769488 | tf_op jit(solution)/shard_map/all_gather | solution.py:195
  49.1 7.9 all-gather
  57.5 10.4 all_gather.20
  90.2 7.7 all-gather.7.cloned.1.call-done
  103.6 9.2 reshape.523
  112.8 8.5 copy.436
  121.3 9.8 reshape.524
  136.9 66.6 %while.64 = (s32[]{:T(128)}, bf16[6,512,64]{1,2,0:T(8,128)(2,1)}, f32[6,512]{1,0:T(8,128)S(1)}, s32[6]{0:T(128)S(1)}, s32[1024]{0:T(1024)S(1)}, /*index=5*/s32[1...) while((s32[]{:T(128)}, bf16[6,512,64]{1,2,0:T(8,128)(2,1)}, ...), condition=%wide.region_6.7_spmd.clone, body=%wide.region_3.6_spmd.clone.sunk | while | flops 139984416 | bytes 15508489 | solution.py:102
  217.0 112.4 %all-reduce.10.cloned.1.call-done = f32[1024,768]{1,0:T(8,128)} async-done(((f32[1024,768]{1,0:T(8,128)}), f32[1024,768]{1,0:T(8,128)}) %all-reduce.10.cloned.1.call-update) | async-done | bytes 3145744 | tf_op jit(solution)/shard_map/psum | solution.py:48
  339.7 10.2 reshape.525
  349.8 9.8 fusion.169
  359.7 9.9 copy.380
  372.3 9.9 copy.381
  385.0 96.6 %while.66 = (s32[]{:T(128)}, bf16[6,512,64]{1,2,0:T(8,128)(2,1)S(1)}, f32[6,512]{1,0:T(8,128)S(1)}, s32[6]{0:T(128)S(1)}, s32[1024]{0:T(1024)S(1)}, /*index=5*/b...) while((s32[]{:T(128)}, ...), condition=%wide.region_13.14_spmd.clone, body=%wide.region_10.13_spmd.clone.sunk | while | flops 555777536 | bytes 61139956 | solution.py:102
  486.1 10.4 all_gather.23
  496.5 108.9 %all-reduce.12.cloned.1.call-done = f32[1024,768]{1,0:T(8,128)} async-done(((f32[1024,768]{1,0:T(8,128)}), f32[1024,768]{1,0:T(8,128)}) %all-reduce.12.cloned.1.call-update) | async-done | bytes 3145744 | tf_op jit(solution)/shard_map/psum | solution.py:48
  610.2 23.2 %all-gather.9.cloned.1.call-done = bf16[2,768,512]{2,1,0:T(8,128)(2,1)} async-done(((bf16[2,96,512]{2,1,0:T(8,128)(2,1)}), bf16[2,768,512]{2,1,0:T(8,128)(2,1)}) %all-gather.9.cloned.1.call-update) | async-done | bytes 1572880 | tf_op jit(solution)/shard_map/all_gather | solution.py:197
  646.4 120.2 %all-reduce.14.cloned.1.call-done = f32[1024,768]{1,0:T(8,128)} async-done(((f32[1024,768]{1,0:T(8,128)}), f32[1024,768]{1,0:T(8,128)}) %all-reduce.14.cloned.1.call-update) | async-done | bytes 3145744 | tf_op jit(solution)/shard_map/psum | solution.py:48
  777.9 183.9 %while.67 = (s32[]{:T(128)}, bf16[6,512,64]{1,2,0:T(8,128)(2,1)}, f32[6,4096,64]{1,2,0:T(8,128)}, f32[6,4096,64]{1,2,0:T(8,128)}, s32[6]{0:T(128)S(1)}, /*index=...) while((s32[]{:T(128)}, bf16[6,512,64]{1,2,0:T(8,128)(2,1)}, ...), condition=%wide.region_23.24_spmd.clone, body=%wide.region_21.23_spmd.clone.sunk | while | flops 1363475968 | bytes 135972912 | solution.py:146
  785.9 6.7 multiply_reduce_fusion.21
  792.5 7.9 multiply_convert_fusion.11
  823.2 7.9 multiply_convert_fusion.11
  847.2 6.7 multiply_reduce_fusion.21
  853.8 7.9 multiply_convert_fusion.11
  877.9 6.7 multiply_reduce_fusion.21
  884.6 7.9 multiply_convert_fusion.11
  908.5 6.7 multiply_reduce_fusion.21
  915.2 7.9 multiply_convert_fusion.11
  939.2 6.7 multiply_reduce_fusion.21
  945.8 7.9 multiply_convert_fusion.11
  971.1 115.8 %all-reduce.16.cloned.1.call-done = f32[1024,768]{1,0:T(8,128)} async-done(((f32[1024,768]{1,0:T(8,128)}), f32[1024,768]{1,0:T(8,128)}) %all-reduce.16.cloned.1.call-update) | async-done | bytes 3145744 | tf_op jit(solution)/shard_map/psum | solution.py:48
  1100.6 85.1 %while.65 = (s32[]{:T(128)}, bf16[6,512,64]{1,2,0:T(8,128)(2,1)}, f32[6,1024,64]{1,2,0:T(8,128)}, f32[6,1024,64]{1,2,0:T(8,128)}, s32[6]{0:T(128)S(1)}, /*index=...) while((s32[]{:T(128)}, bf16[6,512,64]{1,2,0:T(8,128)(2,1)}, ...), condition=%wide.region_28.29_spmd.clone, body=%wide.region_26.28_spmd.clone.sunk | while | flops 341933600 | bytes 17727756 | solution.py:146
  1233.5 11.1 copy.392
  1274.1 99.4 %all-to-all-done.1 = bf16[1,2,2048,384]{3,1,0,2:T(2,128)(2,1)} async-done(((bf16[1,2,2048,384]{3,1,0,2:T(2,128)(2,1)}), bf16[1,2,2048,384]{3,1,0,2:T(2,128)(2,1)}, u32[]{:S(2)}, u32[]{:S(2)}) %all-to-all-start.1) | async-done | bytes 3145760 | tf_op jit(solution)/shard_map/all_to_all | solution.py:326
  1377.9 10.2 reshape.533
  1388.2 7.7 copy.395
  1395.9 8.3 reshape.534
  1404.2 77.3 %all-reduce.20.cloned.1.call-done = (f32[1024,768]{1,0:T(8,128)}, f32[1024,768]{1,0:T(8,128)}) async-done(((f32[1024,768]{1,0:T(8,128)}, f32[1024,768]{1,0:T(8,128)}), (f32[1024,768]{1,0:T(8,128)}, f32[1024,768]{1,0:T(8,128)})) %all-reduce.20.cloned.1.call-update) | async-done | bytes 6291472 | tf_op jit(solution)/shard_map/psum | solution.py:48
  1492.4 7.7 reshape.535
  1500.1 6.7 copy.396
  1515.7 38.4 %all-reduce.18.cloned.1.call-done = f32[2,768,512]{2,0,1:T(2,128)} async-done(((f32[2,768,512]{2,0,1:T(2,128)}), f32[2,768,512]{2,0,1:T(2,128)}) %all-reduce.18.cloned.1.call-update) | async-done | bytes 3145744
  1558.2 38.6 %reduce-scatter.14.cloned.1.call-done = f32[512,96]{0,1:T(8,128)} async-done(((f32[512,768]{0,1:T(8,128)}), f32[512,96]{0,1:T(8,128)}) %reduce-scatter.14.cloned.1.call-update) | async-done | bytes 196624 | tf_op jit(solution)/shard_map/reduce_scatter | solution.py:375
  1599.4 37.7 %reduce-scatter.18.cloned.1.call-done = f32[96,384]{1,0:T(8,128)} async-done(((f32[768,384]{1,0:T(8,128)}), f32[96,384]{1,0:T(8,128)}) %reduce-scatter.18.cloned.1.call-update) | async-done | bytes 147472
  1642.9 6.9 fusion.108
  1649.8 33.1 %reduce-scatter.16.cloned.1.call-done = f32[96,768]{1,0:T(8,128)} async-done(((f32[768,768]{1,0:T(8,128)}), f32[96,768]{1,0:T(8,128)}) %reduce-scatter.16.cloned.1.call-update) | async-done | bytes 294928
  1690.4 30.2 %reduce-scatter.20.cloned.1.call-done = f32[96,3]{1,0:T(8,128)} async-done(((f32[768,3]{1,0:T(8,128)}), f32[96,3]{1,0:T(8,128)}) %reduce-scatter.20.cloned.1.call-update) | async-done | bytes 1168
  1722.2 118.5 %reduce-scatter.12.cloned.1.call-done = f32[1,2,96,192]{2,3,1,0:T(8,128)} async-done(((f32[32,2,96,192]{2,3,1,0:T(8,128)}), f32[1,2,96,192]{2,3,1,0:T(8,128)}) %reduce-scatter.12.cloned.1.call-update) | async-done | bytes 147472 | tf_op jit(solution)/shard_map/reduce_scatter | solution.py:341
  1849.2 40.1 %all-reduce.1 = (f32[14]{0:T(128)S(1)}, f32[14]{0:T(128)S(1)}) all-reduce(f32[14]{0:T(128)S(1)} %concatenate.15, f32[14]{0:T(128)S(1)} %copy-done.80), channel_id=1, replica_groups=mesh['dp'=8,'head'=4] {'dp','head'}, use_global_device_ids=true, to_apply=%region_55.56 | all-reduce | flops 28 | bytes 224 | tf_op jit(solution)/shard_map/psum | solution.py:412
  (628 shorter events, 533.5 us)
Async XLA Ops:
  7.2 90.7 %copy-start = (bf16[16,64,768]{2,1,0:T(8,128)(2,1)S(1)}, bf16[16,64,768]{2,1,0:T(8,128)(2,1)}, u32[]{:S(2)}) copy-start(bf16[16,64,768]{2,1,0:T(8,128)(2,1)} %param.31) | copy-start | bytes 4718596
  7.2 41.3 %copy-start.65 = (f32[3,96]{1,0:T(4,128)S(1)}, f32[3,96]{1,0:T(4,128)}, u32[]{:S(2)}) copy-start(f32[3,96]{1,0:T(4,128)} %param.40) | copy-start | bytes 3460
  7.2 49.9 %copy-start.83 = (s32[8]{0:T(128)S(1)}, s32[8]{0:T(128)}, u32[]{:S(2)}) copy-start(s32[8]{0:T(128)} %param.33) | copy-start | bytes 100
  7.2 50.1 %copy-start.32 = (f32[2,192,96]{2,1,0:T(8,128)S(1)}, f32[2,192,96]{2,1,0:T(8,128)}, u32[]{:S(2)}) copy-start(f32[2,192,96]{2,1,0:T(8,128)} %param.37) | copy-start | bytes 442372
  7.3 36.7 %all-gather.5.cloned.1.call-start = ((), (), s32[]{:S(2)}) async-start(), calls=%async_computation.7 | async-start | bytes 3538944 | tf_op jit(solution)/shard_map/all_gather | solution.py:195
  10.3 87.7 %all-gather.7.cloned.1.call-start = ((), (), s32[]{:S(2)}) async-start(), calls=%async_computation.9 | async-start | bytes 2949120 | tf_op jit(solution)/shard_map/all_gather | solution.py:246
  48.4 24.1 %copy-start.12 = (bf16[1024,768]{1,0:T(8,128)(2,1)S(1)}, bf16[1024,768]{1,0:T(8,128)(2,1)}, u32[]{:S(2)}) copy-start(bf16[1024,768]{1,0:T(8,128)(2,1)} %param.30) | copy-start | bytes 4718596
  72.4 132.6 %copy-start.26 = (bf16[1,192,768]{2,1,0:T(8,128)(2,1)}, bf16[1,192,768]{2,1,0:T(8,128)(2,1)S(1)}, u32[]{:S(2)}) copy-start(bf16[1,192,768]{2,1,0:T(8,128)(2,1)S(1)} %copy.425) | copy-start | bytes 884740
  72.6 259.2 %copy-start.50 = (f32[768]{0:T(1024)}, f32[768]{0:T(1024)S(1)}, u32[]{:S(2)}) copy-start(f32[768]{0:T(1024)S(1)} %get-tuple-element.1076) | copy-start | bytes 9220
  72.6 698.3 %copy-start.61 = (f32[768]{0:T(1024)}, f32[768]{0:T(1024)S(1)}, u32[]{:S(2)}) copy-start(f32[768]{0:T(1024)S(1)} %get-tuple-element.1075) | copy-start | bytes 9220
  131.2 204.6 %all-to-all-start = ((bf16[32,2,64,384]{3,2,1,0:T(8,128)(2,1)}), bf16[32,2,64,384]{3,2,1,0:T(8,128)(2,1)}, u32[]{:S(2)}, u32[]{:S(2)}) async-start(bf16[32,2,64,384]{3,2,1,0:T(8,128)(2,1)} %reshape.524), calls=%async_computation | async-start | bytes 6291456 | tf_op jit(solution)/shard_map/all_to_all | solution.py:254
  136.1 193.3 %all-reduce.10.cloned.1.call-start = ((), (), s32[]{:S(2)}) async-start(), calls=%async_computation.8 | async-start | bytes 6291456 | tf_op jit(solution)/shard_map/psum | solution.py:48
  203.6 292.9 %copy-start.46 = (s32[1,1024]{1,0:T(1,128)}, s32[1,1024]{1,0:T(1,128)S(1)}, u32[]{:S(2)}) copy-start(s32[1,1024]{1,0:T(1,128)S(1)} %get-tuple-element.1781) | copy-start | bytes 12292
  208.1 397.3 %all-reduce.12.cloned.1.call-start = ((), (), s32[]{:S(2)}) async-start(), calls=%async_computation.10 | async-start | bytes 6291456 | tf_op jit(solution)/shard_map/psum | solution.py:48
  217.0 114.8 %copy-start.28 = (bf16[1,768,192]{1,2,0:T(8,128)(2,1)}, bf16[1,768,192]{1,2,0:T(8,128)(2,1)S(1)}, u32[]{:S(2)}) copy-start(bf16[1,768,192]{1,2,0:T(8,128)(2,1)S(1)} %copy.426) | copy-start | bytes 884740
  385.0 97.8 %copy-start.29 = (bf16[1,192,768]{2,1,0:T(8,128)(2,1)S(1)}, bf16[1,192,768]{2,1,0:T(8,128)(2,1)}, u32[]{:S(2)}) copy-start(bf16[1,192,768]{2,1,0:T(8,128)(2,1)} %copy.428) | copy-start | bytes 884740
  485.1 148.3 %all-gather.9.cloned.1.call-start = ((), (), s32[]{:S(2)}) async-start(), calls=%async_computation.11 | async-start | bytes 1769472 | tf_op jit(solution)/shard_map/all_gather | solution.py:197
  485.9 280.6 %all-reduce.14.cloned.1.call-start = ((), (), s32[]{:S(2)}) async-start(), calls=%async_computation.12 | async-start | bytes 6291456 | tf_op jit(solution)/shard_map/psum | solution.py:48
  496.5 141.3 %copy-start.24 = (bf16[512,768]{0,1:T(8,128)(2,1)}, bf16[512,768]{0,1:T(8,128)(2,1)S(1)}, u32[]{:S(2)}) copy-start(bf16[512,768]{0,1:T(8,128)(2,1)S(1)} %all_gather.23) | copy-start | bytes 2359300
  496.5 274.5 %copy-start.67 = (f32[1024]{0:T(1024)}, f32[1024]{0:T(1024)S(1)}, u32[]{:S(2)}) copy-start(f32[1024]{0:T(1024)S(1)} %compare_select_fusion.1) | copy-start | bytes 12292
  610.2 160.7 %copy-start.57 = (f32[1024]{0:T(1024)}, f32[1024]{0:T(1024)S(1)}, u32[]{:S(2)}) copy-start(f32[1024]{0:T(1024)S(1)} %fusion.151) | copy-start | bytes 12292
  646.3 440.6 %all-reduce.16.cloned.1.call-start = ((), (), s32[]{:S(2)}) async-start(), calls=%async_computation.13 | async-start | bytes 6291456 | tf_op jit(solution)/shard_map/psum | solution.py:48
  966.7 120.3 %copy-start.49 = (f32[1024]{0:T(1024)S(1)}, f32[1024]{0:T(1024)}, u32[]{:S(2)}) copy-start(f32[1024]{0:T(1024)} %copy-done.48) | copy-start | bytes 12292
  966.7 120.2 %copy-start.51 = (f32[768]{0:T(1024)S(1)}, f32[768]{0:T(1024)}, u32[]{:S(2)}) copy-start(f32[768]{0:T(1024)} %copy-done.50) | copy-start | bytes 9220
  966.7 514.7 %all-reduce.20.cloned.1.call-start = ((), (), s32[]{:S(2)}) async-start(), calls=%async_computation.20 | async-start | bytes 12582912 | tf_op jit(solution)/shard_map/psum | solution.py:48
  971.1 120.2 %copy-start.54 = (f32[1024]{0:T(1024)S(1)}, f32[1024]{0:T(1024)}, u32[]{:S(2)}) copy-start(f32[1024]{0:T(1024)} %copy-done.53) | copy-start | bytes 12292
  1197.2 356.9 %all-reduce.18.cloned.1.call-start = ((), (), s32[]{:S(2)}) async-start(), calls=%async_computation.19 | async-start | bytes 6291456
  1210.4 386.3 %reduce-scatter.14.cloned.1.call-start = ((), (), s32[]{:S(2)}) async-start(), calls=%async_computation.15 | async-start | bytes 1769472 | tf_op jit(solution)/shard_map/reduce_scatter | solution.py:375
  1244.6 128.9 %all-to-all-start.1 = ((bf16[1,2,2048,384]{3,1,0,2:T(2,128)(2,1)}), bf16[1,2,2048,384]{3,1,0,2:T(2,128)(2,1)}, u32[]{:S(2)}, u32[]{:S(2)}) async-start(bf16[1,2,2048,384]{3,1,0,2:T(2,128)(2,1)} %copy.392), calls=%async_computation.1 | async-start | bytes 6291456 | tf_op jit(solution)/shard_map/all_to_all | solution.py:326
  1249.5 387.6 %reduce-scatter.18.cloned.1.call-start = ((), (), s32[]{:S(2)}) async-start(), calls=%async_computation.17 | async-start | bytes 1327104
  1258.9 424.0 %reduce-scatter.16.cloned.1.call-start = ((), (), s32[]{:S(2)}) async-start(), calls=%async_computation.16 | async-start | bytes 2654208
  1273.8 446.8 %reduce-scatter.20.cloned.1.call-start = ((), (), s32[]{:S(2)}) async-start(), calls=%async_computation.18 | async-start | bytes 442368
  1485.4 355.2 %reduce-scatter.12.cloned.1.call-start = ((), (), s32[]{:S(2)}) async-start(), calls=%async_computation.14 | async-start | bytes 6488064 | tf_op jit(solution)/shard_map/reduce_scatter | solution.py:341
  1506.8 48.4 %copy-start.18 = (f32[2,96,512]{2,1,0:T(8,128)S(1)}, f32[2,96,512]{2,1,0:T(8,128)}, u32[]{:S(2)}) copy-start(f32[2,96,512]{2,1,0:T(8,128)} %param.38) | copy-start | bytes 1179652
  1515.7 125.2 %copy-start.72 = (f32[6]{0:T(128)S(1)}, f32[6]{0:T(128)}, u32[]{:S(2)}) copy-start(f32[6]{0:T(128)} %get-tuple-element.1212) | copy-start | bytes 76
  1638.3 11.4 copy-start.39
  1642.9 42.2 %copy-start.64 = (f32[1024]{0:T(1024)S(1)}, f32[1024]{0:T(1024)}, u32[]{:S(2)}) copy-start(f32[1024]{0:T(1024)} %copy-done.63) | copy-start | bytes 12292
  1685.1 36.4 %copy-start.66 = (f32[3,96]{1,0:T(4,128)S(1)}, f32[3,96]{1,0:T(4,128)}, u32[]{:S(2)}) copy-start(f32[3,96]{1,0:T(4,128)} %param.40) | copy-start | bytes 3460
  1685.1 36.4 %copy-start.75 = (f32[3,96]{1,0:T(4,128)S(1)}, f32[3,96]{1,0:T(4,128)}, u32[]{:S(2)}) copy-start(f32[3,96]{1,0:T(4,128)} %param.50) | copy-start | bytes 3460
  1685.1 36.4 %copy-start.76 = (f32[3,96]{1,0:T(4,128)S(1)}, f32[3,96]{1,0:T(4,128)}, u32[]{:S(2)}) copy-start(f32[3,96]{1,0:T(4,128)} %param.49) | copy-start | bytes 3460
  1690.4 153.2 %copy-start.73 = (f32[2]{0:T(128)S(1)}, f32[2]{0:T(128)}, u32[]{:S(2)}) copy-start(f32[2]{0:T(128)} %get-tuple-element.1070) | copy-start | bytes 28
  1690.4 153.2 %copy-start.74 = (f32[2]{0:T(128)S(1)}, f32[2]{0:T(128)}, u32[]{:S(2)}) copy-start(f32[2]{0:T(128)} %get-tuple-element.1074) | copy-start | bytes 28
  1721.5 127.8 %copy-start.71 = (f32[3,96]{1,0:T(4,128)}, f32[3,96]{1,0:T(4,128)S(1)}, u32[]{:S(2)}) copy-start(f32[3,96]{1,0:T(4,128)S(1)} %copy.421) | copy-start | bytes 3460
  1844.3 49.5 %copy-start.16 = (f32[6,96,192]{1,2,0:T(8,128)S(1)}, f32[6,96,192]{1,2,0:T(8,128)}, u32[]{:S(2)}) copy-start(f32[6,96,192]{1,2,0:T(8,128)} %copy.405) | copy-start | bytes 1327108
  1895.1 11.3 copy-start.77
  1895.1 12.4 copy-start.33
  1895.1 12.4 copy-start.40
  1895.1 12.4 copy-start.41
  (88 other events, 376.6 us)
Sparse Core Ops, SparseCore 0:
  10.5 33.3 all-gather.4
  48.6 49.2 all-gather.6
  208.2 121.0 all-reduce.9
  485.2 120.0 all-reduce.11
  607.7 25.6 all-gather.8
  646.4 120.0 all-reduce.13
  966.8 120.0 all-reduce.15
  1197.4 284.0 all-reduce.19
  1484.7 69.3 all-reduce.17
  1558.2 38.4 reduce-scatter.13
  1600.3 36.7 reduce-scatter.17
  1640.3 42.4 reduce-scatter.15
  1686.8 33.7 reduce-scatter.19
  1727.0 113.5 reduce-scatter.11
where the time goes:
time: 1930 us; the launch traced here: 1920 us
  waiting for transfers between devices  995 us (52%)
  matrix products  296 us (15%)
  local copies, waits for them, and re-layouts  294 us (15%)
  other arithmetic  139 us (7%)
  loops' own time  95.1 us (5%)
  blocking collectives  68.8 us (4%)
    psum x5, waiting for transfers between devices, head_total(): return lax.psum(partial_value, 'head')  535 us
    unnamed x18, waiting for transfers between devices  140 us
    reduce_scatter x1, waiting for transfers between devices, per_device(): lax.psum_scatter(spread_part, ('dp', 'head'), scatter_dimension=0, tiled=...  118 us
    all_to_all x1, waiting for transfers between devices, per_device(): lax.all_to_all(sending, ('dp', 'head'), split_axis=2, concat_axis=0, tile...  99.4 us
    unnamed x201, local copies, waits for them, and re-layouts  70.6 us
    convert_element_type x12, other arithmetic, single(): grad_scores = (probs * (grad_probs - inner)).astype(jnp.bfloat16)  49.1 us
    dot_general x12, matrix products, single(): jnp.einsum('rk,ke->re', weights, value_heads[head_index], preferred_eleme...  49.1 us
    dot_general x12, matrix products, single(): jnp.einsum('re,ke->rk', grad_set, value_heads[head_index], preferred_elem...  48.9 us
  transfers between devices with their start and end apart: 16, of which 15 were waited for; matrix products, arithmetic and copies ran while one was open for 13% of the time, Pallas kernels for 0%

commit v1 on v0

v1 whole, which is shorter than its diff:
```python
import jax
import jax.numpy as jnp
from jax import lax
from jax.experimental import pallas as pl
from jax.experimental.pallas import tpu as pltpu
from jax.sharding import PartitionSpec as P

HEAD_DIM = 64
IMG_DEV = 2
STEPS_DONE = 10


group_scale = (1.0, 0.5, 2.0)
first_decay = 0.9
second_decay = 0.999
learn_rate = 0.5
weight_decay = 0.01
adam_eps = 1e-06
norm_eps = 1e-06
masked_score = -1e30


def token_layout(lengths, groups, image_map, tok_rows, img_count):
    text_count = lengths.shape[1]
    text_ends = jnp.cumsum(lengths, axis=1)
    position = jnp.arange(tok_rows, dtype=jnp.int32)
    segment = jnp.sum((position[None, :, None] >= text_ends[:, None, :]).astype(jnp.int32), axis=2)
    chosen = (segment[:, :, None] == jnp.arange(text_count, dtype=jnp.int32)[None, None, :]).astype(
        jnp.int32
    )
    group_tok = jnp.sum(chosen * groups[:, None, :], axis=2)
    image_tok = jnp.sum(chosen * (image_map % img_count)[:, None, :], axis=2)
    scale_table = jnp.array(group_scale, dtype=jnp.float32)
    picked = (group_tok[:, :, None] == jnp.arange(3, dtype=jnp.int32)[None, None, :]).astype(
        jnp.float32
    )
    weight_tok = jnp.sum(picked * scale_table, axis=2) * (segment < text_count).astype(jnp.float32)
    return (segment, image_tok, weight_tok)


def rms_norm(values, gain):
    return values * lax.rsqrt(jnp.mean(values * values, axis=-1, keepdims=True) + norm_eps) * gain


def gated_hidden(gate, upward):
    return jax.nn.gelu(gate, approximate=True) * upward


BLOCK = 256
LANES = 128
LOG2E = 1.4426950408889634
NT = (((1,), (1,)), ((), ()))
TN = (((0,), (0,)), ((), ()))
VMEM_LIMIT = 50 * 1024 * 1024


def mm(a, b, dims=(((1,), (0,)), ((), ()))):
    return lax.dot_general(a, b, dims, preferred_element_type=jnp.float32)


def half_lanes(block, half):
    lane = lax.broadcasted_iota(jnp.int32, (1, LANES), 1)
    return jnp.where((lane // HEAD_DIM) == half, block, jnp.zeros_like(block))


def span_mask(start_ref, block, keys):
    low = block * BLOCK
    key_pos = lax.broadcasted_iota(jnp.int32, (keys, BLOCK), 0)
    query_pos = low + lax.broadcasted_iota(jnp.int32, (keys, BLOCK), 1)
    return (key_pos >= start_ref[0:1, low : low + BLOCK]) & (key_pos <= query_pos)


def self_forward_kernel(qkv_ref, start_ref, out_ref, sums_ref):
    rows = qkv_ref.shape[0]
    scale = HEAD_DIM ** (-0.5)
    sums_ref[...] = jnp.zeros_like(sums_ref)
    for pair in range(2):
        lanes = slice(LANES * pair, LANES * (pair + 1))
        for block in range(rows // BLOCK):
            own = slice(block * BLOCK, (block + 1) * BLOCK)
            keys = (block + 1) * BLOCK
            key_set = qkv_ref[0:keys, 256 + LANES * pair : 256 + LANES * (pair + 1)]
            value_set = qkv_ref[0:keys, 512 + LANES * pair : 512 + LANES * (pair + 1)]
            query_set = qkv_ref[own, lanes]
            allowed = span_mask(start_ref, block, keys)
            pieces = []
            for half in range(2 - pair):
                scores = mm(key_set, half_lanes(query_set, half), NT)
                scores = jnp.where(allowed, scores, masked_score)
                largest = jnp.max(scores, axis=0, keepdims=True)
                weights = jnp.exp2((scores - largest) * (scale * LOG2E))
                total = jnp.sum(weights, axis=0, keepdims=True)
                mixed = mm(value_set, weights.astype(jnp.bfloat16), TN) / total
                pieces.append(mixed[half * HEAD_DIM : (half + 1) * HEAD_DIM])
                row = 2 * pair + half
                sums_ref[row : row + 1, own] = largest * scale + jnp.log(total)
            if pair == 1:
                pieces.append(jnp.zeros_like(pieces[0]))
            out_ref[own, lanes] = jnp.concatenate(pieces, axis=0).T.astype(jnp.bfloat16)


def self_forward(qkv, starts):
    rows = qkv.shape[0]
    return pl.pallas_call(
        self_forward_kernel,
        out_shape=(
            jax.ShapeDtypeStruct((rows, 256), jnp.bfloat16),
            jax.ShapeDtypeStruct((8, rows), jnp.float32),
        ),
        compiler_params=pltpu.CompilerParams(vmem_limit_bytes=VMEM_LIMIT),
        cost_estimate=pl.CostEstimate(
            flops=3 * rows * rows * 256, bytes_accessed=rows * 2048, transcendentals=2 * rows * rows
        ),
        name="self_forward",
    )(qkv, starts)


def self_backward_kernel(
    qkv_ref, grad_ref, out_ref, sums_ref, start_ref, result_ref, key_acc, value_acc
):
    rows = qkv_ref.shape[0]
    scale = HEAD_DIM ** (-0.5)
    for pair in range(2):
        lanes = slice(LANES * pair, LANES * (pair + 1))
        key_lanes = slice(256 + LANES * pair, 256 + LANES * (pair + 1))
        value_lanes = slice(512 + LANES * pair, 512 + LANES * (pair + 1))
        for block in reversed(range(rows // BLOCK)):
            own = slice(block * BLOCK, (block + 1) * BLOCK)
            keys = (block + 1) * BLOCK
            key_set = qkv_ref[0:keys, key_lanes]
            value_set = qkv_ref[0:keys, value_lanes]
            query_set = qkv_ref[own, lanes]
            grad_set = grad_ref[own, lanes]
            allowed = span_mask(start_ref, block, keys)
            product = (
                grad_set.astype(jnp.float32) * out_ref[own, lanes].astype(jnp.float32)
            ).T
            pieces = []
            key_part = None
            for half in range(2 - pair):
                row = 2 * pair + half
                inner = jnp.sum(
                    product[half * HEAD_DIM : (half + 1) * HEAD_DIM], axis=0, keepdims=True
                )
                query_half = half_lanes(query_set, half)
                grad_half = half_lanes(grad_set, half)
                scores = mm(key_set, query_half, NT)
                probs = jnp.where(
                    allowed,
                    jnp.exp2(scores * (scale * LOG2E) - sums_ref[row : row + 1, own] * LOG2E),
                    0.0,
                )
                grad_probs = mm(value_set, grad_half, NT)
                grad_scores = (probs * (grad_probs - inner)).astype(jnp.bfloat16)
                value_new = mm(probs.astype(jnp.bfloat16), grad_half)
                key_new = mm(grad_scores, query_half)
                key_part = key_new if key_part is None else key_part + key_new
                value_part = value_new if half == 0 else value_part + value_new
                mixed = mm(key_set, grad_scores, TN) * scale
                pieces.append(mixed[half * HEAD_DIM : (half + 1) * HEAD_DIM])
            if pair == 1:
                pieces.append(jnp.zeros_like(pieces[0]))
            result_ref[own, lanes] = jnp.concatenate(pieces, axis=0).T.astype(jnp.bfloat16)
            if keys == rows:
                key_acc[...] = key_part
                value_acc[...] = value_part
            else:
                key_acc[0:keys, :] += key_part
                value_acc[0:keys, :] += value_part
        result_ref[:, key_lanes] = (key_acc[...] * scale).astype(jnp.bfloat16)
        result_ref[:, value_lanes] = value_acc[...].astype(jnp.bfloat16)


def self_backward(qkv, grad_out, out, sums, starts):
    rows = qkv.shape[0]
    return pl.pallas_call(
        self_backward_kernel,
        out_shape=jax.ShapeDtypeStruct((rows, 768), jnp.bfloat16),
        scratch_shapes=[
            pltpu.VMEM((rows, LANES), jnp.float32),
            pltpu.VMEM((rows, LANES), jnp.float32),
        ],
        compiler_params=pltpu.CompilerParams(vmem_limit_bytes=VMEM_LIMIT),
        cost_estimate=pl.CostEstimate(
            flops=3 * rows * rows * 640, bytes_accessed=rows * 5120, transcendentals=2 * rows * rows
        ),
        name="self_backward",
    )(qkv, grad_out, out, sums, starts)


def image_blocks(split, image, blocks):
    if image == 0:
        return 0, (split + BLOCK - 1) // BLOCK
    return split // BLOCK, blocks


def own_columns(split, image, low):
    column = low + lax.broadcasted_iota(jnp.int32, (1, BLOCK), 1)
    return column < split if image == 0 else column >= split


def own_rows(split, image, low):
    row = low + lax.broadcasted_iota(jnp.int32, (BLOCK, LANES), 0)
    return row < split if image == 0 else row >= split


def cross_forward_kernel(split_ref, query_ref, key_ref, value_ref, out_ref, sums_ref):
    rows = query_ref.shape[0]
    keys = key_ref.shape[0] // IMG_DEV
    scale = HEAD_DIM ** (-0.5)
    split = split_ref[0]
    for image in range(IMG_DEV):
        first, last = image_blocks(split, image, rows // BLOCK)

        def step(block, carry):
            low = pl.multiple_of(block * BLOCK, BLOCK)
            query_set = query_ref[pl.ds(low, BLOCK), :]
            key_set = key_ref[image * keys : (image + 1) * keys, :]
            value_set = value_ref[image * keys : (image + 1) * keys, :]
            kept = own_columns(split, image, low)
            pieces = []
            for half in range(2):
                scores = mm(key_set, half_lanes(query_set, half), NT)
                largest = jnp.max(scores, axis=0, keepdims=True)
                weights = jnp.exp2((scores - largest) * (scale * LOG2E))
                total = jnp.sum(weights, axis=0, keepdims=True)
                mixed = mm(value_set, weights.astype(jnp.bfloat16), TN) / total
                pieces.append(mixed[half * HEAD_DIM : (half + 1) * HEAD_DIM])
                held = sums_ref[0, half : half + 1, pl.ds(low, BLOCK)]
                sums_ref[0, half : half + 1, pl.ds(low, BLOCK)] = jnp.where(
                    kept, largest * scale + jnp.log(total), held
                )
            fresh = jnp.concatenate(pieces, axis=0).T
            held = out_ref[pl.ds(low, BLOCK), :].astype(jnp.float32)
            out_ref[pl.ds(low, BLOCK), :] = jnp.where(
                own_rows(split, image, low), fresh, held
            ).astype(jnp.bfloat16)
            return carry

        lax.fori_loop(first, last, step, 0)


def cross_forward(split, queries, pairs):
    rows, width = queries.shape
    keys = pairs.shape[0]
    groups = width // LANES
    return pl.pallas_call(
        cross_forward_kernel,
        grid=(groups,),
        in_specs=[
            pl.BlockSpec(memory_space=pltpu.SMEM),
            pl.BlockSpec((rows, LANES), lambda j: (0, j)),
            pl.BlockSpec((keys, LANES), lambda j: (0, j)),
            pl.BlockSpec((keys, LANES), lambda j: (0, groups + j)),
        ],
        out_specs=(
            pl.BlockSpec((rows, LANES), lambda j: (0, j)),
            pl.BlockSpec((1, 8, rows), lambda j: (j, 0, 0)),
        ),
        out_shape=(
            jax.ShapeDtypeStruct((rows, width), jnp.bfloat16),
            jax.ShapeDtypeStruct((groups, 8, rows), jnp.float32),
        ),
        compiler_params=pltpu.CompilerParams(vmem_limit_bytes=VMEM_LIMIT),
        cost_estimate=pl.CostEstimate(
            flops=groups * rows * keys * 512,
            bytes_accessed=keys * 1536,
            transcendentals=groups * rows * keys,
        ),
        name="cross_forward",
    )(split, queries, pairs, pairs)


def cross_backward_kernel(
    split_ref,
    query_ref,
    grad_ref,
    stats_ref,
    key_ref,
    value_ref,
    query_out,
    key_out,
    value_out,
    key_acc,
    value_acc,
):
    rows = query_ref.shape[0]
    keys = key_ref.shape[0] // IMG_DEV
    scale = HEAD_DIM ** (-0.5)
    split = split_ref[0]
    for image in range(IMG_DEV):
        first, last = image_blocks(split, image, rows // BLOCK)
        span = slice(image * keys, (image + 1) * keys)
        key_acc[...] = jnp.zeros_like(key_acc)
        value_acc[...] = jnp.zeros_like(value_acc)

        def step(block, carry):
            low = pl.multiple_of(block * BLOCK, BLOCK)
            query_set = query_ref[pl.ds(low, BLOCK), :]
            grad_set = grad_ref[pl.ds(low, BLOCK), :]
            key_set = key_ref[span, :]
            value_set = value_ref[span, :]
            kept = own_columns(split, image, low)
            pieces = []
            for half in range(2):
                sums = stats_ref[0, half : half + 1, pl.ds(low, BLOCK)]
                inner = stats_ref[0, 2 + half : 3 + half, pl.ds(low, BLOCK)]
                shift = jnp.where(kept, sums * LOG2E, -masked_score)
                query_half = half_lanes(query_set, half)
                grad_half = half_lanes(grad_set, half)
                scores = mm(key_set, query_half, NT)
                probs = jnp.exp2(scores * (scale * LOG2E) - shift)
                grad_probs = mm(value_set, grad_half, NT)
                grad_scores = (probs * (grad_probs - inner)).astype(jnp.bfloat16)
                value_new = mm(probs.astype(jnp.bfloat16), grad_half)
                key_new = mm(grad_scores, query_half)
                value_part = value_new if half == 0 else value_part + value_new
                key_part = key_new if half == 0 else key_part + key_new
                mixed = mm(key_set, grad_scores, TN) * scale
                pieces.append(mixed[half * HEAD_DIM : (half + 1) * HEAD_DIM])
            key_acc[...] += key_part
            value_acc[...] += value_part
            fresh = jnp.concatenate(pieces, axis=0).T
            held = query_out[pl.ds(low, BLOCK), :].astype(jnp.float32)
            query_out[pl.ds(low, BLOCK), :] = jnp.where(
                own_rows(split, image, low), fresh, held
            ).astype(jnp.bfloat16)
            return carry

        lax.fori_loop(first, last, step, 0)
        key_out[span, :] = (key_acc[...] * scale).astype(jnp.bfloat16)
        value_out[span, :] = value_acc[...].astype(jnp.bfloat16)


def cross_backward(split, queries, grads, stats, pairs):
    rows, width = queries.shape
    keys = pairs.shape[0]
    groups = width // LANES
    return pl.pallas_call(
        cross_backward_kernel,
        grid=(groups,),
        in_specs=[
            pl.BlockSpec(memory_space=pltpu.SMEM),
            pl.BlockSpec((rows, LANES), lambda j: (0, j)),
            pl.BlockSpec((rows, LANES), lambda j: (0, j)),
            pl.BlockSpec((1, 8, rows), lambda j: (j, 0, 0)),
            pl.BlockSpec((keys, LANES), lambda j: (0, j)),
            pl.BlockSpec((keys, LANES), lambda j: (0, groups + j)),
        ],
        out_specs=(
            pl.BlockSpec((rows, LANES), lambda j: (0, j)),
            pl.BlockSpec((keys, LANES), lambda j: (0, j)),
            pl.BlockSpec((keys, LANES), lambda j: (0, j)),
        ),
        out_shape=(
            jax.ShapeDtypeStruct((rows, width), jnp.bfloat16),
            jax.ShapeDtypeStruct((keys, width), jnp.bfloat16),
            jax.ShapeDtypeStruct((keys, width), jnp.bfloat16),
        ),
        scratch_shapes=[
            pltpu.VMEM((keys // IMG_DEV, LANES), jnp.float32),
            pltpu.VMEM((keys // IMG_DEV, LANES), jnp.float32),
        ],
        compiler_params=pltpu.CompilerParams(vmem_limit_bytes=VMEM_LIMIT),
        cost_estimate=pl.CostEstimate(
            flops=groups * rows * keys * 1280,
            bytes_accessed=keys * 3072,
            transcendentals=groups * rows * keys,
        ),
        name="cross_backward",
    )(split, queries, grads, stats, pairs, pairs)


def rms_pull(values, gain, grad):
    inverse = lax.rsqrt(jnp.mean(values * values, axis=-1, keepdims=True) + norm_eps)
    hat = values * inverse
    scaled = grad * gain
    inner = jnp.mean(scaled * hat, axis=-1, keepdims=True)
    return inverse * (scaled - hat * inner), jnp.sum(grad * hat, axis=0)


def head_swap(blocks):
    return lax.all_to_all(blocks, "head", split_axis=0, concat_axis=0, tiled=True)


def two_terms(values):
    high = lax.reduce_precision(values, exponent_bits=8, mantissa_bits=7)
    return high.astype(jnp.bfloat16), (values - high).astype(jnp.bfloat16)


def after(array, *earlier):
    return lax.optimization_barrier((array, *earlier))[0]


def head_spread(block):
    head_count = lax.axis_size("head")
    return head_swap(jnp.broadcast_to(block[None], (head_count, *block.shape)))


def lamb_step(weight, grad, first, second, decay):
    mean = first_decay * first + (1.0 - first_decay) * grad
    square = second_decay * second + (1.0 - second_decay) * grad * grad
    step = (
        mean
        / (1.0 - first_decay**STEPS_DONE)
        / (jnp.sqrt(square / (1.0 - second_decay**STEPS_DONE)) + adam_eps)
        + decay * weight
    )
    return (mean, square, step)


def per_device(
    tokens,
    memory,
    cotangent,
    lengths,
    groups,
    image_map,
    entry_weights,
    exit_weights,
    expand_weights,
    contract_weights,
    norm_gains,
    entry_first,
    entry_second,
    exit_first,
    exit_second,
    expand_first,
    expand_second,
    contract_first,
    contract_second,
    gains_first,
    gains_second,
):
    dp_count = lax.axis_size("dp")
    head_count = lax.axis_size("head")
    dp_index = lax.axis_index("dp")
    head_index = lax.axis_index("head")
    group = head_index % 2
    bf16 = jnp.bfloat16
    f32 = jnp.float32
    tok_rows, width = tokens.shape
    local = entry_weights.shape[2]
    hidden = expand_weights.shape[2]
    shard = width // dp_count
    row_count = tok_rows // head_count
    patch_local = memory.shape[1]
    patches = dp_count * patch_local
    heads = local // HEAD_DIM
    order = (0, 2, 1, 3)

    entry_low = entry_weights.astype(bf16).transpose(1, 0, 2)
    exit_low = exit_weights.astype(bf16).transpose(2, 0, 1)
    expand_low = expand_weights.astype(bf16).transpose(1, 0, 2)
    contract_low = contract_weights.astype(bf16).transpose(1, 0)[:, None]
    gains_low = jnp.pad(norm_gains.astype(bf16).transpose(1, 0), ((0, 0), (0, LANES - 3)))
    own_first = jnp.pad(entry_low[:, 0:3], ((0, 0), (0, 0), (0, 256 - local)))
    own_first = jnp.concatenate([own_first.reshape(shard, 768), gains_low], axis=1)
    first_set = jnp.concatenate([entry_low[:, 3:6], exit_low], axis=1)
    first_set = lax.all_gather(first_set, "head", axis=0)
    own_first = after(own_first, first_set)
    self_full = lax.all_gather(own_first, "dp", axis=0, tiled=True)
    self_weights = self_full[:, 0:768]
    gain_values = self_full[:, 768 : 768 + 3].astype(f32).transpose(1, 0)

    first_set = jnp.stack([first_set[h] for h in order], axis=2)
    natural = first_set[:, 3][:, (0, 2, 1, 3)]
    pair_set = first_set[:, 1:3].reshape(shard, 2, 2, 2 * local)
    pair_set = jnp.where(group == 0, pair_set[:, :, 0], pair_set[:, :, 1])
    first_set = jnp.concatenate(
        [
            natural.reshape(shard, width),
            first_set[:, 0].reshape(shard, width),
            pair_set.reshape(shard, width),
            first_set[:, 4].reshape(shard, width),
        ],
        axis=1,
    )
    first_full = lax.all_gather(first_set, "dp", axis=0, tiled=True)
    exit_self_t = first_full[:, 0:768]
    cross_query = first_full[:, 768:1536]
    cross_pair = first_full[:, 1536:2304]
    exit_cross_t = first_full[:, 2304:3072]

    images_here = memory.reshape(dp_count, IMG_DEV * patch_local, width)
    images_here = after(images_here, self_full)
    moved = lax.all_to_all(images_here, "dp", split_axis=0, concat_axis=0, tiled=True)
    moved = (
        moved.reshape(dp_count, IMG_DEV, patch_local, width)
        .transpose(1, 0, 2, 3)
        .reshape(IMG_DEV, patches, width)
    )
    near = [(s, s ^ 1) for s in range(head_count)]
    other = lax.ppermute(moved, "head", near)
    memory_pair = jnp.concatenate([moved, other], axis=1).reshape(2 * IMG_DEV * patches, width)

    second_set = jnp.concatenate([expand_low, contract_low], axis=1)
    second_set = head_spread(after(second_set, self_full))
    second_set = second_set.transpose(1, 2, 0, 3).reshape(shard, 3 * head_count * hidden)
    second_full = lax.all_gather(after(second_set, first_full), "dp", axis=0, tiled=True)
    inner_width = head_count * hidden
    gate_weights = second_full[:, 0:inner_width]
    up_weights = second_full[:, inner_width : 2 * inner_width]
    contract_t = second_full[:, 2 * inner_width :]

    segments, images, weights = token_layout(
        lengths.reshape(1, -1), groups.reshape(1, -1), image_map.reshape(1, -1), tok_rows, IMG_DEV
    )
    image_tok = images[0]
    weight_tok = weights[0]
    text_ends = jnp.cumsum(lengths)
    position = jnp.arange(tok_rows, dtype=jnp.int32)
    starts = jnp.max(
        jnp.where(position[None, :] >= text_ends[:, None], text_ends[:, None], 0), axis=0
    ).reshape(1, tok_rows)
    of_zero = (image_tok == 0).astype(jnp.int32)
    before = jnp.cumsum(of_zero)
    split = before[-1]
    place = jnp.where(image_tok == 0, before - 1, split + position - before)
    sorter = (place[None, :] == position[:, None]).astype(bf16)
    unsorter = (place[:, None] == position[None, :]).astype(bf16)
    split = split.reshape(1)

    def own(array):
        return lax.dynamic_slice_in_dim(array, head_index * row_count, row_count)

    stream = tokens.astype(f32)
    hidden_one = rms_norm(stream, gain_values[0]).astype(bf16)
    qkv = mm(hidden_one, self_weights).astype(bf16)
    self_out, self_sums = self_forward(qkv, starts)
    self_rows = head_swap(self_out[:, 0:local].reshape(head_count, row_count, local))
    self_rows = self_rows.transpose(1, 0, 2).reshape(row_count, width)
    stream_rows = own(stream)
    stream_one = stream_rows + mm(self_rows, exit_self_t, NT)
    hidden_two = rms_norm(stream_one, gain_values[1]).astype(bf16)

    def to_groups(rows):
        pieces = [rows[:, 0 : width // 2], rows[:, width // 2 :]]
        return jnp.stack(pieces + pieces)

    query_rows = mm(hidden_two, cross_query).astype(bf16)
    queries = head_swap(to_groups(query_rows)).reshape(tok_rows, width // 2)
    queries = mm(sorter, queries).astype(bf16)
    pairs = mm(memory_pair, cross_pair).astype(bf16)
    cross_out, cross_sums = cross_forward(split, queries, pairs)
    cross_out = mm(unsorter, cross_out).astype(bf16)
    high, low = two_terms(cross_sums[:, 0:2].reshape(2 * heads, tok_rows))
    tail = jnp.concatenate([high, low, jnp.zeros((4, tok_rows), bf16)], axis=0)
    tail = mm(tail, sorter).astype(bf16)
    tail = tail.reshape(16, head_count, row_count).transpose(1, 0, 2)
    tail = jnp.pad(tail, ((0, 0), (0, 0), (0, width // 2 - row_count)))
    sending = jnp.concatenate(
        [cross_out.reshape(head_count, row_count, width // 2), tail], axis=1
    )
    got = head_swap(sending)
    spread = (
        jnp.arange(2 * heads)[:, None] == (jnp.arange(width // 2) // HEAD_DIM)[None, :]
    ).astype(f32)

    def lanes_of(per_head):
        return lax.dot_general(
            per_head, spread, TN, precision=lax.Precision.HIGHEST, preferred_element_type=f32
        )

    merged = []
    merged_sums = []
    for g in range(2):
        part = [got[g], got[g + 2]]
        sums = [
            p[row_count : row_count + 2 * heads, 0:row_count].astype(f32)
            + p[row_count + 2 * heads : row_count + 4 * heads, 0:row_count].astype(f32)
            for p in part
        ]
        largest = jnp.maximum(sums[0], sums[1])
        both = [jnp.exp(s - largest) for s in sums]
        total = both[0] + both[1]
        merged.append(
            lanes_of(both[0] / total) * part[0][0:row_count].astype(f32)
            + lanes_of(both[1] / total) * part[1][0:row_count].astype(f32)
        )
        merged_sums.append(largest + jnp.log(total))
    cross_rows = jnp.concatenate(merged, axis=1).astype(bf16)
    stream_two = stream_one + mm(cross_rows, exit_cross_t, NT)
    hidden_three = rms_norm(stream_two, gain_values[2]).astype(bf16)

    gate = mm(hidden_three, gate_weights)
    upward = mm(hidden_three, up_weights)
    activated, pull_gate = jax.vjp(gated_hidden, gate, upward)
    activated_low = activated.astype(bf16)
    output_rows = stream_two + mm(activated_low, contract_t, NT)
    grad_rows = own(cotangent).astype(f32) * own(weight_tok)[:, None]
    grad_low = grad_rows.astype(bf16)
    grad_gate, grad_up = pull_gate(mm(grad_low, contract_t))
    grad_gate = grad_gate.astype(bf16)
    grad_up = grad_up.astype(bf16)
    grad_normed = mm(grad_gate, gate_weights, NT) + mm(grad_up, up_weights, NT)
    second_part = jnp.concatenate(
        [
            mm(hidden_three, grad_gate, TN).astype(bf16),
            mm(hidden_three, grad_up, TN).astype(bf16),
            mm(grad_low, activated_low, TN).astype(bf16),
        ],
        axis=1,
    )
    grad_input, gain_three = rms_pull(stream_two, gain_values[2], grad_normed)
    grad_rows = grad_rows + grad_input

    second_grads = lax.psum_scatter(second_part, "dp", scatter_dimension=0, tiled=True)

    grad_low = grad_rows.astype(bf16)
    exit_cross_part = mm(grad_low, cross_rows, TN).astype(bf16)
    grad_cross = mm(grad_low, exit_cross_t).astype(bf16)
    product = grad_cross.astype(f32) * cross_rows.astype(f32)
    tails = []
    for g in range(2):
        inner = lax.dot_general(
            spread,
            product[:, g * (width // 2) : (g + 1) * (width // 2)],
            NT,
            precision=lax.Precision.HIGHEST,
            preferred_element_type=f32,
        )
        tails.append(jnp.concatenate([*two_terms(merged_sums[g]), *two_terms(inner)], axis=0))
    tail = jnp.stack(tails + tails)
    tail = jnp.pad(tail, ((0, 0), (0, 32 - 8 * heads), (0, width // 2 - row_count)))
    got = head_swap(jnp.concatenate([to_groups(grad_cross), tail], axis=1))
    grads = mm(sorter, got[:, 0:row_count].reshape(tok_rows, width // 2)).astype(bf16)
    stats = (
        got[:, row_count : row_count + 8 * heads, 0:row_count]
        .transpose(1, 0, 2)
        .reshape(8 * heads, tok_rows)
    )
    stats = mm(stats, unsorter)
    sums = (stats[0 : 2 * heads] + stats[2 * heads : 4 * heads]).reshape(heads, 2, tok_rows)
    inner = (stats[4 * heads : 6 * heads] + stats[6 * heads :]).reshape(heads, 2, tok_rows)
    stats = jnp.concatenate([sums, inner, jnp.zeros((heads, 4, tok_rows), f32)], axis=1)
    grad_query, grad_key, grad_value = cross_backward(split, queries, grads, stats, pairs)
    grad_query = mm(unsorter, grad_query).astype(bf16)
    got = head_swap(grad_query.reshape(head_count, row_count, width // 2)).astype(f32)
    grad_query = jnp.concatenate([got[0] + got[2], got[1] + got[3]], axis=1).astype(bf16)
    query_part = mm(hidden_two, grad_query, TN).astype(bf16)
    grad_input, gain_two = rms_pull(
        stream_one, gain_values[1], mm(grad_query, cross_query, NT)
    )
    grad_rows = grad_rows + grad_input

    grad_pair = jnp.concatenate([grad_key, grad_value], axis=1)
    pair_part = mm(memory_pair, grad_pair, TN).astype(bf16)
    memory_part = mm(grad_pair, cross_pair, NT).reshape(IMG_DEV, 2, patches, width)
    returned = lax.ppermute(memory_part[:, 1].astype(bf16), "head", near)
    memory_sum = (memory_part[:, 0] + returned.astype(f32)).astype(bf16)
    memory_sum = (
        memory_sum.reshape(IMG_DEV, dp_count, patch_local, width)
        .transpose(1, 0, 2, 3)
        .reshape(dp_count, IMG_DEV * patch_local, width)
    )
    memory_grads = lax.all_to_all(memory_sum, "dp", split_axis=0, concat_axis=0, tiled=True)
    memory_grads = memory_grads.reshape(memory.shape).astype(f32)

    grad_low = grad_rows.astype(bf16)
    exit_self_part = mm(grad_low, self_rows, TN).astype(bf16)
    grad_self = mm(grad_low, exit_self_t).astype(bf16)
    grad_self = after(grad_self, second_grads)
    grad_self = head_swap(grad_self.reshape(row_count, head_count, local).transpose(1, 0, 2))
    grad_self = jnp.pad(grad_self.reshape(tok_rows, local), ((0, 0), (0, 256 - local)))
    grad_qkv = self_backward(qkv, grad_self, self_out, self_sums, starts)
    self_part = mm(hidden_one, grad_qkv, TN)
    grad_normed = mm(grad_qkv, self_weights, NT)
    inverse = lax.rsqrt(jnp.mean(stream * stream, axis=-1, keepdims=True) + norm_eps)
    gain_one = jnp.sum(grad_normed * stream * inverse, axis=0)
    grad_normed = head_swap(
        grad_normed.astype(bf16).reshape(head_count, row_count, width)
    ).astype(f32)
    grad_normed = jnp.sum(grad_normed, axis=0)
    grad_input, _ = rms_pull(stream_rows, gain_values[0], grad_normed)
    grad_rows = grad_rows + grad_input
    token_grads = head_spread(grad_rows.astype(bf16)).reshape(tok_rows, width).astype(f32)
    output = head_spread(output_rows.astype(bf16)).reshape(tok_rows, width).astype(f32)

    second_grads = second_grads.reshape(shard, 3, head_count, hidden).transpose(2, 0, 1, 3)
    second_grads = jnp.sum(head_swap(second_grads).astype(f32), axis=0)
    expand_grads = second_grads[:, 0:2].transpose(1, 0, 2)
    contract_grads = second_grads[:, 2].transpose(1, 0)

    first_part = jnp.concatenate([exit_self_part, query_part, pair_part, exit_cross_part], axis=1)
    first_grads = lax.psum_scatter(first_part, "dp", scatter_dimension=0, tiled=True)
    sets = first_grads.reshape(shard, 4, head_count, local)
    blocks = []
    for h in range(head_count):
        slot = order.index(h)
        mine = sets[:, 2].reshape(shard, 2, 2, local)[:, :, slot % 2]
        mine = jnp.where(group == h % 2, mine, jnp.zeros_like(mine))
        blocks.append(
            jnp.concatenate(
                [sets[:, 1, slot][:, None], mine, sets[:, 0, h][:, None], sets[:, 3, slot][:, None]],
                axis=1,
            )
        )
    first_grads = jnp.sum(head_swap(jnp.stack(blocks)).astype(f32), axis=0)
    exit_grads = first_grads[:, 3:5].transpose(1, 2, 0)

    gain_part = jnp.stack([gain_one, gain_two, gain_three])
    self_part = self_part.reshape(width, 3, 256)[:, :, 0:local].reshape(width, 3 * local)
    high, low = two_terms(gain_part.transpose(1, 0))
    self_part = jnp.concatenate([self_part.astype(bf16), high, low], axis=1)
    self_part = jnp.pad(self_part, ((0, 0), (0, 58)))
    self_grads = lax.all_to_all(
        self_part.reshape(dp_count, shard, -1), "dp", split_axis=0, concat_axis=0, tiled=True
    )
    self_grads = jnp.sum(self_grads.astype(f32), axis=0)
    gain_grads = self_grads[:, 3 * local : 3 * local + 3] + self_grads[:, 3 * local + 3 : 3 * local + 6]
    gain_grads = lax.psum(gain_grads, "head").transpose(1, 0)
    entry_grads = jnp.concatenate(
        [self_grads[:, 0 : 3 * local].reshape(shard, 3, local), first_grads[:, 0:3]], axis=1
    ).transpose(1, 0, 2)

    entry_mean, entry_square, entry_step = lamb_step(
        entry_weights, entry_grads, entry_first, entry_second, weight_decay
    )
    exit_mean, exit_square, exit_step = lamb_step(
        exit_weights, exit_grads, exit_first, exit_second, weight_decay
    )
    expand_mean, expand_square, expand_step = lamb_step(
        expand_weights, expand_grads, expand_first, expand_second, weight_decay
    )
    contract_mean, contract_square, contract_step = lamb_step(
        contract_weights, contract_grads, contract_first, contract_second, weight_decay
    )
    gains_mean, gains_square, gains_step = lamb_step(
        norm_gains, gain_grads, gains_first, gains_second, 0.0
    )
    weight_local = jnp.concatenate(
        [
            jnp.sum(entry_weights * entry_weights, axis=(1, 2)),
            jnp.sum(exit_weights * exit_weights, axis=(1, 2)),
            jnp.sum(expand_weights * expand_weights, axis=(1, 2)),
            jnp.sum(contract_weights * contract_weights).reshape(1),
            jnp.sum(norm_gains * norm_gains, axis=1) / head_count,
        ]
    )
    step_local = jnp.concatenate(
        [
            jnp.sum(entry_step * entry_step, axis=(1, 2)),
            jnp.sum(exit_step * exit_step, axis=(1, 2)),
            jnp.sum(expand_step * expand_step, axis=(1, 2)),
            jnp.sum(contract_step * contract_step).reshape(1),
            jnp.sum(gains_step * gains_step, axis=1) / head_count,
        ]
    )
    weight_squares, step_squares = lax.psum(lax.psum(jnp.stack([weight_local, step_local]), "dp"), "head")
    weight_norm = jnp.sqrt(weight_squares)
    step_norm = jnp.sqrt(step_squares)
    ratio = learn_rate * weight_norm / (step_norm + adam_eps)
    entry_new = entry_weights - ratio[0:6][:, None, None] * entry_step
    exit_new = exit_weights - ratio[6:8][:, None, None] * exit_step
    expand_new = expand_weights - ratio[8:10][:, None, None] * expand_step
    contract_new = contract_weights - ratio[10] * contract_step
    gains_new = norm_gains - ratio[11:14][:, None] * gains_step
    trust_norms = jnp.stack([weight_norm, step_norm])
    return (
        output,
        token_grads,
        memory_grads,
        entry_grads,
        exit_grads,
        expand_grads,
        contract_grads,
        gain_grads,
        entry_mean,
        exit_mean,
        expand_mean,
        contract_mean,
        gains_mean,
        entry_square,
        exit_square,
        expand_square,
        contract_square,
        gains_square,
        entry_new,
        exit_new,
        expand_new,
        contract_new,
        gains_new,
        entry_new.astype(jnp.bfloat16),
        exit_new.astype(jnp.bfloat16),
        expand_new.astype(jnp.bfloat16),
        contract_new.astype(jnp.bfloat16),
        trust_norms,
    )


def solution(mesh):
    in_specs = (
        P("dp", None),
        P(None, ("dp", "head"), None),
        P("dp", None),
        P("dp"),
        P("dp"),
        P("dp"),
        P(None, "dp", "head"),
        P(None, "head", "dp"),
        P(None, "dp", "head"),
        P("head", "dp"),
        P(None, "dp"),
        P(None, "dp", "head"),
        P(None, "dp", "head"),
        P(None, "head", "dp"),
        P(None, "head", "dp"),
        P(None, "dp", "head"),
        P(None, "dp", "head"),
        P("head", "dp"),
        P("head", "dp"),
        P(None, "dp"),
        P(None, "dp"),
    )
    out_specs = (
        P("dp", None),
        P("dp", None),
        P(None, ("dp", "head"), None),
        P(None, "dp", "head"),
        P(None, "head", "dp"),
        P(None, "dp", "head"),
        P("head", "dp"),
        P(None, "dp"),
        P(None, "dp", "head"),
        P(None, "head", "dp"),
        P(None, "dp", "head"),
        P("head", "dp"),
        P(None, "dp"),
        P(None, "dp", "head"),
        P(None, "head", "dp"),
        P(None, "dp", "head"),
        P("head", "dp"),
        P(None, "dp"),
        P(None, "dp", "head"),
        P(None, "head", "dp"),
        P(None, "dp", "head"),
        P("head", "dp"),
        P(None, "dp"),
        P(None, "dp", "head"),
        P(None, "head", "dp"),
        P(None, "dp", "head"),
        P("head", "dp"),
        P(),
    )
    return jax.shard_map(
        per_device, mesh=mesh, in_specs=in_specs, out_specs=out_specs, check_vma=False
    )
```

time: 1930 us -> 664 us (0.34)
  waiting for transfers between devices: 995 us -> 166 us
  matrix products: 296 us -> 68.2 us
  local copies, waits for them, and re-layouts: 294 us -> 74.4 us
  loops' own time: 95.1 us -> 0 us
  starting transfers between devices: 11.4 us -> 89 us
  other arithmetic: 139 us -> 69.7 us
  Pallas kernels: 0 us -> 65.6 us
  blocking collectives: 68.8 us -> 107 us
    psum x5 -> x0, waiting for transfers between devices: 535 us -> none  [head_total(): return lax.psum(partial_value, 'head')]
    dot_general x104 -> x36, matrix products: 293 us -> 68.2 us  [the longest x30 65.9 us: mm(): return lax.dot_general(a, b, dims, preferred_element_type=jnp.float32)]
    reduce_scatter x2 -> x1, waiting for transfers between devices: 157 us -> 0.02 us  [per_device(): lax.psum_scatter(second_part, 'dp', scatter_dimension=0, tiled=True)]
    unnamed x18 -> x6, waiting for transfers between devices: 140 us -> 0.1 us
    another operation x4 -> x0, loops' own time: 95.1 us -> none  [the longest x2 47.6 us: attend_forward(): results, log_sums = lax.map(single, jnp.arange(head_count * block_count))]
    all_to_all x2 -> x14, starting transfers between devices: 9.8 us -> 85.5 us  [the longest x11 72.5 us: head_swap(): lax.all_to_all(blocks, 'head', split_axis=0, concat_axis=0, tiled=True)]
    pallas_call x0 -> x4, Pallas kernels: none -> 65.6 us  [the longest x1 26.3 us: cross_backward(): pl.pallas_call(cross_backward_kernel, grid=(groups,), in_specs=[pl.BlockS...]
    reshape x11, local copies, waits for them, and re-layouts: 65.5 us -> 8.65 us  [the longest x2 5.31 us: per_device(): second_grads.reshape(shard, 3, head_count, hidden).transpose(2, 0, 1, 3)]
  transfers between devices with their start and end apart: 16 -> 21, of which waited for: 15 -> 13; matrix products, arithmetic and copies ran while one was open for 13% -> 26% of each run, Pallas kernels for 0% -> 10%
where the time goes in v1:
time: 664 us; the launch traced here: 655 us
  waiting for transfers between devices  166 us (25%)
  blocking collectives  107 us (16%)
  starting transfers between devices  89 us (13%)
  local copies, waits for them, and re-layouts  74.4 us (11%)
  other arithmetic  69.7 us (10%)
  matrix products  68.2 us (10%)
  Pallas kernels  65.6 us (10%)
  between operations  15.8 us (2%)
    all_to_all x11, starting transfers between devices, head_swap(): lax.all_to_all(blocks, 'head', split_axis=0, concat_axis=0, tiled=True)  72.5 us
    all_to_all x11, waiting for transfers between devices, head_swap(): lax.all_to_all(blocks, 'head', split_axis=0, concat_axis=0, tiled=True)  70.1 us
    dot_general x30, matrix products, mm(): return lax.dot_general(a, b, dims, preferred_element_type=jnp.float32)  65.9 us
    unnamed x132, local copies, waits for them, and re-layouts  41.8 us
    all_to_all x1, blocking collectives, head_swap(): lax.all_to_all(blocks, 'head', split_axis=0, concat_axis=0, tiled=True)  31.2 us
    ppermute x1, waiting for transfers between devices, per_device(): other = lax.ppermute(moved, 'head', near)  29.9 us
    pallas_call x1, Pallas kernels, cross_backward(): pl.pallas_call(cross_backward_kernel, grid=(groups,), in_specs=[pl.BlockS...  26.3 us
    pallas_call x1, Pallas kernels, cross_forward(): pl.pallas_call(cross_forward_kernel, grid=(groups,), in_specs=[pl.BlockSp...  26 us
  transfers between devices with their start and end apart: 21, of which 13 were waited for; matrix products, arithmetic and copies ran while one was open for 26% of the time, Pallas kernels for 10%

profile of v1, /device:TPU:18, one launch (start us, length us, event | category | flops | bytes accessed | tf_op | source)
XLA Modules:
  0.0 655.3 jit_solution(321964497168196813)
XLA Ops:
  10.9 20.4 %all-gather = bf16[384,5,192]{2,0,1:T(8,128)(2,1)S(1)} all-gather(bf16[96,5,192]{2,0,1:T(8,128)(2,1)S(1)} %pad_maximum_fusion.14), channel_id=2, replica_groups=mesh['dp'=8,'head'=4] {'head'}, dimensions={0}, use_global_device_ids=true | all-gather | bytes 921600 | tf_op jit(solution)/shard_map/all_gather | solution.py:460
  36.8 31.2 %all_to_all.75 = bf16[4,96,3,512]{3,1,2,0:T(8,128)(2,1)S(1)} all-to-all(bf16[4,96,3,512]{3,1,2,0:T(8,128)(2,1)S(1)} %broadcast_in_dim.28), channel_id=1, replica_groups=mesh['dp'=8,'head'=4] {'head'}, dimensions={0} | all-to-all | bytes 2359296 | tf_op jit(solution)/shard_map/all_to_all | solution.py:383
  70.6 7.5 %all-gather.7.cloned.1.call-done = bf16[768,3072]{1,0:T(8,128)(2,1)} async-done(((bf16[96,3072]{1,0:T(8,128)(2,1)}), bf16[768,3072]{1,0:T(8,128)(2,1)}) %all-gather.7.cloned.1.call-update) | async-done | bytes 4718608 | tf_op jit(solution)/shard_map/all_gather | solution.py:479
  78.4 4.6 all-to-all-start.2
  88.1 5.8 self_forward.1
  96.0 17.1 %all-to-all-done.2 = bf16[8,128,768]{2,1,0:T(8,128)(2,1)S(1)} async-done(((bf16[8,128,768]{2,1,0:T(8,128)(2,1)}), bf16[8,128,768]{2,1,0:T(8,128)(2,1)S(1)}, u32[]{:S(2)}, u32[]{:S(2)}) %all-to-all-start.2) | async-done | bytes 1572896 | tf_op jit(solution)/shard_map/all_to_all | solution.py:487
  113.1 5.1 all-to-all-start
  118.2 3.3 convert_element_type.296
  130.5 7.0 %all-to-all-start.1 = ((bf16[4,256,384]{2,1,0:T(8,128)(2,1)}), bf16[4,256,384]{2,1,0:T(8,128)(2,1)S(1)}, u32[]{:S(2)}, u32[]{:S(2)}) async-start(bf16[4,256,384]{2,1,0:T(8,128)(2,1)} %pad_maximum_fusion.6), calls=%async_computation.1 | async-start | bytes 1572864 | tf_op jit(solution)/shard_map/all_to_all | solution.py:383
  138.8 29.9 %collective-permute-done = bf16[2,512,768]{2,1,0:T(8,128)(2,1)} collective-permute-done((bf16[2,512,768]{2,1,0:T(8,128)(2,1)}, bf16[2,512,768]{2,1,0:T(8,128)(2,1)}, u32[]{:S(2)}, u32[]{:S(2)}) %collective-permute-start) | collective-permute-done | bytes 1572896 | tf_op jit(solution)/shard_map/ppermute | solution.py:494
  172.5 5.2 convolution_convert_fusion.3.key_ref.value_ref
  179.0 26.0 %cross_forward.1 = (bf16[1024,384]{1,0:T(8,128)(2,1)S(1)}, f32[3,8,1024]{2,1,0:T(8,128)S(1)}) custom-call(s32[1]{0:T(128)} %slice.324.split_ref, bf16[1024,384]{1,0:T(8,128)(2,1)S(1)} %fusion.37.query_ref, bf16[2048,768]{1,0:T(8,128)(2,1)} %convolution_convert_fusion.3.key_ref.value_ref, bf16[2048,768]{1,0:T(8,128)(2,1)} %convolution_convert_fusion.3.key_ref.value_ref), custom_call_target="tpu_custom_call" | custom-call | flops 3221225472 | bytes 3145728 | tf_op jit(solution)/shard_map/cross_forward/pallas_call | solution.py:247
  208.1 6.1 all-to-all-start.3
  214.7 12.4 %all-to-all-done.3 = bf16[4,272,384]{2,1,0:T(8,128)(2,1)S(1)} async-done(((bf16[4,272,384]{2,1,0:T(8,128)(2,1)}), bf16[4,272,384]{2,1,0:T(8,128)(2,1)S(1)}, u32[]{:S(2)}, u32[]{:S(2)}) %all-to-all-start.3) | async-done | bytes 835616 | tf_op jit(solution)/shard_map/all_to_all | solution.py:383
  231.2 3.0 fusion.14
  234.3 2.9 fusion.8
  237.2 4.5 fusion.26
  245.1 4.5 pad_maximum_fusion
  250.5 3.3 fusion.12
  253.8 3.1 multiply_reduce_fusion.2
  262.5 7.5 %all-to-all-start.6 = ((bf16[4,288,384]{2,1,0:T(8,128)(2,1)}), bf16[4,288,384]{2,1,0:T(8,128)(2,1)}, u32[]{:S(2)}, u32[]{:S(2)}) async-start(bf16[4,288,384]{2,1,0:T(8,128)(2,1)} %pad_maximum_fusion.5), calls=%async_computation.6 | async-start | bytes 1769472 | tf_op jit(solution)/shard_map/all_to_all | solution.py:383
  271.7 14.2 %all-to-all-done.6 = bf16[4,288,384]{2,1,0:T(8,128)(2,1)} async-done(((bf16[4,288,384]{2,1,0:T(8,128)(2,1)}), bf16[4,288,384]{2,1,0:T(8,128)(2,1)}, u32[]{:S(2)}, u32[]{:S(2)}) %all-to-all-start.6) | async-done | bytes 884768 | tf_op jit(solution)/shard_map/all_to_all | solution.py:383
  290.1 26.3 %cross_backward.1 = (bf16[1024,384]{1,0:T(8,128)(2,1)S(1)}, bf16[2048,384]{1,0:T(8,128)(2,1)S(1)}, bf16[2048,384]{1,0:T(8,128)(2,1)}) custom-call(s32[1]{0:T(128)} %slice.324.split_ref, bf16[1024,384]{1,0:T(8,128)(2,1)S(1)} %fusion.37.query_ref, bf16[1024,384]{1,0:T(8,128)(2,1)S(1)} %fusion.38.grad_ref, f32[3,8,1024]{2,1,0:T(8,128)S(1)} %maximum_maximum_fusion.stats_ref, ...), custom_call_target="tpu_custom_call" | custom-call | flops 8053063680 | bytes 6291456 | tf_op jit(solution)/shard_map/cross_backward/pallas_call | solution.py:339
  318.6 6.9 %all-to-all-start.7 = ((bf16[4,256,384]{2,1,0:T(8,128)(2,1)}), bf16[4,256,384]{2,1,0:T(8,128)(2,1)S(1)}, u32[]{:S(2)}, u32[]{:S(2)}) async-start(bf16[4,256,384]{2,1,0:T(8,128)(2,1)} %bitcast.298), calls=%async_computation.7 | async-start | bytes 1572864 | tf_op jit(solution)/shard_map/all_to_all | solution.py:383
  329.0 3.8 convolution_convert_fusion.7
  332.8 8.0 %all-to-all-done.7 = bf16[4,256,384]{2,1,0:T(8,128)(2,1)S(1)} async-done(((bf16[4,256,384]{2,1,0:T(8,128)(2,1)}), bf16[4,256,384]{2,1,0:T(8,128)(2,1)S(1)}, u32[]{:S(2)}, u32[]{:S(2)}) %all-to-all-start.7) | async-done | bytes 786464 | tf_op jit(solution)/shard_map/all_to_all | solution.py:383
  348.2 6.7 %copy.376 = bf16[768,3072]{1,0:T(8,128)(2,1)} copy(bf16[768,3072]{0,1:T(8,128)(2,1)} %pad_maximum_fusion.1) | data formatting | bytes 9437184
  356.4 2.9 fusion.45
  360.5 6.8 %all-to-all-start.5 = ((bf16[4,256,768]{2,1,0:T(8,128)(2,1)}), bf16[4,256,768]{2,1,0:T(8,128)(2,1)S(1)}, u32[]{:S(2)}, u32[]{:S(2)}) async-start(bf16[4,256,768]{2,1,0:T(8,128)(2,1)} %broadcast_in_dim.29), calls=%async_computation.5 | async-start | bytes 3145728 | tf_op jit(solution)/shard_map/all_to_all | solution.py:383
  367.4 5.5 fusion.55
  381.3 19.3 %all-to-all-done.5 = bf16[4,256,768]{2,1,0:T(8,128)(2,1)S(1)} async-done(((bf16[4,256,768]{2,1,0:T(8,128)(2,1)}), bf16[4,256,768]{2,1,0:T(8,128)(2,1)S(1)}, u32[]{:S(2)}, u32[]{:S(2)}) %all-to-all-start.5) | async-done | bytes 1572896 | tf_op jit(solution)/shard_map/all_to_all | solution.py:383
  400.6 6.8 %all-to-all-start.8 = ((bf16[4,256,192]{1,2,0:T(8,128)(2,1)}), bf16[4,256,192]{1,2,0:T(8,128)(2,1)S(1)}, u32[]{:S(2)}, u32[]{:S(2)}) async-start(bf16[4,256,192]{1,2,0:T(8,128)(2,1)} %bitcast.293), calls=%async_computation.9 | async-start | bytes 786432 | tf_op jit(solution)/shard_map/all_to_all | solution.py:383
  407.4 22.6 %collective-permute-done.1 = bf16[2,512,768]{2,1,0:T(8,128)(2,1)} collective-permute-done((bf16[2,512,768]{2,1,0:T(8,128)(2,1)}, bf16[2,512,768]{2,1,0:T(8,128)(2,1)}, u32[]{:S(2)}, u32[]{:S(2)}) %collective-permute-start.1) | collective-permute-done | bytes 1572896 | tf_op jit(solution)/shard_map/ppermute | solution.py:650
  433.9 4.2 all-to-all-start.11
  446.2 10.7 %all-to-all-done.11 = bf16[8,128,768]{2,1,0:T(8,128)(2,1)} async-done(((bf16[8,128,768]{2,1,0:T(8,128)(2,1)}), bf16[8,128,768]{2,1,0:T(8,128)(2,1)}, u32[]{:S(2)}, u32[]{:S(2)}) %all-to-all-start.11) | async-done | bytes 1572896 | tf_op jit(solution)/shard_map/all_to_all | solution.py:657
  456.9 7.4 %all-to-all-start.13 = ((bf16[4,96,5,192]{1,3,2,0:T(8,128)(2,1)}), bf16[4,96,5,192]{1,3,2,0:T(8,128)(2,1)}, u32[]{:S(2)}, u32[]{:S(2)}) async-start(bf16[4,96,5,192]{1,3,2,0:T(8,128)(2,1)} %pad_maximum_fusion.3), calls=%async_computation.14 | async-start | bytes 1966080 | tf_op jit(solution)/shard_map/all_to_all | solution.py:383
  464.2 7.5 %self_backward.1 = bf16[1024,768]{1,0:T(8,128)(2,1)S(1)} custom-call(bf16[1024,768]{1,0:T(8,128)(2,1)} %copy-done, bf16[1024,256]{1,0:T(8,128)(2,1)S(1)} %pad.28.grad_ref, bf16[1024,256]{1,0:T(8,128)(2,1)S(1)} %get-tuple-element.41.out_ref, f32[8,1024]{1,0:T(8,128)S(1)} %get-tuple-element.49.sums_ref, s32[1,1024]{1,0:T(1,128)S(1)} %bitcast.273), custom_call_target="tpu_custom_call" | custom-call | flops 2013265920 | bytes 5242880 | tf_op jit(solution)/shard_map/self_backward/pallas_call | solution.py:176
  481.6 4.1 all-to-all-done.13
  485.8 4.2 all-to-all-start.12
  495.3 7.1 %all-to-all-done.12 = bf16[8,96,640]{2,1,0:T(8,128)(2,1)} async-done(((bf16[8,96,640]{2,1,0:T(8,128)(2,1)}), bf16[8,96,640]{2,1,0:T(8,128)(2,1)}, u32[]{:S(2)}, u32[]{:S(2)}) %all-to-all-start.12) | async-done | bytes 983072 | tf_op jit(solution)/shard_map/all_to_all | solution.py:707
  502.4 7.6 %all-to-all-start.14 = ((bf16[4,96,3,512]{3,1,2,0:T(8,128)(2,1)}), bf16[4,96,3,512]{3,1,2,0:T(8,128)(2,1)}, u32[]{:S(2)}, u32[]{:S(2)}) async-start(bf16[4,96,3,512]{3,1,2,0:T(8,128)(2,1)} %bitcast.276), calls=%async_computation.15 | async-start | bytes 2359296 | tf_op jit(solution)/shard_map/all_to_all | solution.py:383
  518.8 3.4 convert.42
  523.8 12.0 %all-to-all-done.14 = bf16[4,96,3,512]{3,1,2,0:T(8,128)(2,1)} async-done(((bf16[4,96,3,512]{3,1,2,0:T(8,128)(2,1)}), bf16[4,96,3,512]{3,1,2,0:T(8,128)(2,1)}, u32[]{:S(2)}, u32[]{:S(2)}) %all-to-all-start.14) | async-done | bytes 1179680 | tf_op jit(solution)/shard_map/all_to_all | solution.py:383
  535.8 7.2 %all-to-all-start.9 = ((bf16[4,256,768]{2,1,0:T(8,128)(2,1)}), bf16[4,256,768]{2,1,0:T(8,128)(2,1)S(1)}, u32[]{:S(2)}, u32[]{:S(2)}) async-start(bf16[4,256,768]{2,1,0:T(8,128)(2,1)} %bitcast.292), calls=%async_computation.10 | async-start | bytes 3145728 | tf_op jit(solution)/shard_map/all_to_all | solution.py:383
  560.8 19.7 %psum.21 = f32[3,96]{1,0:T(4,128)S(1)} all-reduce(f32[3,96]{1,0:T(4,128)S(1)} %add_bitcast_fusion.1), channel_id=1, replica_groups=mesh['dp'=8,'head'=4] {'head'}, use_global_device_ids=true, to_apply=%region_25.26 | all-reduce | flops 288 | bytes 2304 | tf_op jit(solution)/shard_map/psum | solution.py:712
  592.4 4.2 all-to-all-start.10
  596.6 10.6 %psum.22 = f32[2,14]{1,0:T(2,128)S(1)} all-reduce(f32[2,14]{1,0:T(2,128)S(1)} %pad_maximum_fusion.21), channel_id=1, replica_groups=mesh['dp'=8,'head'=4] {'dp'}, use_global_device_ids=true, to_apply=%region_36.37 | all-reduce | flops 28 | bytes 224 | tf_op jit(solution)/shard_map/psum | solution.py:750
  607.2 25.4 %psum.23 = f32[2,14]{1,0:T(2,128)S(1)} all-reduce(f32[2,14]{1,0:T(2,128)S(1)} %psum.22), channel_id=1, replica_groups=mesh['dp'=8,'head'=4] {'head'}, use_global_device_ids=true, to_apply=%region_37.38 | all-reduce | flops 28 | bytes 224 | tf_op jit(solution)/shard_map/psum | solution.py:750
  (334 shorter events, 164.2 us)
Async XLA Ops:
  7.2 29.5 %all-gather.5.cloned.1.call-start = ((), (), s32[]{:S(2)}) async-start(), calls=%async_computation.17 | async-start | bytes 1548288 | tf_op jit(solution)/shard_map/all_gather | solution.py:462
  10.7 67.5 %all-gather.7.cloned.1.call-start = ((), (), s32[]{:S(2)}) async-start(), calls=%async_computation.18 | async-start | bytes 5308416 | tf_op jit(solution)/shard_map/all_gather | solution.py:479
  36.1 195.1 %all-gather.9.cloned.1.call-start = ((), (), s32[]{:S(2)}) async-start(), calls=%async_computation.19 | async-start | bytes 10616832 | tf_op jit(solution)/shard_map/all_gather | solution.py:500
  68.9 9.2 %copy-start.56 = (s32[8]{0:T(128)S(1)}, s32[8]{0:T(128)}, u32[]{:S(2)}) copy-start(s32[8]{0:T(128)} %param.26) | copy-start | bytes 100
  78.4 34.7 %all-to-all-start.2 = ((bf16[8,128,768]{2,1,0:T(8,128)(2,1)}), bf16[8,128,768]{2,1,0:T(8,128)(2,1)S(1)}, u32[]{:S(2)}, u32[]{:S(2)}) async-start(bf16[8,128,768]{2,1,0:T(8,128)(2,1)} %bitcast.291), calls=%async_computation.2 | async-start | bytes 3145728 | tf_op jit(solution)/shard_map/all_to_all | solution.py:487
  83.0 3.6 copy-start.5
  88.1 30.1 %copy-start.55 = (s32[8]{0:T(128)S(1)}, s32[8]{0:T(128)}, u32[]{:S(2)}) copy-start(s32[8]{0:T(128)} %param.28) | copy-start | bytes 100
  113.1 12.1 %all-to-all-start = ((bf16[4,256,192]{1,2,0:T(8,128)(2,1)}), bf16[4,256,192]{1,2,0:T(8,128)(2,1)S(1)}, u32[]{:S(2)}, u32[]{:S(2)}) async-start(bf16[4,256,192]{1,2,0:T(8,128)(2,1)} %copy.342), calls=%async_computation | async-start | bytes 786432 | tf_op jit(solution)/shard_map/all_to_all | solution.py:383
  123.7 45.1 %collective-permute-start = (bf16[2,512,768]{2,1,0:T(8,128)(2,1)}, bf16[2,512,768]{2,1,0:T(8,128)(2,1)}, u32[]{:S(2)}, u32[]{:S(2)}) collective-permute-start(bf16[2,512,768]{2,1,0:T(8,128)(2,1)} %bitcast.27), channel_id=1, source_target_pairs={{0,1},{1,0},{2,3},{3,2},{4,5},{5,4},{6,7},{7,6},{8,9},{9,8},{10,11... | collective-permute-start | bytes 4718600 | tf_op jit(solution)/shard_map/ppermute | solution.py:494
  127.3 101.7 %copy-start.3 = (f32[256,768]{1,0:T(8,128)}, f32[256,768]{1,0:T(8,128)S(1)}, u32[]{:S(2)}) copy-start(f32[256,768]{1,0:T(8,128)S(1)} %get-tuple-element.382) | copy-start | bytes 2359300
  130.5 47.2 %all-to-all-start.1 = ((bf16[4,256,384]{2,1,0:T(8,128)(2,1)}), bf16[4,256,384]{2,1,0:T(8,128)(2,1)S(1)}, u32[]{:S(2)}, u32[]{:S(2)}) async-start(bf16[4,256,384]{2,1,0:T(8,128)(2,1)} %pad_maximum_fusion.6), calls=%async_computation.1 | async-start | bytes 1572864 | tf_op jit(solution)/shard_map/all_to_all | solution.py:383
  207.2 7.3 %copy-start.52 = (f32[3]{0:T(128)S(1)}, f32[3]{0:T(128)}, u32[]{:S(2)}) copy-start(f32[3]{0:T(128)} %constant.171.clone) | copy-start | bytes 40
  208.1 18.9 %all-to-all-start.3 = ((bf16[4,272,384]{2,1,0:T(8,128)(2,1)}), bf16[4,272,384]{2,1,0:T(8,128)(2,1)S(1)}, u32[]{:S(2)}, u32[]{:S(2)}) async-start(bf16[4,272,384]{2,1,0:T(8,128)(2,1)} %fusion.66), calls=%async_computation.3 | async-start | bytes 1671168 | tf_op jit(solution)/shard_map/all_to_all | solution.py:383
  214.3 166.1 %reduce-scatter.5.cloned.1.call-start = ((), (), s32[]{:S(2)}) async-start(), calls=%async_computation.20 | async-start | bytes 10616832 | tf_op jit(solution)/shard_map/reduce_scatter | solution.py:608
  231.0 26.0 %copy-start.14 = (f32[256,768]{1,0:T(8,128)}, f32[256,768]{1,0:T(8,128)S(1)}, u32[]{:S(2)}) copy-start(f32[256,768]{1,0:T(8,128)S(1)} %get-tuple-element.384) | copy-start | bytes 2359300
  258.4 11.7 %copy-start.1 = (f32[256,768]{1,0:T(8,128)}, f32[256,768]{1,0:T(8,128)S(1)}, u32[]{:S(2)}) copy-start(f32[256,768]{1,0:T(8,128)S(1)} %multiply_add_fusion.1) | copy-start | bytes 2359300
  261.3 8.7 %copy-start.24 = (bf16[256,384]{1,0:T(8,128)(2,1)S(1)}, bf16[256,384]{1,0:T(8,128)(2,1)}, u32[]{:S(2)}) copy-start(bf16[256,384]{1,0:T(8,128)(2,1)} %copy-done.22) | copy-start | bytes 589828
  261.4 8.7 %copy-start.27 = (bf16[256,384]{1,0:T(8,128)(2,1)S(1)}, bf16[256,384]{1,0:T(8,128)(2,1)}, u32[]{:S(2)}) copy-start(bf16[256,384]{1,0:T(8,128)(2,1)} %copy-done.25) | copy-start | bytes 589828
  262.5 23.4 %all-to-all-start.6 = ((bf16[4,288,384]{2,1,0:T(8,128)(2,1)}), bf16[4,288,384]{2,1,0:T(8,128)(2,1)}, u32[]{:S(2)}, u32[]{:S(2)}) async-start(bf16[4,288,384]{2,1,0:T(8,128)(2,1)} %pad_maximum_fusion.5), calls=%async_computation.6 | async-start | bytes 1769472 | tf_op jit(solution)/shard_map/all_to_all | solution.py:383
  318.6 22.3 %all-to-all-start.7 = ((bf16[4,256,384]{2,1,0:T(8,128)(2,1)}), bf16[4,256,384]{2,1,0:T(8,128)(2,1)S(1)}, u32[]{:S(2)}, u32[]{:S(2)}) async-start(bf16[4,256,384]{2,1,0:T(8,128)(2,1)} %bitcast.298), calls=%async_computation.7 | async-start | bytes 1572864 | tf_op jit(solution)/shard_map/all_to_all | solution.py:383
  325.4 112.8 %reduce-scatter.7.cloned.1.call-start = ((), (), s32[]{:S(2)}) async-start(), calls=%async_computation.21 | async-start | bytes 5308416
  332.8 8.2 %copy-start.4 = (f32[256,768]{1,0:T(8,128)S(1)}, f32[256,768]{1,0:T(8,128)}, u32[]{:S(2)}) copy-start(f32[256,768]{1,0:T(8,128)} %copy-done.3) | copy-start | bytes 2359300
  360.5 40.1 %all-to-all-start.5 = ((bf16[4,256,768]{2,1,0:T(8,128)(2,1)}), bf16[4,256,768]{2,1,0:T(8,128)(2,1)S(1)}, u32[]{:S(2)}, u32[]{:S(2)}) async-start(bf16[4,256,768]{2,1,0:T(8,128)(2,1)} %broadcast_in_dim.29), calls=%async_computation.5 | async-start | bytes 3145728 | tf_op jit(solution)/shard_map/all_to_all | solution.py:383
  376.8 53.2 %collective-permute-start.1 = (bf16[2,512,768]{2,1,0:T(8,128)(2,1)}, bf16[2,512,768]{2,1,0:T(8,128)(2,1)}, u32[]{:S(2)}, u32[]{:S(2)}) collective-permute-start(bf16[2,512,768]{2,1,0:T(8,128)(2,1)} %fusion.34), channel_id=1, source_target_pairs={{0,1},{1,0},{2,3},{3,2},{4,5},{5,4},{6,7},{7,6},{8,9},{9,8},{10,11... | collective-permute-start | bytes 4718600 | tf_op jit(solution)/shard_map/ppermute | solution.py:650
  400.6 33.3 %all-to-all-start.8 = ((bf16[4,256,192]{1,2,0:T(8,128)(2,1)}), bf16[4,256,192]{1,2,0:T(8,128)(2,1)S(1)}, u32[]{:S(2)}, u32[]{:S(2)}) async-start(bf16[4,256,192]{1,2,0:T(8,128)(2,1)} %bitcast.293), calls=%async_computation.9 | async-start | bytes 786432 | tf_op jit(solution)/shard_map/all_to_all | solution.py:383
  433.9 22.9 %all-to-all-start.11 = ((bf16[8,128,768]{2,1,0:T(8,128)(2,1)}), bf16[8,128,768]{2,1,0:T(8,128)(2,1)}, u32[]{:S(2)}, u32[]{:S(2)}) async-start(bf16[8,128,768]{2,1,0:T(8,128)(2,1)} %bitcast.63), calls=%async_computation.12 | async-start | bytes 3145728 | tf_op jit(solution)/shard_map/all_to_all | solution.py:657
  456.9 28.9 %all-to-all-start.13 = ((bf16[4,96,5,192]{1,3,2,0:T(8,128)(2,1)}), bf16[4,96,5,192]{1,3,2,0:T(8,128)(2,1)}, u32[]{:S(2)}, u32[]{:S(2)}) async-start(bf16[4,96,5,192]{1,3,2,0:T(8,128)(2,1)} %pad_maximum_fusion.3), calls=%async_computation.14 | async-start | bytes 1966080 | tf_op jit(solution)/shard_map/all_to_all | solution.py:383
  464.2 7.5 %copy-start.6 = (bf16[1024,768]{1,0:T(8,128)(2,1)S(1)}, bf16[1024,768]{1,0:T(8,128)(2,1)}, u32[]{:S(2)}) copy-start(bf16[1024,768]{1,0:T(8,128)(2,1)} %param.23) | copy-start | bytes 4718596
  464.2 7.5 %copy-start.47 = (bf16[768,896]{1,0:T(8,128)(2,1)S(1)}, bf16[768,896]{1,0:T(8,128)(2,1)}, u32[]{:S(2)}) copy-start(bf16[768,896]{1,0:T(8,128)(2,1)} %all-gather.5.cloned.1.call-done) | copy-start | bytes 4128772
  485.8 16.6 %all-to-all-start.12 = ((bf16[8,96,640]{2,1,0:T(8,128)(2,1)}), bf16[8,96,640]{2,1,0:T(8,128)(2,1)}, u32[]{:S(2)}, u32[]{:S(2)}) async-start(bf16[8,96,640]{2,1,0:T(8,128)(2,1)} %bitcast.278), calls=%async_computation.13 | async-start | bytes 1966080 | tf_op jit(solution)/shard_map/all_to_all | solution.py:707
  502.4 33.4 %all-to-all-start.14 = ((bf16[4,96,3,512]{3,1,2,0:T(8,128)(2,1)}), bf16[4,96,3,512]{3,1,2,0:T(8,128)(2,1)}, u32[]{:S(2)}, u32[]{:S(2)}) async-start(bf16[4,96,3,512]{3,1,2,0:T(8,128)(2,1)} %bitcast.276), calls=%async_computation.15 | async-start | bytes 2359296 | tf_op jit(solution)/shard_map/all_to_all | solution.py:383
  523.7 12.1 %copy-start.16 = (f32[96,5,192]{0,2,1:T(8,128)}, f32[96,5,192]{0,2,1:T(8,128)S(1)}, u32[]{:S(2)}) copy-start(f32[96,5,192]{0,2,1:T(8,128)S(1)} %convert_reduce_fusion.2) | copy-start | bytes 1105924
  523.7 19.2 %copy-start.20 = (f32[2,192,96]{2,1,0:T(8,128)S(1)}, f32[2,192,96]{2,1,0:T(8,128)}, u32[]{:S(2)}) copy-start(f32[2,192,96]{2,1,0:T(8,128)} %param.30) | copy-start | bytes 442372
  535.8 52.3 %all-to-all-start.9 = ((bf16[4,256,768]{2,1,0:T(8,128)(2,1)}), bf16[4,256,768]{2,1,0:T(8,128)(2,1)S(1)}, u32[]{:S(2)}, u32[]{:S(2)}) async-start(bf16[4,256,768]{2,1,0:T(8,128)(2,1)} %bitcast.292), calls=%async_computation.10 | async-start | bytes 3145728 | tf_op jit(solution)/shard_map/all_to_all | solution.py:383
  553.6 26.9 %copy-start.48 = (f32[3,96]{1,0:T(4,128)S(1)}, f32[3,96]{1,0:T(4,128)}, u32[]{:S(2)}) copy-start(f32[3,96]{1,0:T(4,128)} %param.33) | copy-start | bytes 3460
  553.6 26.9 %copy-start.50 = (f32[3,96]{1,0:T(4,128)S(1)}, f32[3,96]{1,0:T(4,128)}, u32[]{:S(2)}) copy-start(f32[3,96]{1,0:T(4,128)} %param.43) | copy-start | bytes 3460
  553.6 26.9 %copy-start.51 = (f32[3,96]{1,0:T(4,128)S(1)}, f32[3,96]{1,0:T(4,128)}, u32[]{:S(2)}) copy-start(f32[3,96]{1,0:T(4,128)} %param.42) | copy-start | bytes 3460
  558.7 26.7 %copy-start.11 = (f32[2,96,512]{2,1,0:T(8,128)S(1)}, f32[2,96,512]{2,1,0:T(8,128)}, u32[]{:S(2)}) copy-start(f32[2,96,512]{2,1,0:T(8,128)} %param.31) | copy-start | bytes 1179652
  580.5 6.1 copy-start.49
  580.5 4.8 copy-start.40
  580.6 4.8 copy-start.41
  591.1 42.1 %copy-start.7 = (f32[6,96,192]{1,2,0:T(8,128)S(1)}, f32[6,96,192]{1,2,0:T(8,128)}, u32[]{:S(2)}) copy-start(f32[6,96,192]{1,2,0:T(8,128)} %get-tuple-element.313) | copy-start | bytes 1327108
  592.4 54.0 %all-to-all-start.10 = ((bf16[4,256,768]{2,1,0:T(8,128)(2,1)}), bf16[4,256,768]{2,1,0:T(8,128)(2,1)S(1)}, u32[]{:S(2)}, u32[]{:S(2)}) async-start(bf16[4,256,768]{2,1,0:T(8,128)(2,1)} %broadcast_in_dim.31), calls=%async_computation.11 | async-start | bytes 3145728 | tf_op jit(solution)/shard_map/all_to_all | solution.py:383
  633.2 7.8 %copy-start.18 = (f32[512,96]{0,1:T(8,128)S(1)}, f32[512,96]{0,1:T(8,128)}, u32[]{:S(2)}) copy-start(f32[512,96]{0,1:T(8,128)} %param.32) | copy-start | bytes 589828
  635.6 8.0 %copy-start.21 = (f32[2,192,96]{2,1,0:T(8,128)S(1)}, f32[2,192,96]{2,1,0:T(8,128)}, u32[]{:S(2)}) copy-start(f32[2,192,96]{2,1,0:T(8,128)} %param.30) | copy-start | bytes 442372
  635.6 8.0 %copy-start.38 = (f32[2,192,96]{2,1,0:T(8,128)S(1)}, f32[2,192,96]{2,1,0:T(8,128)}, u32[]{:S(2)}) copy-start(f32[2,192,96]{2,1,0:T(8,128)} %get-tuple-element.309) | copy-start | bytes 442372
  635.6 9.7 %copy-start.29 = (f32[2,96,512]{2,1,0:T(8,128)S(1)}, f32[2,96,512]{2,1,0:T(8,128)}, u32[]{:S(2)}) copy-start(f32[2,96,512]{2,1,0:T(8,128)} %get-tuple-element.306) | copy-start | bytes 1179652
  635.6 9.7 %copy-start.30 = (f32[2,96,512]{2,1,0:T(8,128)S(1)}, f32[2,96,512]{2,1,0:T(8,128)}, u32[]{:S(2)}) copy-start(f32[2,96,512]{2,1,0:T(8,128)} %get-tuple-element.307) | copy-start | bytes 1179652
  (30 other events, 60.0 us)
Sparse Core Ops, SparseCore 0:
  10.8 25.9 all-gather.4
  39.2 38.9 all-gather.6
  80.0 70.1 all-gather.8
  249.8 77.2 reduce-scatter.4
  355.0 54.7 reduce-scatter.6

commit v2 on v1

--- a/solution.py
+++ b/solution.py
@@ -109,7 +109,7 @@
         ),
         compiler_params=pltpu.CompilerParams(vmem_limit_bytes=VMEM_LIMIT),
         cost_estimate=pl.CostEstimate(
-            flops=3 * rows * rows * 256, bytes_accessed=rows * 2048, transcendentals=2 * rows * rows
+            flops=6 * 10**9, bytes_accessed=rows * 2048, transcendentals=2 * rows * rows
         ),
         name="self_forward",
     )(qkv, starts)
@@ -182,7 +182,7 @@
         ],
         compiler_params=pltpu.CompilerParams(vmem_limit_bytes=VMEM_LIMIT),
         cost_estimate=pl.CostEstimate(
-            flops=3 * rows * rows * 640, bytes_accessed=rows * 5120, transcendentals=2 * rows * rows
+            flops=8 * 10**9, bytes_accessed=rows * 5120, transcendentals=2 * rows * rows
         ),
         name="self_backward",
     )(qkv, grad_out, out, sums, starts)
@@ -263,7 +263,7 @@
         ),
         compiler_params=pltpu.CompilerParams(vmem_limit_bytes=VMEM_LIMIT),
         cost_estimate=pl.CostEstimate(
-            flops=groups * rows * keys * 512,
+            flops=28 * 10**9,
             bytes_accessed=keys * 1536,
             transcendentals=groups * rows * keys,
         ),
@@ -363,12 +363,51 @@
         ],
         compiler_params=pltpu.CompilerParams(vmem_limit_bytes=VMEM_LIMIT),
         cost_estimate=pl.CostEstimate(
-            flops=groups * rows * keys * 1280,
+            flops=28 * 10**9,
             bytes_accessed=keys * 3072,
             transcendentals=groups * rows * keys,
         ),
         name="cross_backward",
     )(split, queries, grads, stats, pairs, pairs)
+
+
+def hidden_grads_kernel(rows_ref, grad_ref, gate_ref, up_ref, act_ref, out_ref):
+    part = pl.program_id(0)
+    source = (gate_ref, up_ref, act_ref)
+    for index in range(3):
+
+        @pl.when(part == index)
+        def _():
+            left = grad_ref if index == 2 else rows_ref
+            out_ref[...] = mm(left[...], source[index][...], TN).astype(jnp.bfloat16)
+
+
+def hidden_grads(rows, grads, gate, upward, act):
+    row_count, width = rows.shape
+    inner_width = gate.shape[1]
+    blocks = lax.axis_size("head")
+    block = inner_width // blocks
+    whole = pl.BlockSpec((row_count, width), lambda p, j: (0, 0))
+
+    def column(index):
+        return pl.BlockSpec(
+            (row_count, block), lambda p, j: (0, jnp.clip((p - index) * blocks + j, 0, blocks - 1))
+        )
+
+    return pl.pallas_call(
+        hidden_grads_kernel,
+        grid=(3, blocks),
+        in_specs=[whole, whole, column(0), column(1), column(2)],
+        out_specs=pl.BlockSpec((width, block), lambda p, j: (0, j * 3 + p)),
+        out_shape=jax.ShapeDtypeStruct((width, 3 * inner_width), jnp.bfloat16),
+        compiler_params=pltpu.CompilerParams(vmem_limit_bytes=VMEM_LIMIT),
+        cost_estimate=pl.CostEstimate(
+            flops=6 * row_count * width * inner_width,
+            bytes_accessed=6 * width * inner_width,
+            transcendentals=0,
+        ),
+        name="hidden_grads",
+    )(rows, grads, gate, upward, act)
 
 
 def rms_pull(values, gain, grad):
@@ -379,24 +418,90 @@
     return inverse * (scaled - hat * inner), jnp.sum(grad * hat, axis=0)
 
 
-def head_swap(blocks):
-    return lax.all_to_all(blocks, "head", split_axis=0, concat_axis=0, tiled=True)
-
-
 def two_terms(values):
     high = lax.reduce_precision(values, exponent_bits=8, mantissa_bits=7)
     return high.astype(jnp.bfloat16), (values - high).astype(jnp.bfloat16)
 
 
 def after(array, *earlier):
-    return lax.optimization_barrier((array, *earlier))[0]
-
-
-def head_spread(block):
+    marks = [e[(0,) * e.ndim].astype(jnp.float32) for e in earlier]
+    mark = sum(marks[1:], marks[0])
+    return jnp.where(mark == mark, array, jnp.asarray(jnp.nan, array.dtype))
+
+
+def pick(array, index):
+    return lax.dynamic_index_in_dim(array, index, 0, keepdims=False)
+
+
+def send(array, bits, axis=("dp", "head")):
+    dp_count = lax.axis_size("dp")
     head_count = lax.axis_size("head")
-    return head_swap(jnp.broadcast_to(block[None], (head_count, *block.shape)))
-
-
+    dp_bits, head_bits = bits
+    if head_bits == 0:
+        return lax.ppermute(array, "dp", [(s, s ^ dp_bits) for s in range(dp_count)])
+    if dp_bits == 0:
+        return lax.ppermute(array, "head", [(s, s ^ head_bits) for s in range(head_count)])
+    pairs = [
+        (i * head_count + h, (i ^ dp_bits) * head_count + (h ^ head_bits))
+        for i in range(dp_count)
+        for h in range(head_count)
+    ]
+    return lax.ppermute(array, ("dp", "head"), pairs)
+
+
+def in_order(pieces, index):
+    bit = 1
+    while bit < len(pieces):
+        flip = (index & bit) != 0
+        pieces = [jnp.where(flip, pieces[s ^ bit], pieces[s]) for s in range(len(pieces))]
+        bit *= 2
+    return pieces
+
+
+def head_spread(block, far, late=None):
+    head_count = lax.axis_size("head")
+    head_index = lax.axis_index("head")
+    held = jnp.stack(in_order([block, far], head_index // 2))
+    came = send(held, (0, 1))
+    came = came if late is None else after(came, late)
+    lower, upper = in_order([held, came], head_index % 2)
+    return [(lower, upper)[h % 2][h // 2] for h in range(head_count)]
+
+
+def chip_pieces(blocks, chip):
+    return [pick(blocks, chip)] + [
+        send(pick(blocks, chip ^ d), (2 * d, 0)) for d in range(1, blocks.shape[0])
+    ]
+
+
+def chip_spread(block, chip):
+    chips = lax.axis_size("dp") // 2
+    return in_order([block] + [send(block, (2 * d, 0)) for d in range(1, chips)], chip)
+
+
+def member_pieces(block_of):
+    return [block_of(0)] + [send(block_of(d), (d & 1, d >> 1)) for d in range(1, 4)]
+
+
+def head_halving(blocks):
+    head_count = lax.axis_size("head")
+    index = lax.axis_index("head")
+    low, high = index % 2, index // 2
+    by_low = blocks.reshape(head_count // 2, 2, *blocks.shape[1:])
+    mine = lax.dynamic_index_in_dim(by_low, low, 1, keepdims=False)
+    theirs = lax.dynamic_index_in_dim(by_low, 1 - low, 1, keepdims=False)
+    both = mine.astype(jnp.float32) + send(theirs, (0, 1)).astype(jnp.float32)
+    sent = both.astype(blocks.dtype)
+    total = pick(both, high)
+    for d in range(1, head_count // 2):
+        total = total + send(pick(sent, high ^ d), (0, 2 * d)).astype(jnp.float32)
+    return total
+
+
+def all_sum(values):
+    total = values + send(values, (1, 0))
+    total = sum(chip_spread(total, lax.axis_index("dp") // 2))
+    return sum(head_spread(total, send(total, (0, 2))))
 def lamb_step(weight, grad, first, second, decay):
     mean = first_decay * first + (1.0 - first_decay) * grad
     square = second_decay * second + (1.0 - second_decay) * grad * grad
@@ -436,79 +541,108 @@
     head_count = lax.axis_size("head")
     dp_index = lax.axis_index("dp")
     head_index = lax.axis_index("head")
-    group = head_index % 2
+    chips = dp_count // 2
+    chip, core = dp_index // 2, dp_index % 2
+    side, near = head_index // 2, head_index % 2
+    member = 2 * near + core
+    here = core == side
     bf16 = jnp.bfloat16
     f32 = jnp.float32
     tok_rows, width = tokens.shape
+    half_width = width // 2
     local = entry_weights.shape[2]
     hidden = expand_weights.shape[2]
     shard = width // dp_count
-    row_count = tok_rows // head_count
-    patch_local = memory.shape[1]
-    patches = dp_count * patch_local
+    row_count = tok_rows // 4
+    image_count, patch_local = memory.shape[0:2]
     heads = local // HEAD_DIM
-    order = (0, 2, 1, 3)
+
+    def quarter(array):
+        return pick(array.reshape(4, row_count, *array.shape[1:]), member)
+
+    layout = jnp.stack([lengths, groups, image_map])
+    layout = jnp.where(here, layout, send(layout, (1, 0)))
+    stream_low = jnp.where(here, tokens, send(tokens, (1, 0)))
+    other_rows = pick(cotangent.reshape(4, row_count, width), member ^ 1)
+    cotangent_rows = jnp.where(here, quarter(cotangent), send(other_rows, (1, 0)))
 
     entry_low = entry_weights.astype(bf16).transpose(1, 0, 2)
     exit_low = exit_weights.astype(bf16).transpose(2, 0, 1)
     expand_low = expand_weights.astype(bf16).transpose(1, 0, 2)
     contract_low = contract_weights.astype(bf16).transpose(1, 0)[:, None]
-    gains_low = jnp.pad(norm_gains.astype(bf16).transpose(1, 0), ((0, 0), (0, LANES - 3)))
-    own_first = jnp.pad(entry_low[:, 0:3], ((0, 0), (0, 0), (0, 256 - local)))
-    own_first = jnp.concatenate([own_first.reshape(shard, 768), gains_low], axis=1)
-    first_set = jnp.concatenate([entry_low[:, 3:6], exit_low], axis=1)
-    first_set = lax.all_gather(first_set, "head", axis=0)
-    own_first = after(own_first, first_set)
-    self_full = lax.all_gather(own_first, "dp", axis=0, tiled=True)
-    self_weights = self_full[:, 0:768]
-    gain_values = self_full[:, 768 : 768 + 3].astype(f32).transpose(1, 0)
-
-    first_set = jnp.stack([first_set[h] for h in order], axis=2)
-    natural = first_set[:, 3][:, (0, 2, 1, 3)]
-    pair_set = first_set[:, 1:3].reshape(shard, 2, 2, 2 * local)
-    pair_set = jnp.where(group == 0, pair_set[:, :, 0], pair_set[:, :, 1])
-    first_set = jnp.concatenate(
+    gains_low = jnp.pad(norm_gains.astype(bf16).transpose(1, 0), ((0, 0), (0, HEAD_DIM - 3)))
+
+    def across(array):
+        pairs = [
+            (i * head_count + h, (i ^ 1) * head_count + (h ^ 2))
+            for i in range(dp_count)
+            for h in range(head_count)
+            if i % 2 != h // 2
+        ]
+        return jnp.where(here, array, lax.ppermute(array, ("dp", "head"), pairs))
+
+    moved = lax.all_to_all(
+        memory.reshape(dp_count, IMG_DEV * patch_local, width),
+        "dp",
+        split_axis=0,
+        concat_axis=0,
+        tiled=True,
+    )
+    patches = dp_count * patch_local
+    moved = moved.reshape(dp_count, IMG_DEV, patch_local, width).transpose(1, 0, 2, 3)
+    moved = moved.reshape(IMG_DEV, patches, width)
+    held = across(moved)
+    other = send(held, (1, 0))
+    memory_pair = jnp.concatenate([held, other], axis=1)
+    memory_pair = memory_pair.reshape(2 * IMG_DEV * patches, width)
+
+    own_set = entry_low[:, 0:3].reshape(shard, 3 * local)
+    rest_set = jnp.concatenate([exit_low[:, 0:1], entry_low[:, 3:6], exit_low[:, 1:2]], axis=1)
+    rest_set = rest_set.reshape(shard, 5 * local)
+    far_set = send(jnp.concatenate([own_set, rest_set], axis=1), (0, 2))
+    far_set = after(far_set, moved)
+    far_set, far_rest = far_set[:, 0 : 3 * local], far_set[:, 3 * local :]
+    mine = jnp.where(core == 0, own_set, far_set)
+    theirs = jnp.where(core == 0, far_set, own_set)
+    mine = jnp.concatenate([mine, gains_low], axis=1)
+    theirs = send(jnp.concatenate([theirs, gains_low], axis=1), (1, 0))
+
+    rest_set = jnp.stack(head_spread(rest_set, far_rest)).reshape(head_count, shard, 5, local)
+    rest_set = rest_set.transpose(1, 2, 0, 3).reshape(shard, 5 * width)
+    rest_full = lax.all_gather(rest_set, "dp", axis=0, tiled=True)
+    exit_self_t = rest_full[:, 0:width]
+    cross_query = rest_full[:, width : 2 * width]
+    cross_pair = jnp.concatenate(
         [
-            natural.reshape(shard, width),
-            first_set[:, 0].reshape(shard, width),
-            pair_set.reshape(shard, width),
-            first_set[:, 4].reshape(shard, width),
+            jnp.where(
+                core == 0,
+                rest_full[:, w * width : w * width + half_width],
+                rest_full[:, w * width + half_width : (w + 1) * width],
+            )
+            for w in (2, 3)
         ],
         axis=1,
     )
-    first_full = lax.all_gather(first_set, "dp", axis=0, tiled=True)
-    exit_self_t = first_full[:, 0:768]
-    cross_query = first_full[:, 768:1536]
-    cross_pair = first_full[:, 1536:2304]
-    exit_cross_t = first_full[:, 2304:3072]
-
-    images_here = memory.reshape(dp_count, IMG_DEV * patch_local, width)
-    images_here = after(images_here, self_full)
-    moved = lax.all_to_all(images_here, "dp", split_axis=0, concat_axis=0, tiled=True)
-    moved = (
-        moved.reshape(dp_count, IMG_DEV, patch_local, width)
-        .transpose(1, 0, 2, 3)
-        .reshape(IMG_DEV, patches, width)
-    )
-    near = [(s, s ^ 1) for s in range(head_count)]
-    other = lax.ppermute(moved, "head", near)
-    memory_pair = jnp.concatenate([moved, other], axis=1).reshape(2 * IMG_DEV * patches, width)
-
-    second_set = jnp.concatenate([expand_low, contract_low], axis=1)
-    second_set = head_spread(after(second_set, self_full))
-    second_set = second_set.transpose(1, 2, 0, 3).reshape(shard, 3 * head_count * hidden)
-    second_full = lax.all_gather(after(second_set, first_full), "dp", axis=0, tiled=True)
-    inner_width = head_count * hidden
-    gate_weights = second_full[:, 0:inner_width]
-    up_weights = second_full[:, inner_width : 2 * inner_width]
-    contract_t = second_full[:, 2 * inner_width :]
+    exit_cross_t = rest_full[:, 4 * width :]
+
+    self_set = jnp.concatenate(in_order([mine, theirs], core), axis=0)
+    self_full = [after(p, held) for p in chip_spread(self_set, chip)]
+    self_full = jnp.concatenate(self_full, axis=0)
+    gain_values = self_full[:, 3 * local : 3 * local + 3].astype(f32).transpose(1, 0)
+    self_weights = jnp.concatenate(
+        [
+            jnp.pad(self_full[:, s * local : (s + 1) * local], ((0, 0), (0, 256 - local)))
+            for s in range(3)
+        ],
+        axis=1,
+    )
 
     segments, images, weights = token_layout(
-        lengths.reshape(1, -1), groups.reshape(1, -1), image_map.reshape(1, -1), tok_rows, IMG_DEV
+        layout[0:1], layout[1:2], layout[2:3], tok_rows, IMG_DEV
     )
     image_tok = images[0]
     weight_tok = weights[0]
-    text_ends = jnp.cumsum(lengths)
+    text_ends = jnp.cumsum(layout[0])
     position = jnp.arange(tok_rows, dtype=jnp.int32)
     starts = jnp.max(
         jnp.where(position[None, :] >= text_ends[:, None], text_ends[:, None], 0), axis=0
@@ -521,40 +655,52 @@
     unsorter = (place[:, None] == position[None, :]).astype(bf16)
     split = split.reshape(1)
 
-    def own(array):
-        return lax.dynamic_slice_in_dim(array, head_index * row_count, row_count)
-
-    stream = tokens.astype(f32)
+    stream = stream_low.astype(f32)
     hidden_one = rms_norm(stream, gain_values[0]).astype(bf16)
     qkv = mm(hidden_one, self_weights).astype(bf16)
+    second_set = jnp.concatenate([expand_low, contract_low], axis=1)
+    far_second = send(after(second_set, held), (0, 2))
     self_out, self_sums = self_forward(qkv, starts)
-    self_rows = head_swap(self_out[:, 0:local].reshape(head_count, row_count, local))
-    self_rows = self_rows.transpose(1, 0, 2).reshape(row_count, width)
-    stream_rows = own(stream)
+    columns = jnp.where(core == 0, head_index, head_index ^ 2)
+
+    def by_member(array, d):
+        return pick(array.reshape(4, row_count, *array.shape[1:]), member ^ d)
+
+    self_block = self_out[:, 0:local]
+    pieces = member_pieces(lambda d: by_member(self_block, d))
+    far_second = after(far_second, self_block)
+    pieces = in_order([pieces[0], pieces[2], pieces[1], pieces[3]], columns)
+    self_rows = jnp.concatenate(pieces, axis=1)
+    stream_rows = quarter(stream)
     stream_one = stream_rows + mm(self_rows, exit_self_t, NT)
     hidden_two = rms_norm(stream_one, gain_values[1]).astype(bf16)
-
-    def to_groups(rows):
-        pieces = [rows[:, 0 : width // 2], rows[:, width // 2 :]]
-        return jnp.stack(pieces + pieces)
+    second_set = head_spread(second_set, far_second, stream_one)
+    second_set = jnp.stack(second_set, axis=2).reshape(shard, 3 * head_count * hidden)
+    second_full = lax.all_gather(second_set, "dp", axis=0, tiled=True)
+    inner_width = head_count * hidden
+    gate_weights = second_full[:, 0:inner_width]
+    up_weights = second_full[:, inner_width : 2 * inner_width]
+    contract_t = second_full[:, 2 * inner_width :]
+
+    def by_core(array, d):
+        flip = core == 1 - (d & 1)
+        return jnp.where(flip, array[:, half_width:], array[:, 0:half_width])
 
     query_rows = mm(hidden_two, cross_query).astype(bf16)
-    queries = head_swap(to_groups(query_rows)).reshape(tok_rows, width // 2)
-    queries = mm(sorter, queries).astype(bf16)
+    pieces = member_pieces(lambda d: by_core(query_rows, d))
+    queries = mm(sorter, jnp.concatenate(in_order(pieces, member), axis=0)).astype(bf16)
     pairs = mm(memory_pair, cross_pair).astype(bf16)
     cross_out, cross_sums = cross_forward(split, queries, pairs)
     cross_out = mm(unsorter, cross_out).astype(bf16)
     high, low = two_terms(cross_sums[:, 0:2].reshape(2 * heads, tok_rows))
     tail = jnp.concatenate([high, low, jnp.zeros((4, tok_rows), bf16)], axis=0)
     tail = mm(tail, sorter).astype(bf16)
-    tail = tail.reshape(16, head_count, row_count).transpose(1, 0, 2)
-    tail = jnp.pad(tail, ((0, 0), (0, 0), (0, width // 2 - row_count)))
-    sending = jnp.concatenate(
-        [cross_out.reshape(head_count, row_count, width // 2), tail], axis=1
-    )
-    got = head_swap(sending)
+    tail = tail.reshape(16, 4, row_count).transpose(1, 0, 2)
+    tail = jnp.pad(tail, ((0, 0), (0, 0), (0, half_width - row_count)))
+    blocks = jnp.concatenate([cross_out.reshape(4, row_count, half_width), tail], axis=1)
+    pieces = member_pieces(lambda d: pick(blocks, member ^ d))
     spread = (
-        jnp.arange(2 * heads)[:, None] == (jnp.arange(width // 2) // HEAD_DIM)[None, :]
+        jnp.arange(2 * heads)[:, None] == (jnp.arange(half_width) // HEAD_DIM)[None, :]
     ).astype(f32)
 
     def lanes_of(per_head):
@@ -564,8 +710,7 @@
 
     merged = []
     merged_sums = []
-    for g in range(2):
-        part = [got[g], got[g + 2]]
+    for part in ([pieces[0], pieces[2]], [pieces[1], pieces[3]]):
         sums = [
             p[row_count : row_count + 2 * heads, 0:row_count].astype(f32)
             + p[row_count + 2 * heads : row_count + 4 * heads, 0:row_count].astype(f32)
@@ -579,7 +724,7 @@
             + lanes_of(both[1] / total) * part[1][0:row_count].astype(f32)
         )
         merged_sums.append(largest + jnp.log(total))
-    cross_rows = jnp.concatenate(merged, axis=1).astype(bf16)
+    cross_rows = jnp.concatenate(in_order(merged, core), axis=1).astype(bf16)
     stream_two = stream_one + mm(cross_rows, exit_cross_t, NT)
     hidden_three = rms_norm(stream_two, gain_values[2]).astype(bf16)
 
@@ -588,24 +733,32 @@
     activated, pull_gate = jax.vjp(gated_hidden, gate, upward)
     activated_low = activated.astype(bf16)
     output_rows = stream_two + mm(activated_low, contract_t, NT)
-    grad_rows = own(cotangent).astype(f32) * own(weight_tok)[:, None]
+    grad_rows = cotangent_rows.astype(f32) * quarter(weight_tok)[:, None]
     grad_low = grad_rows.astype(bf16)
     grad_gate, grad_up = pull_gate(mm(grad_low, contract_t))
     grad_gate = grad_gate.astype(bf16)
     grad_up = grad_up.astype(bf16)
+    act_low = grad_low
     grad_normed = mm(grad_gate, gate_weights, NT) + mm(grad_up, up_weights, NT)
-    second_part = jnp.concatenate(
-        [
-            mm(hidden_three, grad_gate, TN).astype(bf16),
-            mm(hidden_three, grad_up, TN).astype(bf16),
-            mm(grad_low, activated_low, TN).astype(bf16),
-        ],
-        axis=1,
-    )
     grad_input, gain_three = rms_pull(stream_two, gain_values[2], grad_normed)
     grad_rows = grad_rows + grad_input
-
-    second_grads = lax.psum_scatter(second_part, "dp", scatter_dimension=0, tiled=True)
+    def rows_within(rows):
+        came = send(rows, (1, 0))
+        return jnp.concatenate(in_order([rows, came], core), axis=0)
+
+    def rows_across(rows):
+        pairs = [
+            (i * head_count + h, i * head_count + (h ^ 2))
+            for i in range(dp_count)
+            for h in range(head_count)
+            if i % 2 == h // 2
+        ]
+        return jnp.where(here, rows, lax.ppermute(rows, ("dp", "head"), pairs))
+
+    def rows_beside(rows):
+        return jnp.concatenate(in_order([rows, send(rows, (0, 1))], near), axis=0)
+
+    output = rows_across(rows_within(output_rows.astype(bf16)))
 
     grad_low = grad_rows.astype(bf16)
     exit_cross_part = mm(grad_low, cross_rows, TN).astype(bf16)
@@ -615,16 +768,20 @@
     for g in range(2):
         inner = lax.dot_general(
             spread,
-            product[:, g * (width // 2) : (g + 1) * (width // 2)],
+            by_core(product, g),
             NT,
             precision=lax.Precision.HIGHEST,
             preferred_element_type=f32,
         )
-        tails.append(jnp.concatenate([*two_terms(merged_sums[g]), *two_terms(inner)], axis=0))
-    tail = jnp.stack(tails + tails)
-    tail = jnp.pad(tail, ((0, 0), (0, 32 - 8 * heads), (0, width // 2 - row_count)))
-    got = head_swap(jnp.concatenate([to_groups(grad_cross), tail], axis=1))
-    grads = mm(sorter, got[:, 0:row_count].reshape(tok_rows, width // 2)).astype(bf16)
+        tail = jnp.concatenate([*two_terms(merged_sums[g]), *two_terms(inner)], axis=0)
+        tails.append(jnp.pad(tail, ((0, 32 - 8 * heads), (0, half_width - row_count))))
+    pieces = member_pieces(
+        lambda d: jnp.concatenate([by_core(grad_cross, d), tails[d & 1]], axis=0)
+    )
+    second_part = hidden_grads(after(hidden_three, grad_cross), after(act_low, grad_cross), grad_gate, grad_up, activated_low)
+    second_grads = lax.psum_scatter(second_part, "dp", scatter_dimension=0, tiled=True)
+    got = after(jnp.stack(in_order(pieces, member)), second_part)
+    grads = mm(sorter, got[:, 0:row_count].reshape(tok_rows, half_width)).astype(bf16)
     stats = (
         got[:, row_count : row_count + 8 * heads, 0:row_count]
         .transpose(1, 0, 2)
@@ -635,84 +792,137 @@
     inner = (stats[4 * heads : 6 * heads] + stats[6 * heads :]).reshape(heads, 2, tok_rows)
     stats = jnp.concatenate([sums, inner, jnp.zeros((heads, 4, tok_rows), f32)], axis=1)
     grad_query, grad_key, grad_value = cross_backward(split, queries, grads, stats, pairs)
-    grad_query = mm(unsorter, grad_query).astype(bf16)
-    got = head_swap(grad_query.reshape(head_count, row_count, width // 2)).astype(f32)
-    grad_query = jnp.concatenate([got[0] + got[2], got[1] + got[3]], axis=1).astype(bf16)
-    query_part = mm(hidden_two, grad_query, TN).astype(bf16)
-    grad_input, gain_two = rms_pull(
-        stream_one, gain_values[1], mm(grad_query, cross_query, NT)
-    )
+    grad_query = after(mm(unsorter, grad_query).astype(bf16), output)
+    output = rows_beside(output).astype(f32)
+    grad_pair = after(jnp.concatenate([grad_key, grad_value], axis=1), grad_query)
+    memory_part = mm(grad_pair, cross_pair, NT).reshape(IMG_DEV, 2, patches, width)
+    memory_came = send(memory_part[:, 1].astype(bf16), (1, 0))
+    pair_part = mm(memory_pair, grad_pair, TN).astype(bf16)
+    pieces = member_pieces(lambda d: by_member(grad_query, d))
+    pieces = [p.astype(f32) for p in pieces]
+    grad_query = jnp.concatenate(
+        in_order([pieces[0] + pieces[2], pieces[1] + pieces[3]], core), axis=1
+    ).astype(bf16)
+    grad_input, gain_two = rms_pull(stream_one, gain_values[1], mm(grad_query, cross_query, NT))
     grad_rows = grad_rows + grad_input
 
-    grad_pair = jnp.concatenate([grad_key, grad_value], axis=1)
-    pair_part = mm(memory_pair, grad_pair, TN).astype(bf16)
-    memory_part = mm(grad_pair, cross_pair, NT).reshape(IMG_DEV, 2, patches, width)
-    returned = lax.ppermute(memory_part[:, 1].astype(bf16), "head", near)
-    memory_sum = (memory_part[:, 0] + returned.astype(f32)).astype(bf16)
-    memory_sum = (
-        memory_sum.reshape(IMG_DEV, dp_count, patch_local, width)
-        .transpose(1, 0, 2, 3)
-        .reshape(dp_count, IMG_DEV * patch_local, width)
-    )
-    memory_grads = lax.all_to_all(memory_sum, "dp", split_axis=0, concat_axis=0, tiled=True)
-    memory_grads = memory_grads.reshape(memory.shape).astype(f32)
+    def core_halves(parts):
+        parts = parts.reshape(-1, chips, 2, shard, width)
+        kept = lax.dynamic_index_in_dim(parts, core, 2, keepdims=False)
+        return kept, send(lax.dynamic_index_in_dim(parts, 1 - core, 2, keepdims=False), (1, 0))
+
+    def chip_sum(parts):
+        pieces = chip_pieces(parts.transpose(1, 0, 2, 3), chip)
+        return sum(p.astype(f32) for p in pieces)
+
+    query_part = mm(after(hidden_two, grad_rows), grad_query, TN).astype(bf16)
+    kept, came = core_halves(jnp.stack([query_part, exit_cross_part]))
+    pair_kept, pair_came = core_halves(pair_part)
+    cross_sums = (kept.astype(f32) + came.astype(f32)).astype(bf16)
+    cross_chips = jnp.concatenate([cross_sums, *in_order([pair_kept, pair_came], core)], axis=0)
 
     grad_low = grad_rows.astype(bf16)
-    exit_self_part = mm(grad_low, self_rows, TN).astype(bf16)
     grad_self = mm(grad_low, exit_self_t).astype(bf16)
-    grad_self = after(grad_self, second_grads)
-    grad_self = head_swap(grad_self.reshape(row_count, head_count, local).transpose(1, 0, 2))
-    grad_self = jnp.pad(grad_self.reshape(tok_rows, local), ((0, 0), (0, 256 - local)))
+    grad_self = after(grad_self, output)
+    by_columns = jnp.stack([grad_self[:, s * local : (s + 1) * local] for s in range(4)])
+    pieces = member_pieces(lambda d: pick(by_columns, columns ^ (2 * (d & 1) + (d >> 1))))
+    grad_self = jnp.pad(
+        jnp.concatenate(in_order(pieces, member), axis=0), ((0, 0), (0, 256 - local))
+    )
     grad_qkv = self_backward(qkv, grad_self, self_out, self_sums, starts)
-    self_part = mm(hidden_one, grad_qkv, TN)
     grad_normed = mm(grad_qkv, self_weights, NT)
     inverse = lax.rsqrt(jnp.mean(stream * stream, axis=-1, keepdims=True) + norm_eps)
     gain_one = jnp.sum(grad_normed * stream * inverse, axis=0)
-    grad_normed = head_swap(
-        grad_normed.astype(bf16).reshape(head_count, row_count, width)
-    ).astype(f32)
-    grad_normed = jnp.sum(grad_normed, axis=0)
+    by_near = grad_normed.reshape(2, 2, row_count, width)
+    kept = lax.dynamic_index_in_dim(by_near, core, 1, keepdims=False)
+    came = lax.dynamic_index_in_dim(by_near, 1 - core, 1, keepdims=False).astype(bf16)
+    self_core = mm(after(hidden_one, came), grad_qkv, TN).astype(bf16)
+    kept = after(kept, self_core) + send(came, (1, 0)).astype(f32)
+    came = send(pick(kept, 1 - near).astype(bf16), (0, 1))
+    cross_chips = after(cross_chips, kept)
+    cross_sums = chip_sum(cross_chips)
+    memory_sum = after(memory_part[:, 0], cross_chips) + memory_came.astype(f32)
+    memory_sum = memory_sum.astype(bf16)
+    second_grads = after(second_grads, memory_sum)
+    second_grads = jnp.concatenate(
+        [second_grads[:, h * 3 * hidden : (h + 1) * 3 * hidden] for h in range(head_count)], axis=0
+    )
+    came = after(came, second_grads)
+    memory_sum = across(memory_sum)
+    second_grads = lax.psum_scatter(second_grads, "head", scatter_dimension=0, tiled=True)
+    second_grads = second_grads.astype(f32)
+    grad_normed = pick(kept, near) + came.astype(f32)
     grad_input, _ = rms_pull(stream_rows, gain_values[0], grad_normed)
-    grad_rows = grad_rows + grad_input
-    token_grads = head_spread(grad_rows.astype(bf16)).reshape(tok_rows, width).astype(f32)
-    output = head_spread(output_rows.astype(bf16)).reshape(tok_rows, width).astype(f32)
-
-    second_grads = second_grads.reshape(shard, 3, head_count, hidden).transpose(2, 0, 1, 3)
-    second_grads = jnp.sum(head_swap(second_grads).astype(f32), axis=0)
-    expand_grads = second_grads[:, 0:2].transpose(1, 0, 2)
-    contract_grads = second_grads[:, 2].transpose(1, 0)
-
-    first_part = jnp.concatenate([exit_self_part, query_part, pair_part, exit_cross_part], axis=1)
-    first_grads = lax.psum_scatter(first_part, "dp", scatter_dimension=0, tiled=True)
-    sets = first_grads.reshape(shard, 4, head_count, local)
-    blocks = []
-    for h in range(head_count):
-        slot = order.index(h)
-        mine = sets[:, 2].reshape(shard, 2, 2, local)[:, :, slot % 2]
-        mine = jnp.where(group == h % 2, mine, jnp.zeros_like(mine))
-        blocks.append(
-            jnp.concatenate(
-                [sets[:, 1, slot][:, None], mine, sets[:, 0, h][:, None], sets[:, 3, slot][:, None]],
-                axis=1,
+    token_grads = (grad_rows + grad_input).astype(bf16)
+
+    exit_self_part = mm(after(grad_low, token_grads), self_rows, TN).astype(bf16)
+    kept, came = core_halves(exit_self_part)
+    gain_part = jnp.stack([gain_one, gain_two, gain_three], axis=1).astype(bf16)
+    gain_part = jnp.pad(gain_part, ((0, 0), (0, width - 3 * local - 3)))
+    self_part = jnp.concatenate(
+        [self_core[:, 256 * s : 256 * s + local] for s in range(3)] + [after(gain_part, token_grads)],
+        axis=1,
+    )
+    self_part = self_part.reshape(chips, 2, shard, width)
+    mine = lax.dynamic_index_in_dim(self_part, core, 1, keepdims=False)
+    theirs = send(lax.dynamic_index_in_dim(self_part, 1 - core, 1, keepdims=False), (1, 0))
+    token_grads = rows_within(token_grads)
+    cross_sums = after(cross_sums, token_grads)
+    token_grads = rows_across(token_grads)
+    self_sums = jnp.stack(in_order([mine, theirs], core))
+    self_sums = jnp.concatenate(
+        [(kept.astype(f32) + came.astype(f32)).astype(bf16), self_sums], axis=0
+    )
+    self_sums = after(self_sums, cross_sums)
+    token_grads = after(token_grads, self_sums, second_grads)
+    self_sums = chip_sum(self_sums)
+
+    sums = jnp.concatenate([self_sums[0:1], cross_sums, self_sums[1:3]], axis=0)
+    sums = after(sums, token_grads, memory_sum)
+    memory_grads = memory_sum.reshape(IMG_DEV, dp_count, patch_local, width).transpose(1, 0, 2, 3)
+    memory_grads = lax.all_to_all(
+        memory_grads.reshape(dp_count, IMG_DEV * patch_local, width),
+        "dp",
+        split_axis=0,
+        concat_axis=0,
+        tiled=True,
+    )
+    memory_grads = memory_grads.reshape(memory.shape).astype(f32)
+    token_grads = rows_beside(token_grads).astype(f32)
+
+    by_head = jnp.stack(
+        [
+            jnp.stack(
+                [sums[w, :, h * local : (h + 1) * local] for w in range(3)]
+                + [
+                    sums[
+                        3 + h // 2,
+                        :,
+                        w * half_width + (h % 2) * local : w * half_width + (h % 2 + 1) * local,
+                    ]
+                    for w in range(2)
+                ]
+                + [sums[5, :, 3 * local :] + sums[6, :, 3 * local :]]
             )
-        )
-    first_grads = jnp.sum(head_swap(jnp.stack(blocks)).astype(f32), axis=0)
-    exit_grads = first_grads[:, 3:5].transpose(1, 2, 0)
-
-    gain_part = jnp.stack([gain_one, gain_two, gain_three])
-    self_part = self_part.reshape(width, 3, 256)[:, :, 0:local].reshape(width, 3 * local)
-    high, low = two_terms(gain_part.transpose(1, 0))
-    self_part = jnp.concatenate([self_part.astype(bf16), high, low], axis=1)
-    self_part = jnp.pad(self_part, ((0, 0), (0, 58)))
-    self_grads = lax.all_to_all(
-        self_part.reshape(dp_count, shard, -1), "dp", split_axis=0, concat_axis=0, tiled=True
-    )
-    self_grads = jnp.sum(self_grads.astype(f32), axis=0)
-    gain_grads = self_grads[:, 3 * local : 3 * local + 3] + self_grads[:, 3 * local + 3 : 3 * local + 6]
-    gain_grads = lax.psum(gain_grads, "head").transpose(1, 0)
-    entry_grads = jnp.concatenate(
-        [self_grads[:, 0 : 3 * local].reshape(shard, 3, local), first_grads[:, 0:3]], axis=1
-    ).transpose(1, 0, 2)
+            for h in range(head_count)
+        ]
+    )
+    by_head = by_head.reshape(2, 2, 6, shard, local)
+    kept = lax.dynamic_index_in_dim(by_head, near, 1, keepdims=False)
+    came = lax.dynamic_index_in_dim(by_head, 1 - near, 1, keepdims=False)
+    kept = kept + send(came.astype(bf16), (0, 1)).astype(f32)
+    own_three, far_three = [
+        jnp.stack([sums[5 + w, :, s * local : (s + 1) * local] for s in range(3)]) for w in range(2)
+    ]
+    far_eight = jnp.concatenate([pick(kept, 1 - side), far_three], axis=0)
+    own_eight = jnp.concatenate([pick(kept, side), own_three], axis=0)
+    first_grads = own_eight + send(far_eight.astype(bf16), (0, 2)).astype(f32)
+    exit_grads = jnp.stack([first_grads[0].T, first_grads[2].T])
+    expand_grads = jnp.stack([second_grads[:, 0:hidden], second_grads[:, hidden : 2 * hidden]])
+    contract_grads = second_grads[:, 2 * hidden :].T
+
+    gain_grads = first_grads[5, :, 0:3].T
+    entry_grads = jnp.stack([first_grads[w] for w in (6, 7, 8, 1, 3, 4)])
 
     entry_mean, entry_square, entry_step = lamb_step(
         entry_weights, entry_grads, entry_first, entry_second, weight_decay
@@ -747,7 +957,7 @@
             jnp.sum(gains_step * gains_step, axis=1) / head_count,
         ]
     )
-    weight_squares, step_squares = lax.psum(lax.psum(jnp.stack([weight_local, step_local]), "dp"), "head")
+    weight_squares, step_squares = all_sum(after(jnp.stack([weight_local, step_local]), token_grads))
     weight_norm = jnp.sqrt(weight_squares)
     step_norm = jnp.sqrt(step_squares)
     ratio = learn_rate * weight_norm / (step_norm + adam_eps)

time: 664 us -> 556 us (0.84)
  blocking collectives: 107 us -> 0 us
  between operations: 15.8 us -> 45.2 us
  local copies, waits for them, and re-layouts: 74.4 us -> 52.5 us
  starting transfers between devices: 89 us -> 68.2 us
  matrix products: 68.2 us -> 56.3 us
  other arithmetic: 69.7 us -> 79.2 us
  Pallas kernels: 65.6 us -> 75 us
    ppermute x2 -> x59, waiting for transfers between devices: 52.5 us -> 152 us  [the longest x17 93.9 us: send(): lax.ppermute(array, 'head', [(s, s ^ head_bits) for s in range(head_count)])]
    all_to_all x14 -> x2, waiting for transfers between devices: 105 us -> 17.6 us  [the longest x1 17.6 us: per_device(): lax.all_to_all(memory.reshape(dp_count, IMG_DEV * patch_local, width), 'd...]
    all_to_all x14 -> x2, starting transfers between devices: 85.5 us -> 8.45 us  [the longest x1 4.4 us: per_device(): lax.all_to_all(memory.reshape(dp_count, IMG_DEV * patch_local, width), 'd...]
    ppermute x2 -> x59, starting transfers between devices: 2.93 us -> 59.6 us  [the longest x17 24.4 us: send(): lax.ppermute(array, 'head', [(s, s ^ head_bits) for s in range(head_count)])]
    psum x3 -> x0, blocking collectives: 55.6 us -> none  [the longest x1 25.4 us: per_device(): lax.psum(lax.psum(jnp.stack([weight_local, step_local]), 'dp'), 'head')]
    unnamed x132 -> x175, local copies, waits for them, and re-layouts: 41.8 us -> 5.2 us
    all_to_all x1 -> x0, blocking collectives: 31.2 us -> none  [head_swap(): lax.all_to_all(blocks, 'head', split_axis=0, concat_axis=0, tiled=True)]
    select_n x5 -> x35, other arithmetic: 1.13 us -> 25.1 us  [the longest x13 8.57 us: after(): return jnp.where(mark == mark, array, jnp.asarray(jnp.nan, array.dtype))]
  transfers between devices with their start and end apart: 21 -> 65, of which waited for: 13 -> 25; matrix products, arithmetic and copies ran while one was open for 26% -> 28% of each run, Pallas kernels for 10% -> 14%
where the time goes in v2:
time: 556 us; the launch traced here: 546 us
  waiting for transfers between devices  170 us (31%)
  other arithmetic  79.2 us (14%)
  Pallas kernels  75 us (13%)
  starting transfers between devices  68.2 us (12%)
  matrix products  56.3 us (10%)
  local copies, waits for them, and re-layouts  52.5 us (9%)
  between operations  45.2 us (8%)
    ppermute x17, waiting for transfers between devices, send(): lax.ppermute(array, 'head', [(s, s ^ head_bits) for s in range(head_count)])  93.9 us
    dot_general x27, matrix products, mm(): return lax.dot_general(a, b, dims, preferred_element_type=jnp.float32)  53.9 us
    pallas_call x1, Pallas kernels, cross_backward(): pl.pallas_call(cross_backward_kernel, grid=(groups,), in_specs=[pl.BlockS...  26.6 us
    ppermute x2, waiting for transfers between devices, across(): return jnp.where(here, array, lax.ppermute(array, ('dp', 'head'), pairs))  26.1 us
    pallas_call x1, Pallas kernels, cross_forward(): pl.pallas_call(cross_forward_kernel, grid=(groups,), in_specs=[pl.BlockSp...  26 us
    ppermute x17, starting transfers between devices, send(): lax.ppermute(array, 'head', [(s, s ^ head_bits) for s in range(head_count)])  24.4 us
    ppermute x32, starting transfers between devices, send(): lax.ppermute(array, 'dp', [(s, s ^ dp_bits) for s in range(dp_count)])  21.8 us
    ppermute x32, waiting for transfers between devices, send(): lax.ppermute(array, 'dp', [(s, s ^ dp_bits) for s in range(dp_count)])  21.3 us
  transfers between devices with their start and end apart: 65, of which 25 were waited for; matrix products, arithmetic and copies ran while one was open for 28% of the time, Pallas kernels for 14%

profile of v2, /device:TPU:18, one launch (start us, length us, event | category | flops | bytes accessed | tf_op | source)
XLA Modules:
  0.0 546.1 jit_solution(9734468649613647522)
XLA Ops:
  7.2 4.4 all-to-all-start
  13.6 17.6 %all-to-all-done = bf16[8,128,768]{2,1,0:T(8,128)(2,1)S(1)} async-done(((bf16[8,128,768]{2,1,0:T(8,128)(2,1)}), bf16[8,128,768]{2,1,0:T(8,128)(2,1)S(1)}, u32[]{:S(2)}, u32[]{:S(2)}) %all-to-all-start) | async-done | bytes 1572896 | tf_op jit(solution)/shard_map/all_to_all | solution.py:584
  34.4 2.4 collective-permute-start.11
  36.8 11.4 %collective-permute-done.11 = bf16[2,96,960]{1,2,0:T(8,128)(2,1)S(1)} collective-permute-done((bf16[2,96,960]{1,2,0:T(8,128)(2,1)S(1)}, bf16[2,96,960]{1,2,0:T(8,128)(2,1)S(1)}, u32[]{:S(2)}, u32[]{:S(2)}) %collective-permute-start.11) | collective-permute-done | bytes 368672 | tf_op jit(solution)/shard_map/ppermute | solution.py:443
  61.8 2.2 multiply_reduce_fusion.1
  64.1 26.1 %collective-permute-done.1 = bf16[2,512,768]{2,1,0:T(8,128)(2,1)} collective-permute-done((bf16[2,512,768]{2,1,0:T(8,128)(2,1)S(1)}, bf16[2,512,768]{2,1,0:T(8,128)(2,1)}, u32[]{:S(2)}, u32[]{:S(2)}) %collective-permute-start.1) | collective-permute-done | bytes 1572896 | tf_op jit(solution)/shard_map/ppermute | solution.py:582
  97.2 5.8 %self_forward.1 = (bf16[1024,256]{1,0:T(8,128)(2,1)S(1)}, f32[8,1024]{1,0:T(8,128)S(1)}) custom-call(bf16[1024,768]{1,0:T(8,128)(2,1)S(1)} %convolution_convert_fusion.1.qkv_ref, s32[1,1024]{1,0:T(1,128)S(1)} %bitcast.393), custom_call_target="tpu_custom_call" | custom-call | flops 6000000000 | bytes 2097152 | tf_op jit(solution)/shard_map/self_forward/pallas_call | solution.py:104
  104.9 4.0 collective-permute-start.10
  113.3 2.4 collective-permute-done.8
  116.5 2.3 multiply_reduce_fusion.8
  120.7 7.8 %collective-permute-done.20 = bf16[2,96,3,512]{3,1,2,0:T(8,128)(2,1)} collective-permute-done((bf16[2,96,3,512]{3,1,2,0:T(8,128)(2,1)S(1)}, bf16[2,96,3,512]{3,1,2,0:T(8,128)(2,1)}, u32[]{:S(2)}, u32[]{:S(2)}) %collective-permute-start.20) | collective-permute-done | bytes 589856 | tf_op jit(solution)/shard_map/ppermute | solution.py:443
  142.2 2.8 convolution_convert_fusion.7
  149.1 4.0 convolution_convert_fusion.key_ref.value_ref
  153.1 3.5 collective-permute-done.13
  158.0 26.0 %cross_forward.1 = (bf16[1024,384]{1,0:T(8,128)(2,1)S(1)}, f32[3,8,1024]{2,1,0:T(8,128)S(1)}) custom-call(s32[1]{0:T(128)} %slice.510.split_ref, bf16[1024,384]{1,0:T(8,128)(2,1)S(1)} %fusion.53.query_ref, bf16[2048,768]{1,0:T(8,128)(2,1)} %convolution_convert_fusion.key_ref.value_ref, bf16[2048,768]{1,0:T(8,128)(2,1)} %convolution_convert_fusion.key_ref.value_ref), custom_call_target="tpu_custom_call" | custom-call | flops 28000000000 | bytes 3145728 | tf_op jit(solution)/shard_map/cross_forward/pallas_call | solution.py:247
  188.6 4.8 collective-permute-done.17
  193.9 4.6 collective-permute-done.18
  202.1 3.1 fusion.16
  205.2 3.5 fusion.20
  208.7 2.9 fusion.29
  221.4 8.9 %hidden_grads.1 = bf16[768,6144]{1,0:T(8,128)(2,1)} custom-call(bf16[256,768]{1,0:T(8,128)(2,1)S(1)} %broadcast_select_fusion.16.rows_ref, bf16[256,768]{1,0:T(8,128)(2,1)S(1)} %broadcast_select_fusion.15.grad_ref, bf16[256,2048]{1,0:T(8,128)(2,1)S(1)} %get-tuple-element.235.gate_ref, bf16[256,2048]{1,0:T(8,128)(2,1)S(1)} %get-tuple-element.236.up_ref, ...), custom_call_target="tpu_custom_call" | custom-call | flops 2415919104 | bytes 9437184 | tf_op jit(solution)/shard_map/hidden_grads/pallas_call | solution.py:397
  230.4 3.9 fusion.61
  238.5 4.9 collective-permute-done.26
  250.1 26.6 %cross_backward.1 = (bf16[1024,384]{1,0:T(8,128)(2,1)S(1)}, bf16[2048,384]{1,0:T(8,128)(2,1)S(1)}, bf16[2048,384]{1,0:T(8,128)(2,1)}) custom-call(s32[1]{0:T(128)} %slice.510.split_ref, bf16[1024,384]{1,0:T(8,128)(2,1)S(1)} %fusion.53.query_ref, bf16[1024,384]{1,0:T(8,128)(2,1)S(1)} %fusion.54.grad_ref, f32[3,8,1024]{2,1,0:T(8,128)S(1)} %maximum_maximum_fusion.stats_ref, ...), custom_call_target="tpu_custom_call" | custom-call | flops 28000000000 | bytes 6291456 | tf_op jit(solution)/shard_map/cross_backward/pallas_call | solution.py:339
  286.1 2.7 fusion.47
  289.4 2.7 fusion.37
  293.5 6.9 %collective-permute-done.30 = bf16[256,384]{1,0:T(8,128)(2,1)S(1)} collective-permute-done((bf16[256,384]{1,0:T(8,128)(2,1)S(1)}, bf16[256,384]{1,0:T(8,128)(2,1)S(1)}, u32[]{:S(2)}, u32[]{:S(2)}) %collective-permute-start.30) | collective-permute-done | bytes 196640 | tf_op jit(solution)/shard_map/ppermute | solution.py:443
  300.4 3.6 collective-permute-start.37
  304.0 2.3 collective-permute-done.29
  319.8 3.8 collective-permute-done.32
  324.9 7.6 %self_backward.1 = bf16[1024,768]{1,0:T(8,128)(2,1)S(1)} custom-call(bf16[1024,768]{1,0:T(8,128)(2,1)} %copy-done, bf16[1024,256]{1,0:T(8,128)(2,1)S(1)} %fusion.121.grad_ref, bf16[1024,256]{1,0:T(8,128)(2,1)S(1)} %get-tuple-element.35.out_ref, f32[8,1024]{1,0:T(8,128)S(1)} %get-tuple-element.39.sums_ref, s32[1,1024]{1,0:T(1,128)S(1)} %bitcast.394), custom_call_target="tpu_custom_call" | custom-call | flops 8000000000 | bytes 5242880 | tf_op jit(solution)/shard_map/self_backward/pallas_call | solution.py:176
  332.5 2.5 multiply_reduce_fusion
  348.0 3.0 fusion.9
  352.2 2.7 collective-permute-start.47
  365.8 16.9 %collective-permute-done.38 = bf16[256,768]{1,0:T(8,128)(2,1)} collective-permute-done((bf16[256,768]{1,0:T(8,128)(2,1)}, bf16[256,768]{1,0:T(8,128)(2,1)}, u32[]{:S(2)}, u32[]{:S(2)}) %collective-permute-start.38) | collective-permute-done | bytes 393248 | tf_op jit(solution)/shard_map/ppermute | solution.py:443
  389.8 2.6 convolution_convert_fusion.2
  415.4 4.1 all-to-all-start.1
  420.6 8.7 %collective-permute-done.50 = bf16[3,96,768]{2,1,0:T(8,128)(2,1)} collective-permute-done((bf16[3,96,768]{2,1,0:T(8,128)(2,1)}, bf16[3,96,768]{2,1,0:T(8,128)(2,1)}, u32[]{:S(2)}, u32[]{:S(2)}) %collective-permute-start.50) | collective-permute-done | bytes 442400 | tf_op jit(solution)/shard_map/ppermute | solution.py:441
  429.3 6.8 %collective-permute-done.49 = bf16[3,96,768]{2,1,0:T(8,128)(2,1)} collective-permute-done((bf16[3,96,768]{2,1,0:T(8,128)(2,1)}, bf16[3,96,768]{2,1,0:T(8,128)(2,1)}, u32[]{:S(2)}, u32[]{:S(2)}) %collective-permute-start.49) | collective-permute-done | bytes 442400 | tf_op jit(solution)/shard_map/ppermute | solution.py:441
  440.9 2.5 select_select_fusion
  459.0 2.9 multiply_reduce_fusion.12
  461.9 14.9 %collective-permute-done.51 = bf16[2,6,96,192]{2,3,1,0:T(8,128)(2,1)S(1)} collective-permute-done((bf16[2,6,96,192]{2,3,1,0:T(8,128)(2,1)}, bf16[2,6,96,192]{2,3,1,0:T(8,128)(2,1)S(1)}, u32[]{:S(2)}, u32[]{:S(2)}) %collective-permute-start.51) | collective-permute-done | bytes 442400 | tf_op jit(solution)/shard_map/ppermute | solution.py:443
  478.7 17.6 %collective-permute-done.52 = bf16[9,96,192]{1,2,0:T(8,128)(2,1)S(1)} collective-permute-done((bf16[9,96,192]{1,2,0:T(8,128)(2,1)S(1)}, bf16[9,96,192]{1,2,0:T(8,128)(2,1)S(1)}, u32[]{:S(2)}, u32[]{:S(2)}) %collective-permute-start.52) | collective-permute-done | bytes 331808 | tf_op jit(solution)/shard_map/ppermute | solution.py:443
  501.0 2.6 multiply_reduce_fusion.16
  503.7 3.2 multiply_reduce_fusion.10
  518.3 2.9 collective-permute-done.54
  521.3 3.4 collective-permute-start.57
  526.8 3.1 collective-permute-start.58
  (542 shorter events, 184.9 us)
Async XLA Ops:
  7.2 23.9 %all-to-all-start = ((bf16[8,128,768]{2,1,0:T(8,128)(2,1)}), bf16[8,128,768]{2,1,0:T(8,128)(2,1)S(1)}, u32[]{:S(2)}, u32[]{:S(2)}) async-start(bf16[8,128,768]{2,1,0:T(8,128)(2,1)} %bitcast.416), calls=%async_computation | async-start | bytes 3145728 | tf_op jit(solution)/shard_map/all_to_all | solution.py:584
  11.6 104.8 %all-gather.3.cloned.1.call-start = ((), (), s32[]{:S(2)}) async-start(), calls=%async_computation.4 | async-start | bytes 6635520 | tf_op jit(solution)/shard_map/all_gather | solution.py:612
  13.2 19.9 %collective-permute-start.2 = (bf16[96,1536]{0,1:T(8,128)(2,1)}, bf16[96,1536]{0,1:T(8,128)(2,1)}, u32[]{:S(2)}, u32[]{:S(2)}) collective-permute-start(bf16[96,1536]{0,1:T(8,128)(2,1)} %pad_maximum_fusion.24), channel_id=1, source_target_pairs={{0,2},{1,3},{2,0},{3,1},{4,6},{5,7},{6,4},{7,5},{8,10},{9,11},{10,... | collective-permute-start | bytes 884744 | tf_op jit(solution)/shard_map/ppermute | solution.py:443
  34.4 13.8 %collective-permute-start.11 = (bf16[2,96,960]{1,2,0:T(8,128)(2,1)S(1)}, bf16[2,96,960]{1,2,0:T(8,128)(2,1)S(1)}, u32[]{:S(2)}, u32[]{:S(2)}) collective-permute-start(bf16[2,96,960]{1,2,0:T(8,128)(2,1)S(1)} %pad_maximum_fusion.20), channel_id=1, source_target_pairs={{0,1},{1,0},{2,3},{3,2},{4,5},{5,4},{6,7},{7,6},{8,9},{9,8},{10,11... | collective-permute-start | bytes 1105928 | tf_op jit(solution)/shard_map/ppermute | solution.py:443
  52.1 150.0 %all-gather.5.cloned.1.call-start = ((), (), s32[]{:S(2)}) async-start(), calls=%async_computation.5 | async-start | bytes 10616832 | tf_op jit(solution)/shard_map/all_gather | solution.py:679
  52.2 9.6 %collective-permute-start = (bf16[1024,768]{1,0:T(8,128)(2,1)}, bf16[1024,768]{1,0:T(8,128)(2,1)}, u32[]{:S(2)}, u32[]{:S(2)}) collective-permute-start(bf16[1024,768]{1,0:T(8,128)(2,1)} %param.22), channel_id=1, source_target_pairs={{0,4},{4,0},{8,12},{12,8},{16,20},{20,16},{24,28},{28,24},{1,5},{5... | collective-permute-start | bytes 4718600 | tf_op jit(solution)/shard_map/ppermute | solution.py:441
  53.5 36.7 %collective-permute-start.1 = (bf16[2,512,768]{2,1,0:T(8,128)(2,1)S(1)}, bf16[2,512,768]{2,1,0:T(8,128)(2,1)}, u32[]{:S(2)}, u32[]{:S(2)}) collective-permute-start(bf16[2,512,768]{2,1,0:T(8,128)(2,1)S(1)} %bitcast.400), channel_id=1, source_target_pairs={{2,4},{3,5},{4,2},{5,3},{10,12},{11,13},{12,10},{13,11},{18,20},{1... | collective-permute-start | bytes 4718600 | tf_op jit(solution)/shard_map/ppermute | solution.py:582
  58.3 35.8 %collective-permute-start.6 = (bf16[192,640]{0,1:T(8,128)(2,1)S(1)}, bf16[192,640]{0,1:T(8,128)(2,1)S(1)}, u32[]{:S(2)}, u32[]{:S(2)}) collective-permute-start(bf16[192,640]{0,1:T(8,128)(2,1)S(1)} %pad_maximum_fusion.29), channel_id=1, source_target_pairs={{0,8},{4,12},{8,0},{12,4},{16,24},{20,28},{24,16},{28,20},{1,9},{5... | collective-permute-start | bytes 737288 | tf_op jit(solution)/shard_map/ppermute | solution.py:441
  58.7 35.4 %collective-permute-start.5 = (bf16[192,640]{0,1:T(8,128)(2,1)S(1)}, bf16[192,640]{0,1:T(8,128)(2,1)S(1)}, u32[]{:S(2)}, u32[]{:S(2)}) collective-permute-start(bf16[192,640]{0,1:T(8,128)(2,1)S(1)} %pad_maximum_fusion.29), channel_id=1, source_target_pairs={{0,16},{4,20},{8,24},{12,28},{16,0},{20,4},{24,8},{28,12},{1,17},{... | collective-permute-start | bytes 737288 | tf_op jit(solution)/shard_map/ppermute | solution.py:441
  60.4 33.8 %collective-permute-start.4 = (bf16[192,640]{0,1:T(8,128)(2,1)S(1)}, bf16[192,640]{0,1:T(8,128)(2,1)S(1)}, u32[]{:S(2)}, u32[]{:S(2)}) collective-permute-start(bf16[192,640]{0,1:T(8,128)(2,1)S(1)} %pad_maximum_fusion.29), channel_id=1, source_target_pairs={{0,24},{4,28},{8,16},{12,20},{16,8},{20,12},{24,0},{28,4},{1,25},{... | collective-permute-start | bytes 737288 | tf_op jit(solution)/shard_map/ppermute | solution.py:441
  94.0 15.1 %collective-permute-start.19 = (bf16[96,3,512]{2,0,1:T(8,128)(2,1)S(1)}, bf16[96,3,512]{2,0,1:T(8,128)(2,1)S(1)}, u32[]{:S(2)}, u32[]{:S(2)}) collective-permute-start(bf16[96,3,512]{2,0,1:T(8,128)(2,1)S(1)} %broadcast_select_fusion.26), channel_id=1, source_target_pairs={{0,2},{1,3},{2,0},{3,1},{4,6},{5,7},{6,4},{7,5},{8,10},{9,11},{10,... | collective-permute-start | bytes 884744 | tf_op jit(solution)/shard_map/ppermute | solution.py:443
  104.9 8.4 %collective-permute-start.10 = (bf16[256,192]{1,0:T(8,128)(2,1)S(1)}, bf16[256,192]{1,0:T(8,128)(2,1)S(1)}, u32[]{:S(2)}, u32[]{:S(2)}) collective-permute-start(bf16[256,192]{1,0:T(8,128)(2,1)S(1)} %get-tuple-element.333), channel_id=1, source_target_pairs={{0,1},{1,0},{2,3},{3,2},{4,5},{5,4},{6,7},{7,6},{8,9},{9,8},{10,11... | collective-permute-start | bytes 294920 | tf_op jit(solution)/shard_map/ppermute | solution.py:443
  109.2 19.2 %collective-permute-start.20 = (bf16[2,96,3,512]{3,1,2,0:T(8,128)(2,1)S(1)}, bf16[2,96,3,512]{3,1,2,0:T(8,128)(2,1)}, u32[]{:S(2)}, u32[]{:S(2)}) collective-permute-start(bf16[2,96,3,512]{3,1,2,0:T(8,128)(2,1)S(1)} %pad_maximum_fusion.17), channel_id=1, source_target_pairs={{0,1},{1,0},{2,3},{3,2},{4,5},{5,4},{6,7},{7,6},{8,9},{9,8},{10,11... | collective-permute-start | bytes 1769480 | tf_op jit(solution)/shard_map/ppermute | solution.py:443
  133.0 229.4 %reduce-scatter.3.cloned.1.call-start = ((), (), s32[]{:S(2)}) async-start(), calls=%async_computation.6 | async-start | bytes 10616832 | tf_op jit(solution)/shard_map/reduce_scatter | solution.py:782
  145.1 8.0 %collective-permute-start.14 = (bf16[256,384]{1,0:T(8,128)(2,1)S(1)}, bf16[256,384]{1,0:T(8,128)(2,1)S(1)}, u32[]{:S(2)}, u32[]{:S(2)}) collective-permute-start(bf16[256,384]{1,0:T(8,128)(2,1)S(1)} %get-tuple-element.348), channel_id=1, source_target_pairs={{0,4},{4,0},{8,12},{12,8},{16,20},{20,16},{24,28},{28,24},{1,5},{5... | collective-permute-start | bytes 589832 | tf_op jit(solution)/shard_map/ppermute | solution.py:441
  145.2 7.9 %collective-permute-start.12 = (bf16[256,384]{1,0:T(8,128)(2,1)S(1)}, bf16[256,384]{1,0:T(8,128)(2,1)S(1)}, u32[]{:S(2)}, u32[]{:S(2)}) collective-permute-start(bf16[256,384]{1,0:T(8,128)(2,1)S(1)} %get-tuple-element.348), channel_id=1, source_target_pairs={{0,5},{1,4},{2,7},{3,6},{4,1},{5,0},{6,3},{7,2},{8,13},{9,12},{10,... | collective-permute-start | bytes 589832 | tf_op jit(solution)/shard_map/ppermute | solution.py:449
  146.2 10.4 %collective-permute-start.13 = (bf16[256,384]{1,0:T(8,128)(2,1)S(1)}, bf16[256,384]{1,0:T(8,128)(2,1)S(1)}, u32[]{:S(2)}, u32[]{:S(2)}) collective-permute-start(bf16[256,384]{1,0:T(8,128)(2,1)S(1)} %get-tuple-element.349), channel_id=1, source_target_pairs={{0,1},{1,0},{2,3},{3,2},{4,5},{5,4},{6,7},{7,6},{8,9},{9,8},{10,11... | collective-permute-start | bytes 589832 | tf_op jit(solution)/shard_map/ppermute | solution.py:443
  187.6 10.9 %collective-permute-start.18 = (bf16[272,384]{1,0:T(8,128)(2,1)S(1)}, bf16[272,384]{1,0:T(8,128)(2,1)S(1)}, u32[]{:S(2)}, u32[]{:S(2)}) collective-permute-start(bf16[272,384]{1,0:T(8,128)(2,1)S(1)} %get-tuple-element.304), channel_id=1, source_target_pairs={{0,1},{1,0},{2,3},{3,2},{4,5},{5,4},{6,7},{7,6},{8,9},{9,8},{10,11... | collective-permute-start | bytes 626696 | tf_op jit(solution)/shard_map/ppermute | solution.py:443
  220.3 23.1 %collective-permute-start.27 = (bf16[288,384]{1,0:T(8,128)(2,1)}, bf16[288,384]{1,0:T(8,128)(2,1)}, u32[]{:S(2)}, u32[]{:S(2)}) collective-permute-start(bf16[288,384]{1,0:T(8,128)(2,1)} %pad_maximum_fusion.34), channel_id=1, source_target_pairs={{0,4},{4,0},{8,12},{12,8},{16,20},{20,16},{24,28},{28,24},{1,5},{5... | collective-permute-start | bytes 663560 | tf_op jit(solution)/shard_map/ppermute | solution.py:441
  220.3 23.1 %collective-permute-start.25 = (bf16[288,384]{1,0:T(8,128)(2,1)}, bf16[288,384]{1,0:T(8,128)(2,1)}, u32[]{:S(2)}, u32[]{:S(2)}) collective-permute-start(bf16[288,384]{1,0:T(8,128)(2,1)} %pad_maximum_fusion.34), channel_id=1, source_target_pairs={{0,5},{1,4},{2,7},{3,6},{4,1},{5,0},{6,3},{7,2},{8,13},{9,12},{10,... | collective-permute-start | bytes 663560 | tf_op jit(solution)/shard_map/ppermute | solution.py:449
  230.3 208.0 %reduce-scatter.5.cloned.1.call-start = ((), (), s32[]{:S(2)}) async-start(), calls=%async_computation.7 | async-start | bytes 1474560 | tf_op jit(solution)/shard_map/reduce_scatter | solution.py:852
  235.5 12.0 %collective-permute-start.21 = (bf16[256,768]{1,0:T(8,128)(2,1)}, bf16[256,768]{1,0:T(8,128)(2,1)}, u32[]{:S(2)}, u32[]{:S(2)}) collective-permute-start(bf16[256,768]{1,0:T(8,128)(2,1)} %fusion.61), channel_id=1, source_target_pairs={{0,4},{4,0},{8,12},{12,8},{16,20},{20,16},{24,28},{28,24},{1,5},{5... | collective-permute-start | bytes 1179656 | tf_op jit(solution)/shard_map/ppermute | solution.py:441
  235.5 7.9 %collective-permute-start.26 = (bf16[288,384]{1,0:T(8,128)(2,1)S(1)}, bf16[288,384]{1,0:T(8,128)(2,1)S(1)}, u32[]{:S(2)}, u32[]{:S(2)}) collective-permute-start(bf16[288,384]{1,0:T(8,128)(2,1)S(1)} %pad_maximum_fusion.35), channel_id=1, source_target_pairs={{0,1},{1,0},{2,3},{3,2},{4,5},{5,4},{6,7},{7,6},{8,9},{9,8},{10,11... | collective-permute-start | bytes 663560 | tf_op jit(solution)/shard_map/ppermute | solution.py:443
  248.8 28.0 %collective-permute-start.22 = (bf16[512,768]{1,0:T(8,128)(2,1)S(1)}, bf16[512,768]{1,0:T(8,128)(2,1)S(1)}, u32[]{:S(2)}, u32[]{:S(2)}) collective-permute-start(bf16[512,768]{1,0:T(8,128)(2,1)S(1)} %pad_maximum_fusion.13), channel_id=1, source_target_pairs={{0,2},{1,3},{6,4},{7,5},{8,10},{9,11},{14,12},{15,13},{16,18},{17,... | collective-permute-start | bytes 2359304 | tf_op jit(solution)/shard_map/ppermute | solution.py:756
  277.4 34.9 %collective-permute-start.23 = (bf16[512,768]{1,0:T(8,128)(2,1)S(1)}, bf16[512,768]{1,0:T(8,128)(2,1)S(1)}, u32[]{:S(2)}, u32[]{:S(2)}) collective-permute-start(bf16[512,768]{1,0:T(8,128)(2,1)S(1)} %broadcast_select_fusion.4), channel_id=1, source_target_pairs={{0,1},{1,0},{2,3},{3,2},{4,5},{5,4},{6,7},{7,6},{8,9},{9,8},{10,11... | collective-permute-start | bytes 2359304 | tf_op jit(solution)/shard_map/ppermute | solution.py:443
  282.9 17.5 %collective-permute-start.30 = (bf16[256,384]{1,0:T(8,128)(2,1)S(1)}, bf16[256,384]{1,0:T(8,128)(2,1)S(1)}, u32[]{:S(2)}, u32[]{:S(2)}) collective-permute-start(bf16[256,384]{1,0:T(8,128)(2,1)S(1)} %get-tuple-element.309), channel_id=1, source_target_pairs={{0,1},{1,0},{2,3},{3,2},{4,5},{5,4},{6,7},{7,6},{8,9},{9,8},{10,11... | collective-permute-start | bytes 589832 | tf_op jit(solution)/shard_map/ppermute | solution.py:443
  284.1 22.2 %collective-permute-start.29 = (bf16[256,384]{1,0:T(8,128)(2,1)S(1)}, bf16[256,384]{1,0:T(8,128)(2,1)S(1)}, u32[]{:S(2)}, u32[]{:S(2)}) collective-permute-start(bf16[256,384]{1,0:T(8,128)(2,1)S(1)} %get-tuple-element.310), channel_id=1, source_target_pairs={{0,5},{1,4},{2,7},{3,6},{4,1},{5,0},{6,3},{7,2},{8,13},{9,12},{10,... | collective-permute-start | bytes 589832 | tf_op jit(solution)/shard_map/ppermute | solution.py:449
  286.1 20.2 %collective-permute-start.28 = (bf16[256,384]{1,0:T(8,128)(2,1)S(1)}, bf16[256,384]{1,0:T(8,128)(2,1)S(1)}, u32[]{:S(2)}, u32[]{:S(2)}) collective-permute-start(bf16[256,384]{1,0:T(8,128)(2,1)S(1)} %get-tuple-element.311), channel_id=1, source_target_pairs={{0,4},{4,0},{8,12},{12,8},{16,20},{20,16},{24,28},{28,24},{1,5},{5... | collective-permute-start | bytes 589832 | tf_op jit(solution)/shard_map/ppermute | solution.py:441
  288.9 29.3 %collective-permute-start.36 = (bf16[1,4,96,768]{3,2,1,0:T(8,128)(2,1)S(1)}, bf16[1,4,96,768]{3,2,1,0:T(8,128)(2,1)S(1)}, u32[]{:S(2)}, u32[]{:S(2)}) collective-permute-start(bf16[1,4,96,768]{3,2,1,0:T(8,128)(2,1)S(1)} %dynamic-slice_bitcast_fusion.6), channel_id=1, source_target_pairs={{0,4},{4,0},{8,12},{12,8},{16,20},{20,16},{24,28},{28,24},{1,5},{5... | collective-permute-start | bytes 1769480 | tf_op jit(solution)/shard_map/ppermute | solution.py:441
  300.4 47.6 %collective-permute-start.37 = (bf16[2,512,768]{2,1,0:T(8,128)(2,1)}, bf16[2,512,768]{2,1,0:T(8,128)(2,1)}, u32[]{:S(2)}, u32[]{:S(2)}) collective-permute-start(bf16[2,512,768]{2,1,0:T(8,128)(2,1)} %fusion.39), channel_id=1, source_target_pairs={{0,4},{4,0},{8,12},{12,8},{16,20},{20,16},{24,28},{28,24},{1,5},{5... | collective-permute-start | bytes 4718600 | tf_op jit(solution)/shard_map/ppermute | solution.py:441
  312.3 29.8 %collective-permute-start.35 = (bf16[2,4,96,768]{3,2,1,0:T(8,128)(2,1)}, bf16[2,4,96,768]{3,2,1,0:T(8,128)(2,1)}, u32[]{:S(2)}, u32[]{:S(2)}) collective-permute-start(bf16[2,4,96,768]{3,2,1,0:T(8,128)(2,1)} %fusion.67), channel_id=1, source_target_pairs={{0,4},{4,0},{8,12},{12,8},{16,20},{20,16},{24,28},{28,24},{1,5},{5... | collective-permute-start | bytes 3538952 | tf_op jit(solution)/shard_map/ppermute | solution.py:441
  335.7 8.0 %collective-permute-start.34 = (bf16[2,256,768]{2,1,0:T(8,128)(2,1)S(1)}, bf16[2,256,768]{2,1,0:T(8,128)(2,1)S(1)}, u32[]{:S(2)}, u32[]{:S(2)}) collective-permute-start(bf16[2,256,768]{2,1,0:T(8,128)(2,1)S(1)} %fusion.89), channel_id=1, source_target_pairs={{0,4},{4,0},{8,12},{12,8},{16,20},{20,16},{24,28},{28,24},{1,5},{5... | collective-permute-start | bytes 2359304 | tf_op jit(solution)/shard_map/ppermute | solution.py:441
  352.2 59.9 %collective-permute-start.47 = (bf16[2,512,768]{2,1,0:T(8,128)(2,1)}, bf16[2,512,768]{2,1,0:T(8,128)(2,1)}, u32[]{:S(2)}, u32[]{:S(2)}) collective-permute-start(bf16[2,512,768]{2,1,0:T(8,128)(2,1)} %fusion.9), channel_id=1, source_target_pairs={{2,4},{3,5},{4,2},{5,3},{10,12},{11,13},{12,10},{13,11},{18,20},{1... | collective-permute-start | bytes 4718600 | tf_op jit(solution)/shard_map/ppermute | solution.py:582
  357.0 25.7 %collective-permute-start.38 = (bf16[256,768]{1,0:T(8,128)(2,1)}, bf16[256,768]{1,0:T(8,128)(2,1)}, u32[]{:S(2)}, u32[]{:S(2)}) collective-permute-start(bf16[256,768]{1,0:T(8,128)(2,1)} %fusion.124), channel_id=1, source_target_pairs={{0,1},{1,0},{2,3},{3,2},{4,5},{5,4},{6,7},{7,6},{8,9},{9,8},{10,11... | collective-permute-start | bytes 1179656 | tf_op jit(solution)/shard_map/ppermute | solution.py:443
  358.9 39.2 %collective-permute-start.40 = (bf16[4,96,768]{2,1,0:T(8,128)(2,1)}, bf16[4,96,768]{2,1,0:T(8,128)(2,1)}, u32[]{:S(2)}, u32[]{:S(2)}) collective-permute-start(bf16[4,96,768]{2,1,0:T(8,128)(2,1)} %get-tuple-element.238), channel_id=1, source_target_pairs={{0,8},{4,12},{8,0},{12,4},{16,24},{20,28},{24,16},{28,20},{1,9},{5... | collective-permute-start | bytes 1769480 | tf_op jit(solution)/shard_map/ppermute | solution.py:441
  359.4 41.6 %collective-permute-start.42 = (bf16[4,96,768]{2,1,0:T(8,128)(2,1)}, bf16[4,96,768]{2,1,0:T(8,128)(2,1)}, u32[]{:S(2)}, u32[]{:S(2)}) collective-permute-start(bf16[4,96,768]{2,1,0:T(8,128)(2,1)} %get-tuple-element.239), channel_id=1, source_target_pairs={{0,24},{4,28},{8,16},{12,20},{16,8},{20,12},{24,0},{28,4},{1,25},{... | collective-permute-start | bytes 1769480 | tf_op jit(solution)/shard_map/ppermute | solution.py:441
  361.6 41.0 %collective-permute-start.41 = (bf16[4,96,768]{2,1,0:T(8,128)(2,1)}, bf16[4,96,768]{2,1,0:T(8,128)(2,1)}, u32[]{:S(2)}, u32[]{:S(2)}) collective-permute-start(bf16[4,96,768]{2,1,0:T(8,128)(2,1)} %get-tuple-element.240), channel_id=1, source_target_pairs={{0,16},{4,20},{8,24},{12,28},{16,0},{20,4},{24,8},{28,12},{1,17},{... | collective-permute-start | bytes 1769480 | tf_op jit(solution)/shard_map/ppermute | solution.py:441
  387.3 9.0 %collective-permute-start.39 = (bf16[256,768]{1,0:T(8,128)(2,1)}, bf16[256,768]{1,0:T(8,128)(2,1)}, u32[]{:S(2)}, u32[]{:S(2)}) collective-permute-start(bf16[256,768]{1,0:T(8,128)(2,1)} %add_convert_fusion), channel_id=1, source_target_pairs={{0,4},{4,0},{8,12},{12,8},{16,20},{20,16},{24,28},{28,24},{1,5},{5... | collective-permute-start | bytes 1179656 | tf_op jit(solution)/shard_map/ppermute | solution.py:441
  396.3 10.0 %collective-permute-start.43 = (bf16[1,4,96,768]{3,2,1,0:T(8,128)(2,1)S(1)}, bf16[1,4,96,768]{3,2,1,0:T(8,128)(2,1)S(1)}, u32[]{:S(2)}, u32[]{:S(2)}) collective-permute-start(bf16[1,4,96,768]{3,2,1,0:T(8,128)(2,1)S(1)} %dynamic-slice_bitcast_fusion.2), channel_id=1, source_target_pairs={{0,4},{4,0},{8,12},{12,8},{16,20},{20,16},{24,28},{28,24},{1,5},{5... | collective-permute-start | bytes 1769480 | tf_op jit(solution)/shard_map/ppermute | solution.py:441
  398.1 8.4 %collective-permute-start.44 = (bf16[4,96,768]{2,1,0:T(8,128)(2,1)S(1)}, bf16[4,96,768]{2,1,0:T(8,128)(2,1)S(1)}, u32[]{:S(2)}, u32[]{:S(2)}) collective-permute-start(bf16[4,96,768]{2,1,0:T(8,128)(2,1)S(1)} %dynamic-slice_bitcast_fusion.1), channel_id=1, source_target_pairs={{0,4},{4,0},{8,12},{12,8},{16,20},{20,16},{24,28},{28,24},{1,5},{5... | collective-permute-start | bytes 1769480 | tf_op jit(solution)/shard_map/ppermute | solution.py:441
  401.1 39.8 %collective-permute-start.45 = (bf16[512,768]{1,0:T(8,128)(2,1)}, bf16[512,768]{1,0:T(8,128)(2,1)}, u32[]{:S(2)}, u32[]{:S(2)}) collective-permute-start(bf16[512,768]{1,0:T(8,128)(2,1)} %pad_maximum_fusion.14), channel_id=1, source_target_pairs={{0,2},{1,3},{6,4},{7,5},{8,10},{9,11},{14,12},{15,13},{16,18},{17,... | collective-permute-start | bytes 2359304 | tf_op jit(solution)/shard_map/ppermute | solution.py:756
  408.0 12.6 %collective-permute-start.48 = (bf16[3,96,768]{2,1,0:T(8,128)(2,1)}, bf16[3,96,768]{2,1,0:T(8,128)(2,1)}, u32[]{:S(2)}, u32[]{:S(2)}) collective-permute-start(bf16[3,96,768]{2,1,0:T(8,128)(2,1)} %get-tuple-element.255), channel_id=1, source_target_pairs={{0,8},{4,12},{8,0},{12,4},{16,24},{20,28},{24,16},{28,20},{1,9},{5... | collective-permute-start | bytes 1327112 | tf_op jit(solution)/shard_map/ppermute | solution.py:441
  408.6 20.8 %collective-permute-start.50 = (bf16[3,96,768]{2,1,0:T(8,128)(2,1)}, bf16[3,96,768]{2,1,0:T(8,128)(2,1)}, u32[]{:S(2)}, u32[]{:S(2)}) collective-permute-start(bf16[3,96,768]{2,1,0:T(8,128)(2,1)} %get-tuple-element.256), channel_id=1, source_target_pairs={{0,24},{4,28},{8,16},{12,20},{16,8},{20,12},{24,0},{28,4},{1,25},{... | collective-permute-start | bytes 1327112 | tf_op jit(solution)/shard_map/ppermute | solution.py:441
  409.5 26.6 %collective-permute-start.49 = (bf16[3,96,768]{2,1,0:T(8,128)(2,1)}, bf16[3,96,768]{2,1,0:T(8,128)(2,1)}, u32[]{:S(2)}, u32[]{:S(2)}) collective-permute-start(bf16[3,96,768]{2,1,0:T(8,128)(2,1)} %get-tuple-element.257), channel_id=1, source_target_pairs={{0,16},{4,20},{8,24},{12,28},{16,0},{20,4},{24,8},{28,12},{1,17},{... | collective-permute-start | bytes 1327112 | tf_op jit(solution)/shard_map/ppermute | solution.py:441
  415.4 114.5 %all-to-all-start.1 = ((bf16[8,128,768]{2,1,0:T(8,128)(2,1)}), bf16[8,128,768]{2,1,0:T(8,128)(2,1)S(1)}, u32[]{:S(2)}, u32[]{:S(2)}) async-start(bf16[8,128,768]{2,1,0:T(8,128)(2,1)} %bitcast.124), calls=%async_computation.3 | async-start | bytes 3145728 | tf_op jit(solution)/shard_map/all_to_all | solution.py:883
  444.6 65.2 %collective-permute-start.46 = (bf16[512,768]{1,0:T(8,128)(2,1)}, bf16[512,768]{1,0:T(8,128)(2,1)}, u32[]{:S(2)}, u32[]{:S(2)}) collective-permute-start(bf16[512,768]{1,0:T(8,128)(2,1)} %select_select_fusion), channel_id=1, source_target_pairs={{0,1},{1,0},{2,3},{3,2},{4,5},{5,4},{6,7},{7,6},{8,9},{9,8},{10,11... | collective-permute-start | bytes 2359304 | tf_op jit(solution)/shard_map/ppermute | solution.py:443
  455.9 20.9 %collective-permute-start.51 = (bf16[2,6,96,192]{2,3,1,0:T(8,128)(2,1)}, bf16[2,6,96,192]{2,3,1,0:T(8,128)(2,1)S(1)}, u32[]{:S(2)}, u32[]{:S(2)}) collective-permute-start(bf16[2,6,96,192]{2,3,1,0:T(8,128)(2,1)} %bitcast.371), channel_id=1, source_target_pairs={{0,1},{1,0},{2,3},{3,2},{4,5},{5,4},{6,7},{7,6},{8,9},{9,8},{10,11... | collective-permute-start | bytes 1327112 | tf_op jit(solution)/shard_map/ppermute | solution.py:443
  477.1 19.2 %collective-permute-start.52 = (bf16[9,96,192]{1,2,0:T(8,128)(2,1)S(1)}, bf16[9,96,192]{1,2,0:T(8,128)(2,1)S(1)}, u32[]{:S(2)}, u32[]{:S(2)}) collective-permute-start(bf16[9,96,192]{1,2,0:T(8,128)(2,1)S(1)} %pad_maximum_fusion.23), channel_id=1, source_target_pairs={{0,2},{1,3},{2,0},{3,1},{4,6},{5,7},{6,4},{7,5},{8,10},{9,11},{10,... | collective-permute-start | bytes 995336 | tf_op jit(solution)/shard_map/ppermute | solution.py:443
  (103 other events, 756.3 us)
Sparse Core Ops, SparseCore 0:
  52.2 57.5 all-gather.2
  133.1 59.5 all-gather.4
  230.5 76.6 reduce-scatter.2
  388.5 36.5 reduce-scatter.4

commit v3 on v2

--- a/solution.py
+++ b/solution.py
@@ -218,17 +218,20 @@
             key_set = key_ref[image * keys : (image + 1) * keys, :]
             value_set = value_ref[image * keys : (image + 1) * keys, :]
             kept = own_columns(split, image, low)
+            halves = jnp.concatenate([half_lanes(query_set, half) for half in range(2)], axis=0)
+            scores = mm(key_set, halves, NT)
+            largest = jnp.max(scores, axis=0, keepdims=True)
+            weights = jnp.exp2((scores - largest) * (scale * LOG2E))
+            total = jnp.sum(weights, axis=0, keepdims=True)
+            mixed = mm(value_set, weights.astype(jnp.bfloat16), TN) / total
+            logs = largest * scale + jnp.log(total)
             pieces = []
             for half in range(2):
-                scores = mm(key_set, half_lanes(query_set, half), NT)
-                largest = jnp.max(scores, axis=0, keepdims=True)
-                weights = jnp.exp2((scores - largest) * (scale * LOG2E))
-                total = jnp.sum(weights, axis=0, keepdims=True)
-                mixed = mm(value_set, weights.astype(jnp.bfloat16), TN) / total
-                pieces.append(mixed[half * HEAD_DIM : (half + 1) * HEAD_DIM])
+                own = slice(half * BLOCK, (half + 1) * BLOCK)
+                pieces.append(mixed[half * HEAD_DIM : (half + 1) * HEAD_DIM, own])
                 held = sums_ref[0, half : half + 1, pl.ds(low, BLOCK)]
                 sums_ref[0, half : half + 1, pl.ds(low, BLOCK)] = jnp.where(
-                    kept, largest * scale + jnp.log(total), held
+                    kept, logs[:, own], held
                 )
             fresh = jnp.concatenate(pieces, axis=0).T
             held = out_ref[pl.ds(low, BLOCK), :].astype(jnp.float32)
@@ -301,25 +304,26 @@
             key_set = key_ref[span, :]
             value_set = value_ref[span, :]
             kept = own_columns(split, image, low)
-            pieces = []
+            shifts, inners = [], []
             for half in range(2):
                 sums = stats_ref[0, half : half + 1, pl.ds(low, BLOCK)]
-                inner = stats_ref[0, 2 + half : 3 + half, pl.ds(low, BLOCK)]
-                shift = jnp.where(kept, sums * LOG2E, -masked_score)
-                query_half = half_lanes(query_set, half)
-                grad_half = half_lanes(grad_set, half)
-                scores = mm(key_set, query_half, NT)
-                probs = jnp.exp2(scores * (scale * LOG2E) - shift)
-                grad_probs = mm(value_set, grad_half, NT)
-                grad_scores = (probs * (grad_probs - inner)).astype(jnp.bfloat16)
-                value_new = mm(probs.astype(jnp.bfloat16), grad_half)
-                key_new = mm(grad_scores, query_half)
-                value_part = value_new if half == 0 else value_part + value_new
-                key_part = key_new if half == 0 else key_part + key_new
-                mixed = mm(key_set, grad_scores, TN) * scale
-                pieces.append(mixed[half * HEAD_DIM : (half + 1) * HEAD_DIM])
-            key_acc[...] += key_part
-            value_acc[...] += value_part
+                inners.append(stats_ref[0, 2 + half : 3 + half, pl.ds(low, BLOCK)])
+                shifts.append(jnp.where(kept, sums * LOG2E, -masked_score))
+            shift = jnp.concatenate(shifts, axis=1)
+            inner = jnp.concatenate(inners, axis=1)
+            queries = jnp.concatenate([half_lanes(query_set, half) for half in range(2)], axis=0)
+            grads = jnp.concatenate([half_lanes(grad_set, half) for half in range(2)], axis=0)
+            scores = mm(key_set, queries, NT)
+            probs = jnp.exp2(scores * (scale * LOG2E) - shift)
+            grad_probs = mm(value_set, grads, NT)
+            grad_scores = (probs * (grad_probs - inner)).astype(jnp.bfloat16)
+            value_acc[...] += mm(probs.astype(jnp.bfloat16), grads)
+            key_acc[...] += mm(grad_scores, queries)
+            mixed = mm(key_set, grad_scores, TN) * scale
+            pieces = [
+                mixed[half * HEAD_DIM : (half + 1) * HEAD_DIM, half * BLOCK : (half + 1) * BLOCK]
+                for half in range(2)
+            ]
             fresh = jnp.concatenate(pieces, axis=0).T
             held = query_out[pl.ds(low, BLOCK), :].astype(jnp.float32)
             query_out[pl.ds(low, BLOCK), :] = jnp.where(
@@ -566,6 +570,24 @@
     other_rows = pick(cotangent.reshape(4, row_count, width), member ^ 1)
     cotangent_rows = jnp.where(here, quarter(cotangent), send(other_rows, (1, 0)))
 
+    segments, images, weights = token_layout(
+        layout[0:1], layout[1:2], layout[2:3], tok_rows, IMG_DEV
+    )
+    image_tok = images[0]
+    weight_tok = weights[0]
+    text_ends = jnp.cumsum(layout[0])
+    position = jnp.arange(tok_rows, dtype=jnp.int32)
+    starts = jnp.max(
+        jnp.where(position[None, :] >= text_ends[:, None], text_ends[:, None], 0), axis=0
+    ).reshape(1, tok_rows)
+    of_zero = (image_tok == 0).astype(jnp.int32)
+    before = jnp.cumsum(of_zero)
+    split = before[-1]
+    place = jnp.where(image_tok == 0, before - 1, split + position - before)
+    sorter = (place[None, :] == position[:, None]).astype(bf16)
+    unsorter = (place[:, None] == position[None, :]).astype(bf16)
+    split = split.reshape(1)
+
     entry_low = entry_weights.astype(bf16).transpose(1, 0, 2)
     exit_low = exit_weights.astype(bf16).transpose(2, 0, 1)
     expand_low = expand_weights.astype(bf16).transpose(1, 0, 2)
@@ -626,6 +648,7 @@
     exit_cross_t = rest_full[:, 4 * width :]
 
     self_set = jnp.concatenate(in_order([mine, theirs], core), axis=0)
+    self_set = after(self_set, place, weight_tok, starts)
     self_full = [after(p, held) for p in chip_spread(self_set, chip)]
     self_full = jnp.concatenate(self_full, axis=0)
     gain_values = self_full[:, 3 * local : 3 * local + 3].astype(f32).transpose(1, 0)
@@ -636,24 +659,6 @@
         ],
         axis=1,
     )
-
-    segments, images, weights = token_layout(
-        layout[0:1], layout[1:2], layout[2:3], tok_rows, IMG_DEV
-    )
-    image_tok = images[0]
-    weight_tok = weights[0]
-    text_ends = jnp.cumsum(layout[0])
-    position = jnp.arange(tok_rows, dtype=jnp.int32)
-    starts = jnp.max(
-        jnp.where(position[None, :] >= text_ends[:, None], text_ends[:, None], 0), axis=0
-    ).reshape(1, tok_rows)
-    of_zero = (image_tok == 0).astype(jnp.int32)
-    before = jnp.cumsum(of_zero)
-    split = before[-1]
-    place = jnp.where(image_tok == 0, before - 1, split + position - before)
-    sorter = (place[None, :] == position[:, None]).astype(bf16)
-    unsorter = (place[:, None] == position[None, :]).astype(bf16)
-    split = split.reshape(1)
 
     stream = stream_low.astype(f32)
     hidden_one = rms_norm(stream, gain_values[0]).astype(bf16)
@@ -793,7 +798,6 @@
     stats = jnp.concatenate([sums, inner, jnp.zeros((heads, 4, tok_rows), f32)], axis=1)
     grad_query, grad_key, grad_value = cross_backward(split, queries, grads, stats, pairs)
     grad_query = after(mm(unsorter, grad_query).astype(bf16), output)
-    output = rows_beside(output).astype(f32)
     grad_pair = after(jnp.concatenate([grad_key, grad_value], axis=1), grad_query)
     memory_part = mm(grad_pair, cross_pair, NT).reshape(IMG_DEV, 2, patches, width)
     memory_came = send(memory_part[:, 1].astype(bf16), (1, 0))
@@ -823,12 +827,18 @@
 
     grad_low = grad_rows.astype(bf16)
     grad_self = mm(grad_low, exit_self_t).astype(bf16)
-    grad_self = after(grad_self, output)
+    output = rows_beside(after(output, grad_self)).astype(f32)
     by_columns = jnp.stack([grad_self[:, s * local : (s + 1) * local] for s in range(4)])
     pieces = member_pieces(lambda d: pick(by_columns, columns ^ (2 * (d & 1) + (d >> 1))))
     grad_self = jnp.pad(
         jnp.concatenate(in_order(pieces, member), axis=0), ((0, 0), (0, 256 - local))
     )
+    second_grads = jnp.concatenate(
+        [second_grads[:, h * 3 * hidden : (h + 1) * 3 * hidden] for h in range(head_count)], axis=0
+    )
+    grad_self = after(grad_self, second_grads)
+    second_grads = lax.psum_scatter(second_grads, "head", scatter_dimension=0, tiled=True)
+    second_grads = second_grads.astype(f32)
     grad_qkv = self_backward(qkv, grad_self, self_out, self_sums, starts)
     grad_normed = mm(grad_qkv, self_weights, NT)
     inverse = lax.rsqrt(jnp.mean(stream * stream, axis=-1, keepdims=True) + norm_eps)
@@ -843,14 +853,7 @@
     cross_sums = chip_sum(cross_chips)
     memory_sum = after(memory_part[:, 0], cross_chips) + memory_came.astype(f32)
     memory_sum = memory_sum.astype(bf16)
-    second_grads = after(second_grads, memory_sum)
-    second_grads = jnp.concatenate(
-        [second_grads[:, h * 3 * hidden : (h + 1) * 3 * hidden] for h in range(head_count)], axis=0
-    )
-    came = after(came, second_grads)
     memory_sum = across(memory_sum)
-    second_grads = lax.psum_scatter(second_grads, "head", scatter_dimension=0, tiled=True)
-    second_grads = second_grads.astype(f32)
     grad_normed = pick(kept, near) + came.astype(f32)
     grad_input, _ = rms_pull(stream_rows, gain_values[0], grad_normed)
     token_grads = (grad_rows + grad_input).astype(bf16)
@@ -911,18 +914,17 @@
     kept = lax.dynamic_index_in_dim(by_head, near, 1, keepdims=False)
     came = lax.dynamic_index_in_dim(by_head, 1 - near, 1, keepdims=False)
     kept = kept + send(came.astype(bf16), (0, 1)).astype(f32)
-    own_three, far_three = [
-        jnp.stack([sums[5 + w, :, s * local : (s + 1) * local] for s in range(3)]) for w in range(2)
-    ]
-    far_eight = jnp.concatenate([pick(kept, 1 - side), far_three], axis=0)
-    own_eight = jnp.concatenate([pick(kept, side), own_three], axis=0)
-    first_grads = own_eight + send(far_eight.astype(bf16), (0, 2)).astype(f32)
+    self_grads = sums[5] + send(sums[6].astype(bf16), (0, 2)).astype(f32)
+    first_grads = pick(kept, side) + send(pick(kept, 1 - side).astype(bf16), (0, 2)).astype(f32)
     exit_grads = jnp.stack([first_grads[0].T, first_grads[2].T])
     expand_grads = jnp.stack([second_grads[:, 0:hidden], second_grads[:, hidden : 2 * hidden]])
     contract_grads = second_grads[:, 2 * hidden :].T
 
     gain_grads = first_grads[5, :, 0:3].T
-    entry_grads = jnp.stack([first_grads[w] for w in (6, 7, 8, 1, 3, 4)])
+    entry_grads = jnp.stack(
+        [self_grads[:, s * local : (s + 1) * local] for s in range(3)]
+        + [first_grads[w] for w in (1, 3, 4)]
+    )
 
     entry_mean, entry_square, entry_step = lamb_step(
         entry_weights, entry_grads, entry_first, entry_second, weight_decay
@@ -957,7 +959,7 @@
             jnp.sum(gains_step * gains_step, axis=1) / head_count,
         ]
     )
-    weight_squares, step_squares = all_sum(after(jnp.stack([weight_local, step_local]), token_grads))
+    weight_squares, step_squares = all_sum(after(jnp.stack([weight_local, step_local]), token_grads, memory_grads))
     weight_norm = jnp.sqrt(weight_squares)
     step_norm = jnp.sqrt(step_squares)
     ratio = learn_rate * weight_norm / (step_norm + adam_eps)

time: 556 us -> 549 us (0.987)
  waiting for transfers between devices: 170 us -> 141 us
  starting transfers between devices: 68.2 us -> 80.9 us
  local copies, waits for them, and re-layouts: 52.5 us -> 62.2 us
    ppermute x17 -> x18, waiting for transfers between devices: 93.9 us -> 70.1 us  [send(): lax.ppermute(array, 'head', [(s, s ^ head_bits) for s in range(head_count)])]
    ppermute x17 -> x18, starting transfers between devices: 24.4 us -> 37.4 us  [send(): lax.ppermute(array, 'head', [(s, s ^ head_bits) for s in range(head_count)])]
    unnamed x175 -> x226, local copies, waits for them, and re-layouts: 5.2 us -> 11.5 us
    slice x24 -> x27, local copies, waits for them, and re-layouts: 15.9 us -> 19.4 us  [after(): marks = [e[(0,) * e.ndim].astype(jnp.float32) for e in earlier]]
  transfers between devices with their start and end apart: 65 -> 66, of which waited for: 25 -> 26; matrix products, arithmetic and copies ran while one was open for 28% -> 30% of each run, Pallas kernels for 14% -> 11%
where the time goes in v3:
time: 549 us; the launch traced here: 540 us
  waiting for transfers between devices  141 us (26%)
  other arithmetic  81.5 us (15%)
  starting transfers between devices  80.9 us (15%)
  Pallas kernels  69.9 us (13%)
  local copies, waits for them, and re-layouts  62.2 us (11%)
  matrix products  59.1 us (11%)
  between operations  45.9 us (8%)
    ppermute x18, waiting for transfers between devices, send(): lax.ppermute(array, 'head', [(s, s ^ head_bits) for s in range(head_count)])  70.1 us
    dot_general x27, matrix products, mm(): return lax.dot_general(a, b, dims, preferred_element_type=jnp.float32)  55.6 us
    ppermute x18, starting transfers between devices, send(): lax.ppermute(array, 'head', [(s, s ^ head_bits) for s in range(head_count)])  37.4 us
    pallas_call x1, Pallas kernels, cross_backward(): pl.pallas_call(cross_backward_kernel, grid=(groups,), in_specs=[pl.BlockS...  26.8 us
    ppermute x2, waiting for transfers between devices, across(): return jnp.where(here, array, lax.ppermute(array, ('dp', 'head'), pairs))  22.8 us
    ppermute x32, waiting for transfers between devices, send(): lax.ppermute(array, 'dp', [(s, s ^ dp_bits) for s in range(dp_count)])  21.3 us
    pallas_call x1, Pallas kernels, cross_forward(): pl.pallas_call(cross_forward_kernel, grid=(groups,), in_specs=[pl.BlockSp...  20.4 us
    slice x27, local copies, waits for them, and re-layouts, after(): marks = [e[(0,) * e.ndim].astype(jnp.float32) for e in earlier]  19.4 us
  transfers between devices with their start and end apart: 66, of which 26 were waited for; matrix products, arithmetic and copies ran while one was open for 30% of the time, Pallas kernels for 11%

profile of v3, /device:TPU:18, one launch (start us, length us, event | category | flops | bytes accessed | tf_op | source)
XLA Modules:
  0.0 540.5 jit_solution(11808403142991498800)
XLA Ops:
  7.2 4.4 all-to-all-start
  13.6 17.6 %all-to-all-done = bf16[8,128,768]{2,1,0:T(8,128)(2,1)S(1)} async-done(((bf16[8,128,768]{2,1,0:T(8,128)(2,1)}), bf16[8,128,768]{2,1,0:T(8,128)(2,1)S(1)}, u32[]{:S(2)}, u32[]{:S(2)}) %all-to-all-start) | async-done | bytes 1572896 | tf_op jit(solution)/shard_map/all_to_all | solution.py:606
  34.4 2.4 collective-permute-start.12
  36.8 11.4 %collective-permute-done.12 = bf16[2,96,960]{1,2,0:T(8,128)(2,1)S(1)} collective-permute-done((bf16[2,96,960]{1,2,0:T(8,128)(2,1)S(1)}, bf16[2,96,960]{1,2,0:T(8,128)(2,1)S(1)}, u32[]{:S(2)}, u32[]{:S(2)}) %collective-permute-start.12) | collective-permute-done | bytes 368672 | tf_op jit(solution)/shard_map/ppermute | solution.py:447
  71.6 20.4 %collective-permute-done.3 = bf16[2,512,768]{2,1,0:T(8,128)(2,1)} collective-permute-done((bf16[2,512,768]{2,1,0:T(8,128)(2,1)S(1)}, bf16[2,512,768]{2,1,0:T(8,128)(2,1)}, u32[]{:S(2)}, u32[]{:S(2)}) %collective-permute-start.3) | collective-permute-done | bytes 1572896 | tf_op jit(solution)/shard_map/ppermute | solution.py:604
  98.3 5.8 %self_forward.1 = (bf16[1024,256]{1,0:T(8,128)(2,1)S(1)}, f32[8,1024]{1,0:T(8,128)S(1)}) custom-call(bf16[1024,768]{1,0:T(8,128)(2,1)S(1)} %convolution_convert_fusion.1.qkv_ref, s32[1,1024]{1,0:T(1,128)S(1)} %bitcast.410), custom_call_target="tpu_custom_call" | custom-call | flops 6000000000 | bytes 2097152 | tf_op jit(solution)/shard_map/self_forward/pallas_call | solution.py:104
  106.1 4.4 collective-permute-start.11
  121.5 8.5 %collective-permute-done.21 = bf16[2,96,3,512]{3,1,2,0:T(8,128)(2,1)} collective-permute-done((bf16[2,96,3,512]{3,1,2,0:T(8,128)(2,1)}, bf16[2,96,3,512]{3,1,2,0:T(8,128)(2,1)}, u32[]{:S(2)}, u32[]{:S(2)}) %collective-permute-start.21) | collective-permute-done | bytes 589856 | tf_op jit(solution)/shard_map/ppermute | solution.py:447
  133.4 2.7 reshape.698
  141.5 2.7 convolution_convert_fusion.7
  148.6 4.4 convolution_convert_fusion.key_ref.value_ref
  153.0 2.9 collective-permute-done.14
  157.3 20.4 %cross_forward.1 = (bf16[1024,384]{1,0:T(8,128)(2,1)S(1)}, f32[3,8,1024]{2,1,0:T(8,128)S(1)}) custom-call(s32[1]{0:T(128)} %slice.492.split_ref, bf16[1024,384]{1,0:T(8,128)(2,1)S(1)} %fusion.53.query_ref, bf16[2048,768]{1,0:T(8,128)(2,1)} %convolution_convert_fusion.key_ref.value_ref, bf16[2048,768]{1,0:T(8,128)(2,1)} %convolution_convert_fusion.key_ref.value_ref), custom_call_target="tpu_custom_call" | custom-call | flops 28000000000 | bytes 3145728 | tf_op jit(solution)/shard_map/cross_forward/pallas_call | solution.py:250
  184.2 3.0 collective-permute-done.18
  187.6 4.6 collective-permute-done.19
  196.1 3.1 fusion.12
  199.2 3.5 fusion.16
  202.7 2.9 multiply_convert_fusion.2
  208.7 2.9 convert_multiply_fusion
  213.8 8.9 %hidden_grads.1 = bf16[768,6144]{1,0:T(8,128)(2,1)} custom-call(bf16[256,768]{1,0:T(8,128)(2,1)S(1)} %broadcast_select_fusion.15.rows_ref, bf16[256,768]{1,0:T(8,128)(2,1)S(1)} %broadcast_select_fusion.14.grad_ref, bf16[256,2048]{1,0:T(8,128)(2,1)S(1)} %get-tuple-element.234.gate_ref, bf16[256,2048]{1,0:T(8,128)(2,1)S(1)} %get-tuple-element.233.up_ref, ...), custom_call_target="tpu_custom_call" | custom-call | flops 2415919104 | bytes 9437184 | tf_op jit(solution)/shard_map/hidden_grads/pallas_call | solution.py:401
  231.4 4.7 fusion.61
  238.8 5.5 %collective-permute-done.25 = bf16[288,384]{1,0:T(8,128)(2,1)S(1)} collective-permute-done((bf16[288,384]{1,0:T(8,128)(2,1)S(1)}, bf16[288,384]{1,0:T(8,128)(2,1)S(1)}, u32[]{:S(2)}, u32[]{:S(2)}) %collective-permute-start.25) | collective-permute-done | bytes 221216 | tf_op jit(solution)/shard_map/ppermute | solution.py:447
  250.0 26.8 %cross_backward.1 = (bf16[1024,384]{1,0:T(8,128)(2,1)S(1)}, bf16[2048,384]{1,0:T(8,128)(2,1)S(1)}, bf16[2048,384]{1,0:T(8,128)(2,1)}) custom-call(s32[1]{0:T(128)} %slice.492.split_ref, bf16[1024,384]{1,0:T(8,128)(2,1)S(1)} %fusion.53.query_ref, bf16[1024,384]{1,0:T(8,128)(2,1)S(1)} %fusion.54.grad_ref, f32[3,8,1024]{2,1,0:T(8,128)S(1)} %maximum_maximum_fusion.stats_ref, ...), custom_call_target="tpu_custom_call" | custom-call | flops 28000000000 | bytes 6291456 | tf_op jit(solution)/shard_map/cross_backward/pallas_call | solution.py:343
  284.3 2.7 fusion.47
  287.0 2.7 fusion.37
  289.9 2.9 collective-permute-done.28
  304.5 2.8 collective-permute-done.32
  314.4 7.9 %self_backward.1 = bf16[1024,768]{1,0:T(8,128)(2,1)S(1)} custom-call(bf16[1024,768]{1,0:T(8,128)(2,1)} %copy-done, bf16[1024,256]{1,0:T(8,128)(2,1)S(1)} %fusion.121.grad_ref, bf16[1024,256]{1,0:T(8,128)(2,1)S(1)} %get-tuple-element.35.out_ref, f32[8,1024]{1,0:T(8,128)S(1)} %get-tuple-element.39.sums_ref, s32[1,1024]{1,0:T(1,128)S(1)} %bitcast.411), custom_call_target="tpu_custom_call" | custom-call | flops 8000000000 | bytes 5242880 | tf_op jit(solution)/shard_map/self_backward/pallas_call | solution.py:176
  330.4 3.3 fusion.48
  347.1 3.1 fusion.9
  350.2 12.1 %collective-permute-done.35 = bf16[256,768]{1,0:T(8,128)(2,1)S(1)} collective-permute-done((bf16[256,768]{1,0:T(8,128)(2,1)S(1)}, bf16[256,768]{1,0:T(8,128)(2,1)S(1)}, u32[]{:S(2)}, u32[]{:S(2)}) %collective-permute-start.35) | collective-permute-done | bytes 393248 | tf_op jit(solution)/shard_map/ppermute | solution.py:447
  376.4 3.8 collective-permute-start.47
  393.5 4.1 collective-permute-done.48
  397.5 10.4 %collective-permute-done.50 = bf16[3,96,768]{2,1,0:T(8,128)(2,1)S(1)} collective-permute-done((bf16[3,96,768]{2,1,0:T(8,128)(2,1)S(1)}, bf16[3,96,768]{2,1,0:T(8,128)(2,1)S(1)}, u32[]{:S(2)}, u32[]{:S(2)}) %collective-permute-start.50) | collective-permute-done | bytes 442400 | tf_op jit(solution)/shard_map/ppermute | solution.py:445
  407.9 2.6 collective-permute-done.49
  417.6 12.2 %collective-permute-start.45 = (bf16[512,768]{1,0:T(8,128)(2,1)}, bf16[512,768]{1,0:T(8,128)(2,1)}, u32[]{:S(2)}, u32[]{:S(2)}) collective-permute-start(bf16[512,768]{1,0:T(8,128)(2,1)} %select_select_fusion), channel_id=1, source_target_pairs={{0,1},{1,0},{2,3},{3,2},{4,5},{5,4},{6,7},{7,6},{8,9},{9,8},{10,11... | collective-permute-start | bytes 2359304 | tf_op jit(solution)/shard_map/ppermute | solution.py:447
  429.7 2.4 collective-permute-done.47
  444.9 4.7 all-to-all-start.1
  452.0 2.7 copy.166
  457.3 2.5 multiply_reduce_fusion.12
  463.5 9.1 %collective-permute-done.52 = bf16[2,6,96,192]{2,3,1,0:T(8,128)(2,1)} collective-permute-done((bf16[2,6,96,192]{2,3,1,0:T(8,128)(2,1)}, bf16[2,6,96,192]{2,3,1,0:T(8,128)(2,1)}, u32[]{:S(2)}, u32[]{:S(2)}) %collective-permute-start.52) | collective-permute-done | bytes 442400 | tf_op jit(solution)/shard_map/ppermute | solution.py:447
  474.3 2.6 collective-permute-start.53
  476.9 12.8 %collective-permute-done.53 = bf16[6,96,192]{1,2,0:T(8,128)(2,1)S(1)} collective-permute-done((bf16[6,96,192]{1,2,0:T(8,128)(2,1)S(1)}, bf16[6,96,192]{1,2,0:T(8,128)(2,1)S(1)}, u32[]{:S(2)}, u32[]{:S(2)}) %collective-permute-start.53) | collective-permute-done | bytes 221216 | tf_op jit(solution)/shard_map/ppermute | solution.py:447
  495.6 2.8 multiply_reduce_fusion.10
  511.4 2.6 collective-permute-done.55
  514.0 3.4 collective-permute-start.58
  518.9 2.7 collective-permute-start.59
  523.6 3.5 convert.51
  (594 shorter events, 198.4 us)
Async XLA Ops:
  7.2 23.9 %all-to-all-start = ((bf16[8,128,768]{2,1,0:T(8,128)(2,1)}), bf16[8,128,768]{2,1,0:T(8,128)(2,1)S(1)}, u32[]{:S(2)}, u32[]{:S(2)}) async-start(bf16[8,128,768]{2,1,0:T(8,128)(2,1)} %bitcast.435), calls=%async_computation | async-start | bytes 3145728 | tf_op jit(solution)/shard_map/all_to_all | solution.py:606
  11.6 105.7 %all-gather.3.cloned.1.call-start = ((), (), s32[]{:S(2)}) async-start(), calls=%async_computation.4 | async-start | bytes 6635520 | tf_op jit(solution)/shard_map/all_gather | solution.py:634
  13.2 19.9 %collective-permute-start.4 = (bf16[96,1536]{0,1:T(8,128)(2,1)}, bf16[96,1536]{0,1:T(8,128)(2,1)}, u32[]{:S(2)}, u32[]{:S(2)}) collective-permute-start(bf16[96,1536]{0,1:T(8,128)(2,1)} %pad_maximum_fusion.22), channel_id=1, source_target_pairs={{0,2},{1,3},{2,0},{3,1},{4,6},{5,7},{6,4},{7,5},{8,10},{9,11},{10,... | collective-permute-start | bytes 884744 | tf_op jit(solution)/shard_map/ppermute | solution.py:447
  34.4 13.9 %collective-permute-start.12 = (bf16[2,96,960]{1,2,0:T(8,128)(2,1)S(1)}, bf16[2,96,960]{1,2,0:T(8,128)(2,1)S(1)}, u32[]{:S(2)}, u32[]{:S(2)}) collective-permute-start(bf16[2,96,960]{1,2,0:T(8,128)(2,1)S(1)} %pad_maximum_fusion.19), channel_id=1, source_target_pairs={{0,1},{1,0},{2,3},{3,2},{4,5},{5,4},{6,7},{7,6},{8,9},{9,8},{10,11... | collective-permute-start | bytes 1105928 | tf_op jit(solution)/shard_map/ppermute | solution.py:447
  52.0 144.0 %all-gather.5.cloned.1.call-start = ((), (), s32[]{:S(2)}) async-start(), calls=%async_computation.5 | async-start | bytes 10616832 | tf_op jit(solution)/shard_map/all_gather | solution.py:684
  52.2 17.3 %collective-permute-start.2 = (bf16[1024,768]{1,0:T(8,128)(2,1)}, bf16[1024,768]{1,0:T(8,128)(2,1)}, u32[]{:S(2)}, u32[]{:S(2)}) collective-permute-start(bf16[1024,768]{1,0:T(8,128)(2,1)} %param.22), channel_id=1, source_target_pairs={{0,4},{4,0},{8,12},{12,8},{16,20},{20,16},{24,28},{28,24},{1,5},{5... | collective-permute-start | bytes 4718600 | tf_op jit(solution)/shard_map/ppermute | solution.py:445
  55.4 36.7 %collective-permute-start.3 = (bf16[2,512,768]{2,1,0:T(8,128)(2,1)S(1)}, bf16[2,512,768]{2,1,0:T(8,128)(2,1)}, u32[]{:S(2)}, u32[]{:S(2)}) collective-permute-start(bf16[2,512,768]{2,1,0:T(8,128)(2,1)S(1)} %bitcast.417), channel_id=1, source_target_pairs={{2,4},{3,5},{4,2},{5,3},{10,12},{11,13},{12,10},{13,11},{18,20},{1... | collective-permute-start | bytes 4718600 | tf_op jit(solution)/shard_map/ppermute | solution.py:604
  66.0 29.6 %collective-permute-start.8 = (bf16[192,640]{0,1:T(8,128)(2,1)S(1)}, bf16[192,640]{0,1:T(8,128)(2,1)S(1)}, u32[]{:S(2)}, u32[]{:S(2)}) collective-permute-start(bf16[192,640]{0,1:T(8,128)(2,1)S(1)} %maximum_select_fusion.9), channel_id=1, source_target_pairs={{0,8},{4,12},{8,0},{12,4},{16,24},{20,28},{24,16},{28,20},{1,9},{5... | collective-permute-start | bytes 737288 | tf_op jit(solution)/shard_map/ppermute | solution.py:445
  66.5 29.2 %collective-permute-start.7 = (bf16[192,640]{0,1:T(8,128)(2,1)S(1)}, bf16[192,640]{0,1:T(8,128)(2,1)S(1)}, u32[]{:S(2)}, u32[]{:S(2)}) collective-permute-start(bf16[192,640]{0,1:T(8,128)(2,1)S(1)} %maximum_select_fusion.9), channel_id=1, source_target_pairs={{0,16},{4,20},{8,24},{12,28},{16,0},{20,4},{24,8},{28,12},{1,17},{... | collective-permute-start | bytes 737288 | tf_op jit(solution)/shard_map/ppermute | solution.py:445
  68.1 27.5 %collective-permute-start.6 = (bf16[192,640]{0,1:T(8,128)(2,1)S(1)}, bf16[192,640]{0,1:T(8,128)(2,1)S(1)}, u32[]{:S(2)}, u32[]{:S(2)}) collective-permute-start(bf16[192,640]{0,1:T(8,128)(2,1)S(1)} %maximum_select_fusion.9), channel_id=1, source_target_pairs={{0,24},{4,28},{8,16},{12,20},{16,8},{20,12},{24,0},{28,4},{1,25},{... | collective-permute-start | bytes 737288 | tf_op jit(solution)/shard_map/ppermute | solution.py:445
  95.5 15.1 %collective-permute-start.20 = (bf16[96,3,512]{2,0,1:T(8,128)(2,1)S(1)}, bf16[96,3,512]{2,0,1:T(8,128)(2,1)S(1)}, u32[]{:S(2)}, u32[]{:S(2)}) collective-permute-start(bf16[96,3,512]{2,0,1:T(8,128)(2,1)S(1)} %broadcast_select_fusion.25), channel_id=1, source_target_pairs={{0,2},{1,3},{2,0},{3,1},{4,6},{5,7},{6,4},{7,5},{8,10},{9,11},{10,... | collective-permute-start | bytes 884744 | tf_op jit(solution)/shard_map/ppermute | solution.py:447
  106.1 9.9 %collective-permute-start.11 = (bf16[256,192]{1,0:T(8,128)(2,1)S(1)}, bf16[256,192]{1,0:T(8,128)(2,1)S(1)}, u32[]{:S(2)}, u32[]{:S(2)}) collective-permute-start(bf16[256,192]{1,0:T(8,128)(2,1)S(1)} %get-tuple-element.325), channel_id=1, source_target_pairs={{0,1},{1,0},{2,3},{3,2},{4,5},{5,4},{6,7},{7,6},{8,9},{9,8},{10,11... | collective-permute-start | bytes 294920 | tf_op jit(solution)/shard_map/ppermute | solution.py:447
  111.6 18.4 %collective-permute-start.21 = (bf16[2,96,3,512]{3,1,2,0:T(8,128)(2,1)}, bf16[2,96,3,512]{3,1,2,0:T(8,128)(2,1)}, u32[]{:S(2)}, u32[]{:S(2)}) collective-permute-start(bf16[2,96,3,512]{3,1,2,0:T(8,128)(2,1)} %pad_maximum_fusion.17), channel_id=1, source_target_pairs={{0,1},{1,0},{2,3},{3,2},{4,5},{5,4},{6,7},{7,6},{8,9},{9,8},{10,11... | collective-permute-start | bytes 1769480 | tf_op jit(solution)/shard_map/ppermute | solution.py:447
  136.2 175.5 %reduce-scatter.3.cloned.1.call-start = ((), (), s32[]{:S(2)}) async-start(), calls=%async_computation.6 | async-start | bytes 10616832 | tf_op jit(solution)/shard_map/reduce_scatter | solution.py:787
  138.1 43.6 %collective-permute-start = (bf16[256,768]{1,0:T(8,128)(2,1)}, bf16[256,768]{1,0:T(8,128)(2,1)S(1)}, u32[]{:S(2)}, u32[]{:S(2)}) collective-permute-start(bf16[256,768]{1,0:T(8,128)(2,1)} %dynamic-slice_bitcast_fusion.9), channel_id=1, source_target_pairs={{0,4},{4,0},{8,12},{12,8},{16,20},{20,16},{24,28},{28,24},{1,5},{5... | collective-permute-start | bytes 1179656 | tf_op jit(solution)/shard_map/ppermute | solution.py:445
  144.3 8.7 %collective-permute-start.15 = (bf16[256,384]{1,0:T(8,128)(2,1)S(1)}, bf16[256,384]{1,0:T(8,128)(2,1)S(1)}, u32[]{:S(2)}, u32[]{:S(2)}) collective-permute-start(bf16[256,384]{1,0:T(8,128)(2,1)S(1)} %get-tuple-element.340), channel_id=1, source_target_pairs={{0,4},{4,0},{8,12},{12,8},{16,20},{20,16},{24,28},{28,24},{1,5},{5... | collective-permute-start | bytes 589832 | tf_op jit(solution)/shard_map/ppermute | solution.py:445
  144.5 8.5 %collective-permute-start.13 = (bf16[256,384]{1,0:T(8,128)(2,1)S(1)}, bf16[256,384]{1,0:T(8,128)(2,1)S(1)}, u32[]{:S(2)}, u32[]{:S(2)}) collective-permute-start(bf16[256,384]{1,0:T(8,128)(2,1)S(1)} %get-tuple-element.340), channel_id=1, source_target_pairs={{0,5},{1,4},{2,7},{3,6},{4,1},{5,0},{6,3},{7,2},{8,13},{9,12},{10,... | collective-permute-start | bytes 589832 | tf_op jit(solution)/shard_map/ppermute | solution.py:453
  145.8 10.1 %collective-permute-start.14 = (bf16[256,384]{1,0:T(8,128)(2,1)S(1)}, bf16[256,384]{1,0:T(8,128)(2,1)S(1)}, u32[]{:S(2)}, u32[]{:S(2)}) collective-permute-start(bf16[256,384]{1,0:T(8,128)(2,1)S(1)} %get-tuple-element.341), channel_id=1, source_target_pairs={{0,1},{1,0},{2,3},{3,2},{4,5},{5,4},{6,7},{7,6},{8,9},{9,8},{10,11... | collective-permute-start | bytes 589832 | tf_op jit(solution)/shard_map/ppermute | solution.py:447
  183.5 8.8 %collective-permute-start.19 = (bf16[272,384]{1,0:T(8,128)(2,1)S(1)}, bf16[272,384]{1,0:T(8,128)(2,1)S(1)}, u32[]{:S(2)}, u32[]{:S(2)}) collective-permute-start(bf16[272,384]{1,0:T(8,128)(2,1)S(1)} %get-tuple-element.293), channel_id=1, source_target_pairs={{0,1},{1,0},{2,3},{3,2},{4,5},{5,4},{6,7},{7,6},{8,9},{9,8},{10,11... | collective-permute-start | bytes 626696 | tf_op jit(solution)/shard_map/ppermute | solution.py:447
  222.8 188.8 %reduce-scatter.5.cloned.1.call-start = ((), (), s32[]{:S(2)}) async-start(), calls=%async_computation.7 | async-start | bytes 1474560 | tf_op jit(solution)/shard_map/reduce_scatter | solution.py:840
  228.5 15.8 %collective-permute-start.26 = (bf16[288,384]{1,0:T(8,128)(2,1)S(1)}, bf16[288,384]{1,0:T(8,128)(2,1)S(1)}, u32[]{:S(2)}, u32[]{:S(2)}) collective-permute-start(bf16[288,384]{1,0:T(8,128)(2,1)S(1)} %pad_maximum_fusion.31), channel_id=1, source_target_pairs={{0,4},{4,0},{8,12},{12,8},{16,20},{20,16},{24,28},{28,24},{1,5},{5... | collective-permute-start | bytes 663560 | tf_op jit(solution)/shard_map/ppermute | solution.py:445
  228.8 15.5 %collective-permute-start.24 = (bf16[288,384]{1,0:T(8,128)(2,1)S(1)}, bf16[288,384]{1,0:T(8,128)(2,1)S(1)}, u32[]{:S(2)}, u32[]{:S(2)}) collective-permute-start(bf16[288,384]{1,0:T(8,128)(2,1)S(1)} %pad_maximum_fusion.31), channel_id=1, source_target_pairs={{0,5},{1,4},{2,7},{3,6},{4,1},{5,0},{6,3},{7,2},{8,13},{9,12},{10,... | collective-permute-start | bytes 663560 | tf_op jit(solution)/shard_map/ppermute | solution.py:453
  236.0 11.5 %collective-permute-start.22 = (bf16[256,768]{1,0:T(8,128)(2,1)}, bf16[256,768]{1,0:T(8,128)(2,1)}, u32[]{:S(2)}, u32[]{:S(2)}) collective-permute-start(bf16[256,768]{1,0:T(8,128)(2,1)} %fusion.61), channel_id=1, source_target_pairs={{0,4},{4,0},{8,12},{12,8},{16,20},{20,16},{24,28},{28,24},{1,5},{5... | collective-permute-start | bytes 1179656 | tf_op jit(solution)/shard_map/ppermute | solution.py:445
  248.7 28.1 %collective-permute-start.23 = (bf16[512,768]{1,0:T(8,128)(2,1)S(1)}, bf16[512,768]{1,0:T(8,128)(2,1)S(1)}, u32[]{:S(2)}, u32[]{:S(2)}) collective-permute-start(bf16[512,768]{1,0:T(8,128)(2,1)S(1)} %pad_maximum_fusion.13), channel_id=1, source_target_pairs={{0,2},{1,3},{6,4},{7,5},{8,10},{9,11},{14,12},{15,13},{16,18},{17,... | collective-permute-start | bytes 2359304 | tf_op jit(solution)/shard_map/ppermute | solution.py:761
  282.8 10.0 %collective-permute-start.28 = (bf16[256,384]{1,0:T(8,128)(2,1)S(1)}, bf16[256,384]{1,0:T(8,128)(2,1)S(1)}, u32[]{:S(2)}, u32[]{:S(2)}) collective-permute-start(bf16[256,384]{1,0:T(8,128)(2,1)S(1)} %get-tuple-element.299), channel_id=1, source_target_pairs={{0,5},{1,4},{2,7},{3,6},{4,1},{5,0},{6,3},{7,2},{8,13},{9,12},{10,... | collective-permute-start | bytes 589832 | tf_op jit(solution)/shard_map/ppermute | solution.py:453
  283.8 9.0 %collective-permute-start.27 = (bf16[256,384]{1,0:T(8,128)(2,1)S(1)}, bf16[256,384]{1,0:T(8,128)(2,1)S(1)}, u32[]{:S(2)}, u32[]{:S(2)}) collective-permute-start(bf16[256,384]{1,0:T(8,128)(2,1)S(1)} %get-tuple-element.300), channel_id=1, source_target_pairs={{0,4},{4,0},{8,12},{12,8},{16,20},{20,16},{24,28},{28,24},{1,5},{5... | collective-permute-start | bytes 589832 | tf_op jit(solution)/shard_map/ppermute | solution.py:445
  289.8 19.5 %collective-permute-start.38 = (bf16[1,4,96,768]{3,2,1,0:T(8,128)(2,1)S(1)}, bf16[1,4,96,768]{3,2,1,0:T(8,128)(2,1)S(1)}, u32[]{:S(2)}, u32[]{:S(2)}) collective-permute-start(bf16[1,4,96,768]{3,2,1,0:T(8,128)(2,1)S(1)} %dynamic-slice_bitcast_fusion.5), channel_id=1, source_target_pairs={{0,4},{4,0},{8,12},{12,8},{16,20},{20,16},{24,28},{28,24},{1,5},{5... | collective-permute-start | bytes 1769480 | tf_op jit(solution)/shard_map/ppermute | solution.py:445
  297.8 12.5 %collective-permute-start.37 = (bf16[2,4,96,768]{3,2,1,0:T(8,128)(2,1)S(1)}, bf16[2,4,96,768]{3,2,1,0:T(8,128)(2,1)S(1)}, u32[]{:S(2)}, u32[]{:S(2)}) collective-permute-start(bf16[2,4,96,768]{3,2,1,0:T(8,128)(2,1)S(1)} %fusion.66), channel_id=1, source_target_pairs={{0,4},{4,0},{8,12},{12,8},{16,20},{20,16},{24,28},{28,24},{1,5},{5... | collective-permute-start | bytes 3538952 | tf_op jit(solution)/shard_map/ppermute | solution.py:445
  304.1 42.9 %collective-permute-start.46 = (bf16[2,512,768]{2,1,0:T(8,128)(2,1)}, bf16[2,512,768]{2,1,0:T(8,128)(2,1)}, u32[]{:S(2)}, u32[]{:S(2)}) collective-permute-start(bf16[2,512,768]{2,1,0:T(8,128)(2,1)} %fusion.39), channel_id=1, source_target_pairs={{0,4},{4,0},{8,12},{12,8},{16,20},{20,16},{24,28},{28,24},{1,5},{5... | collective-permute-start | bytes 4718600 | tf_op jit(solution)/shard_map/ppermute | solution.py:445
  326.4 9.2 %collective-permute-start.34 = (bf16[2,256,768]{2,1,0:T(8,128)(2,1)}, bf16[2,256,768]{2,1,0:T(8,128)(2,1)}, u32[]{:S(2)}, u32[]{:S(2)}) collective-permute-start(bf16[2,256,768]{2,1,0:T(8,128)(2,1)} %fusion.88), channel_id=1, source_target_pairs={{0,4},{4,0},{8,12},{12,8},{16,20},{20,16},{24,28},{28,24},{1,5},{5... | collective-permute-start | bytes 2359304 | tf_op jit(solution)/shard_map/ppermute | solution.py:445
  339.1 23.2 %collective-permute-start.35 = (bf16[256,768]{1,0:T(8,128)(2,1)S(1)}, bf16[256,768]{1,0:T(8,128)(2,1)S(1)}, u32[]{:S(2)}, u32[]{:S(2)}) collective-permute-start(bf16[256,768]{1,0:T(8,128)(2,1)S(1)} %fusion.124), channel_id=1, source_target_pairs={{0,1},{1,0},{2,3},{3,2},{4,5},{5,4},{6,7},{7,6},{8,9},{9,8},{10,11... | collective-permute-start | bytes 1179656 | tf_op jit(solution)/shard_map/ppermute | solution.py:447
  343.5 32.9 %collective-permute-start.39 = (bf16[4,96,768]{2,1,0:T(8,128)(2,1)}, bf16[4,96,768]{2,1,0:T(8,128)(2,1)}, u32[]{:S(2)}, u32[]{:S(2)}) collective-permute-start(bf16[4,96,768]{2,1,0:T(8,128)(2,1)} %get-tuple-element.236), channel_id=1, source_target_pairs={{0,8},{4,12},{8,0},{12,4},{16,24},{20,28},{24,16},{28,20},{1,9},{5... | collective-permute-start | bytes 1769480 | tf_op jit(solution)/shard_map/ppermute | solution.py:445
  344.6 35.6 %collective-permute-start.41 = (bf16[4,96,768]{2,1,0:T(8,128)(2,1)}, bf16[4,96,768]{2,1,0:T(8,128)(2,1)}, u32[]{:S(2)}, u32[]{:S(2)}) collective-permute-start(bf16[4,96,768]{2,1,0:T(8,128)(2,1)} %get-tuple-element.237), channel_id=1, source_target_pairs={{0,24},{4,28},{8,16},{12,20},{16,8},{20,12},{24,0},{28,4},{1,25},{... | collective-permute-start | bytes 1769480 | tf_op jit(solution)/shard_map/ppermute | solution.py:445
  346.8 34.8 %collective-permute-start.40 = (bf16[4,96,768]{2,1,0:T(8,128)(2,1)}, bf16[4,96,768]{2,1,0:T(8,128)(2,1)}, u32[]{:S(2)}, u32[]{:S(2)}) collective-permute-start(bf16[4,96,768]{2,1,0:T(8,128)(2,1)} %get-tuple-element.238), channel_id=1, source_target_pairs={{0,16},{4,20},{8,24},{12,28},{16,0},{20,4},{24,8},{28,12},{1,17},{... | collective-permute-start | bytes 1769480 | tf_op jit(solution)/shard_map/ppermute | solution.py:445
  371.6 13.7 %collective-permute-start.42 = (bf16[1,4,96,768]{3,2,1,0:T(8,128)(2,1)S(1)}, bf16[1,4,96,768]{3,2,1,0:T(8,128)(2,1)S(1)}, u32[]{:S(2)}, u32[]{:S(2)}) collective-permute-start(bf16[1,4,96,768]{3,2,1,0:T(8,128)(2,1)S(1)} %dynamic-slice_bitcast_fusion.1), channel_id=1, source_target_pairs={{0,4},{4,0},{8,12},{12,8},{16,20},{20,16},{24,28},{28,24},{1,5},{5... | collective-permute-start | bytes 1769480 | tf_op jit(solution)/shard_map/ppermute | solution.py:445
  372.3 13.0 %collective-permute-start.43 = (bf16[4,96,768]{2,1,0:T(8,128)(2,1)S(1)}, bf16[4,96,768]{2,1,0:T(8,128)(2,1)S(1)}, u32[]{:S(2)}, u32[]{:S(2)}) collective-permute-start(bf16[4,96,768]{2,1,0:T(8,128)(2,1)S(1)} %dynamic-slice_bitcast_fusion), channel_id=1, source_target_pairs={{0,4},{4,0},{8,12},{12,8},{16,20},{20,16},{24,28},{28,24},{1,5},{5... | collective-permute-start | bytes 1769480 | tf_op jit(solution)/shard_map/ppermute | solution.py:445
  376.4 55.8 %collective-permute-start.47 = (bf16[2,512,768]{2,1,0:T(8,128)(2,1)}, bf16[2,512,768]{2,1,0:T(8,128)(2,1)}, u32[]{:S(2)}, u32[]{:S(2)}) collective-permute-start(bf16[2,512,768]{2,1,0:T(8,128)(2,1)} %fusion.9), channel_id=1, source_target_pairs={{2,4},{3,5},{4,2},{5,3},{10,12},{11,13},{12,10},{13,11},{18,20},{1... | collective-permute-start | bytes 4718600 | tf_op jit(solution)/shard_map/ppermute | solution.py:604
  380.2 33.9 %collective-permute-start.44 = (bf16[512,768]{1,0:T(8,128)(2,1)}, bf16[512,768]{1,0:T(8,128)(2,1)}, u32[]{:S(2)}, u32[]{:S(2)}) collective-permute-start(bf16[512,768]{1,0:T(8,128)(2,1)} %pad_maximum_fusion.14), channel_id=1, source_target_pairs={{0,2},{1,3},{6,4},{7,5},{8,10},{9,11},{14,12},{15,13},{16,18},{17,... | collective-permute-start | bytes 2359304 | tf_op jit(solution)/shard_map/ppermute | solution.py:761
  385.9 11.6 %collective-permute-start.48 = (bf16[3,96,768]{2,1,0:T(8,128)(2,1)S(1)}, bf16[3,96,768]{2,1,0:T(8,128)(2,1)S(1)}, u32[]{:S(2)}, u32[]{:S(2)}) collective-permute-start(bf16[3,96,768]{2,1,0:T(8,128)(2,1)S(1)} %get-tuple-element.250), channel_id=1, source_target_pairs={{0,8},{4,12},{8,0},{12,4},{16,24},{20,28},{24,16},{28,20},{1,9},{5... | collective-permute-start | bytes 1327112 | tf_op jit(solution)/shard_map/ppermute | solution.py:445
  386.6 21.3 %collective-permute-start.50 = (bf16[3,96,768]{2,1,0:T(8,128)(2,1)S(1)}, bf16[3,96,768]{2,1,0:T(8,128)(2,1)S(1)}, u32[]{:S(2)}, u32[]{:S(2)}) collective-permute-start(bf16[3,96,768]{2,1,0:T(8,128)(2,1)S(1)} %get-tuple-element.251), channel_id=1, source_target_pairs={{0,24},{4,28},{8,16},{12,20},{16,8},{20,12},{24,0},{28,4},{1,25},{... | collective-permute-start | bytes 1327112 | tf_op jit(solution)/shard_map/ppermute | solution.py:445
  388.9 21.5 %collective-permute-start.49 = (bf16[3,96,768]{2,1,0:T(8,128)(2,1)S(1)}, bf16[3,96,768]{2,1,0:T(8,128)(2,1)S(1)}, u32[]{:S(2)}, u32[]{:S(2)}) collective-permute-start(bf16[3,96,768]{2,1,0:T(8,128)(2,1)S(1)} %get-tuple-element.252), channel_id=1, source_target_pairs={{0,16},{4,20},{8,24},{12,28},{16,0},{20,4},{24,8},{28,12},{1,17},{... | collective-permute-start | bytes 1327112 | tf_op jit(solution)/shard_map/ppermute | solution.py:445
  397.5 119.8 %collective-permute-start.30 = (bf16[512,768]{1,0:T(8,128)(2,1)}, bf16[512,768]{1,0:T(8,128)(2,1)}, u32[]{:S(2)}, u32[]{:S(2)}) collective-permute-start(bf16[512,768]{1,0:T(8,128)(2,1)} %broadcast_select_fusion.3), channel_id=1, source_target_pairs={{0,1},{1,0},{2,3},{3,2},{4,5},{5,4},{6,7},{7,6},{8,9},{9,8},{10,11... | collective-permute-start | bytes 2359304 | tf_op jit(solution)/shard_map/ppermute | solution.py:447
  417.6 82.2 %collective-permute-start.45 = (bf16[512,768]{1,0:T(8,128)(2,1)}, bf16[512,768]{1,0:T(8,128)(2,1)}, u32[]{:S(2)}, u32[]{:S(2)}) collective-permute-start(bf16[512,768]{1,0:T(8,128)(2,1)} %select_select_fusion), channel_id=1, source_target_pairs={{0,1},{1,0},{2,3},{3,2},{4,5},{5,4},{6,7},{7,6},{8,9},{9,8},{10,11... | collective-permute-start | bytes 2359304 | tf_op jit(solution)/shard_map/ppermute | solution.py:447
  444.9 58.8 %all-to-all-start.1 = ((bf16[8,128,768]{2,1,0:T(8,128)(2,1)}), bf16[8,128,768]{2,1,0:T(8,128)(2,1)}, u32[]{:S(2)}, u32[]{:S(2)}) async-start(bf16[8,128,768]{2,1,0:T(8,128)(2,1)} %bitcast.418), calls=%async_computation.3 | async-start | bytes 3145728 | tf_op jit(solution)/shard_map/all_to_all | solution.py:886
  449.6 12.5 %collective-permute-start.51 = (bf16[96,768]{1,0:T(8,128)(2,1)}, bf16[96,768]{1,0:T(8,128)(2,1)}, u32[]{:S(2)}, u32[]{:S(2)}) collective-permute-start(bf16[96,768]{1,0:T(8,128)(2,1)} %fusion.162), channel_id=1, source_target_pairs={{0,2},{1,3},{2,0},{3,1},{4,6},{5,7},{6,4},{7,5},{8,10},{9,11},{10,... | collective-permute-start | bytes 442376 | tf_op jit(solution)/shard_map/ppermute | solution.py:447
  456.9 15.8 %collective-permute-start.52 = (bf16[2,6,96,192]{2,3,1,0:T(8,128)(2,1)}, bf16[2,6,96,192]{2,3,1,0:T(8,128)(2,1)}, u32[]{:S(2)}, u32[]{:S(2)}) collective-permute-start(bf16[2,6,96,192]{2,3,1,0:T(8,128)(2,1)} %bitcast.445), channel_id=1, source_target_pairs={{0,1},{1,0},{2,3},{3,2},{4,5},{5,4},{6,7},{7,6},{8,9},{9,8},{10,11... | collective-permute-start | bytes 1327112 | tf_op jit(solution)/shard_map/ppermute | solution.py:447
  474.3 15.4 %collective-permute-start.53 = (bf16[6,96,192]{1,2,0:T(8,128)(2,1)S(1)}, bf16[6,96,192]{1,2,0:T(8,128)(2,1)S(1)}, u32[]{:S(2)}, u32[]{:S(2)}) collective-permute-start(bf16[6,96,192]{1,2,0:T(8,128)(2,1)S(1)} %fusion.144), channel_id=1, source_target_pairs={{0,2},{1,3},{2,0},{3,1},{4,6},{5,7},{6,4},{7,5},{8,10},{9,11},{10,... | collective-permute-start | bytes 663560 | tf_op jit(solution)/shard_map/ppermute | solution.py:447
  518.9 8.2 %collective-permute-start.59 = (f32[2,2,14]{2,1,0:T(2,128)S(1)}, f32[2,2,14]{2,1,0:T(2,128)S(1)}, u32[]{:S(2)}, u32[]{:S(2)}) collective-permute-start(f32[2,2,14]{2,1,0:T(2,128)S(1)} %pad_maximum_fusion.36), channel_id=1, source_target_pairs={{0,1},{1,0},{2,3},{3,2},{4,5},{5,4},{6,7},{7,6},{8,9},{9,8},{10,11... | collective-permute-start | bytes 680 | tf_op jit(solution)/shard_map/ppermute | solution.py:447
  (128 other events, 804.8 us)
Sparse Core Ops, SparseCore 0:
  52.2 51.4 all-gather.2
  136.3 59.7 all-gather.4
  222.9 77.1 reduce-scatter.2
  329.2 36.8 reduce-scatter.4

commit v4 on v3

--- a/solution.py
+++ b/solution.py
@@ -783,7 +783,7 @@
     pieces = member_pieces(
         lambda d: jnp.concatenate([by_core(grad_cross, d), tails[d & 1]], axis=0)
     )
-    second_part = hidden_grads(after(hidden_three, grad_cross), after(act_low, grad_cross), grad_gate, grad_up, activated_low)
+    second_part = hidden_grads(after(hidden_three, pieces[1]), after(act_low, pieces[1]), grad_gate, grad_up, activated_low)
     second_grads = lax.psum_scatter(second_part, "dp", scatter_dimension=0, tiled=True)
     got = after(jnp.stack(in_order(pieces, member)), second_part)
     grads = mm(sorter, got[:, 0:row_count].reshape(tok_rows, half_width)).astype(bf16)

time: 549 us -> 541 us (0.985)
    unnamed x226 -> x234, local copies, waits for them, and re-layouts: 11.5 us -> 9.84 us
where the time goes in v4:
time: 541 us; the launch traced here: 533 us
  waiting for transfers between devices  136 us (25%)
  starting transfers between devices  83.1 us (15%)
  other arithmetic  81.3 us (15%)
  Pallas kernels  69.8 us (13%)
  local copies, waits for them, and re-layouts  59.3 us (11%)
  matrix products  57.4 us (11%)
  between operations  46 us (9%)
    ppermute x18, waiting for transfers between devices, send(): lax.ppermute(array, 'head', [(s, s ^ head_bits) for s in range(head_count)])  65 us
    dot_general x27, matrix products, mm(): return lax.dot_general(a, b, dims, preferred_element_type=jnp.float32)  55 us
    ppermute x18, starting transfers between devices, send(): lax.ppermute(array, 'head', [(s, s ^ head_bits) for s in range(head_count)])  38.1 us
    pallas_call x1, Pallas kernels, cross_backward(): pl.pallas_call(cross_backward_kernel, grid=(groups,), in_specs=[pl.BlockS...  26.8 us
    ppermute x32, waiting for transfers between devices, send(): lax.ppermute(array, 'dp', [(s, s ^ dp_bits) for s in range(dp_count)])  22.9 us
    ppermute x2, waiting for transfers between devices, across(): return jnp.where(here, array, lax.ppermute(array, ('dp', 'head'), pairs))  22.6 us
    pallas_call x1, Pallas kernels, cross_forward(): pl.pallas_call(cross_forward_kernel, grid=(groups,), in_specs=[pl.BlockSp...  20.4 us
    ppermute x32, starting transfers between devices, send(): lax.ppermute(array, 'dp', [(s, s ^ dp_bits) for s in range(dp_count)])  19.5 us
  transfers between devices with their start and end apart: 66, of which 26 were waited for; matrix products, arithmetic and copies ran while one was open for 30% of the time, Pallas kernels for 11%

profile of v4, /device:TPU:18, one launch (start us, length us, event | category | flops | bytes accessed | tf_op | source)
XLA Modules:
  0.0 532.9 jit_solution(6134529669846918136)
XLA Ops:
  7.2 4.4 all-to-all-start
  13.6 17.6 %all-to-all-done = bf16[8,128,768]{2,1,0:T(8,128)(2,1)S(1)} async-done(((bf16[8,128,768]{2,1,0:T(8,128)(2,1)}), bf16[8,128,768]{2,1,0:T(8,128)(2,1)S(1)}, u32[]{:S(2)}, u32[]{:S(2)}) %all-to-all-start) | async-done | bytes 1572896 | tf_op jit(solution)/shard_map/all_to_all | solution.py:606
  34.4 2.4 collective-permute-start.12
  36.8 11.4 %collective-permute-done.12 = bf16[2,96,960]{1,2,0:T(8,128)(2,1)S(1)} collective-permute-done((bf16[2,96,960]{1,2,0:T(8,128)(2,1)S(1)}, bf16[2,96,960]{1,2,0:T(8,128)(2,1)S(1)}, u32[]{:S(2)}, u32[]{:S(2)}) %collective-permute-start.12) | collective-permute-done | bytes 368672 | tf_op jit(solution)/shard_map/ppermute | solution.py:447
  71.6 20.4 %collective-permute-done.3 = bf16[2,512,768]{2,1,0:T(8,128)(2,1)} collective-permute-done((bf16[2,512,768]{2,1,0:T(8,128)(2,1)S(1)}, bf16[2,512,768]{2,1,0:T(8,128)(2,1)}, u32[]{:S(2)}, u32[]{:S(2)}) %collective-permute-start.3) | collective-permute-done | bytes 1572896 | tf_op jit(solution)/shard_map/ppermute | solution.py:604
  98.3 5.8 %self_forward.1 = (bf16[1024,256]{1,0:T(8,128)(2,1)S(1)}, f32[8,1024]{1,0:T(8,128)S(1)}) custom-call(bf16[1024,768]{1,0:T(8,128)(2,1)S(1)} %convolution_convert_fusion.1.qkv_ref, s32[1,1024]{1,0:T(1,128)S(1)} %bitcast.410), custom_call_target="tpu_custom_call" | custom-call | flops 6000000000 | bytes 2097152 | tf_op jit(solution)/shard_map/self_forward/pallas_call | solution.py:104
  106.1 4.4 collective-permute-start.11
  111.6 2.4 collective-permute-start.21
  121.5 8.5 %collective-permute-done.21 = bf16[2,96,3,512]{3,1,2,0:T(8,128)(2,1)} collective-permute-done((bf16[2,96,3,512]{3,1,2,0:T(8,128)(2,1)}, bf16[2,96,3,512]{3,1,2,0:T(8,128)(2,1)}, u32[]{:S(2)}, u32[]{:S(2)}) %collective-permute-start.21) | collective-permute-done | bytes 589856 | tf_op jit(solution)/shard_map/ppermute | solution.py:447
  133.4 2.8 reshape.698
  141.6 2.7 convolution_convert_fusion.7
  148.6 4.4 convolution_convert_fusion.key_ref.value_ref
  153.1 2.9 collective-permute-done.14
  157.3 20.4 %cross_forward.1 = (bf16[1024,384]{1,0:T(8,128)(2,1)S(1)}, f32[3,8,1024]{2,1,0:T(8,128)S(1)}) custom-call(s32[1]{0:T(128)} %slice.492.split_ref, bf16[1024,384]{1,0:T(8,128)(2,1)S(1)} %fusion.53.query_ref, bf16[2048,768]{1,0:T(8,128)(2,1)} %convolution_convert_fusion.key_ref.value_ref, bf16[2048,768]{1,0:T(8,128)(2,1)} %convolution_convert_fusion.key_ref.value_ref), custom_call_target="tpu_custom_call" | custom-call | flops 28000000000 | bytes 3145728 | tf_op jit(solution)/shard_map/cross_forward/pallas_call | solution.py:250
  184.2 3.0 collective-permute-done.18
  187.7 4.6 collective-permute-done.19
  196.1 3.1 fusion.12
  199.2 3.5 fusion.16
  202.7 2.9 multiply_convert_fusion.2
  215.0 8.9 %hidden_grads.1 = bf16[768,6144]{1,0:T(8,128)(2,1)} custom-call(bf16[256,768]{1,0:T(8,128)(2,1)S(1)} %broadcast_select_fusion.15.rows_ref, bf16[256,768]{1,0:T(8,128)(2,1)S(1)} %broadcast_select_fusion.14.grad_ref, bf16[256,2048]{1,0:T(8,128)(2,1)S(1)} %get-tuple-element.234.gate_ref, bf16[256,2048]{1,0:T(8,128)(2,1)S(1)} %get-tuple-element.233.up_ref, ...), custom_call_target="tpu_custom_call" | custom-call | flops 2415919104 | bytes 9437184 | tf_op jit(solution)/shard_map/hidden_grads/pallas_call | solution.py:401
  227.7 3.8 fusion.61
  236.9 2.9 collective-permute-done.26
  245.4 26.8 %cross_backward.1 = (bf16[1024,384]{1,0:T(8,128)(2,1)S(1)}, bf16[2048,384]{1,0:T(8,128)(2,1)S(1)}, bf16[2048,384]{1,0:T(8,128)(2,1)}) custom-call(s32[1]{0:T(128)} %slice.492.split_ref, bf16[1024,384]{1,0:T(8,128)(2,1)S(1)} %fusion.53.query_ref, bf16[1024,384]{1,0:T(8,128)(2,1)S(1)} %fusion.54.grad_ref, f32[3,8,1024]{2,1,0:T(8,128)S(1)} %maximum_maximum_fusion.stats_ref, ...), custom_call_target="tpu_custom_call" | custom-call | flops 28000000000 | bytes 6291456 | tf_op jit(solution)/shard_map/cross_backward/pallas_call | solution.py:343
  278.3 2.8 collective-permute-start.28
  281.2 2.7 fusion.47
  283.9 2.7 fusion.37
  300.8 2.8 collective-permute-done.32
  309.9 7.8 %self_backward.1 = bf16[1024,768]{1,0:T(8,128)(2,1)S(1)} custom-call(bf16[1024,768]{1,0:T(8,128)(2,1)} %copy-done, bf16[1024,256]{1,0:T(8,128)(2,1)S(1)} %fusion.121.grad_ref, bf16[1024,256]{1,0:T(8,128)(2,1)S(1)} %get-tuple-element.35.out_ref, f32[8,1024]{1,0:T(8,128)S(1)} %get-tuple-element.39.sums_ref, s32[1,1024]{1,0:T(1,128)S(1)} %bitcast.411), custom_call_target="tpu_custom_call" | custom-call | flops 8000000000 | bytes 5242880 | tf_op jit(solution)/shard_map/self_backward/pallas_call | solution.py:176
  326.4 3.3 fusion.48
  342.9 3.1 fusion.9
  346.0 11.2 %collective-permute-done.35 = bf16[256,768]{1,0:T(8,128)(2,1)S(1)} collective-permute-done((bf16[256,768]{1,0:T(8,128)(2,1)S(1)}, bf16[256,768]{1,0:T(8,128)(2,1)S(1)}, u32[]{:S(2)}, u32[]{:S(2)}) %collective-permute-start.35) | collective-permute-done | bytes 393248 | tf_op jit(solution)/shard_map/ppermute | solution.py:447
  370.8 3.6 collective-permute-start.47
  388.2 3.4 collective-permute-done.48
  391.6 11.6 %collective-permute-done.50 = bf16[3,96,768]{2,1,0:T(8,128)(2,1)S(1)} collective-permute-done((bf16[3,96,768]{2,1,0:T(8,128)(2,1)S(1)}, bf16[3,96,768]{2,1,0:T(8,128)(2,1)S(1)}, u32[]{:S(2)}, u32[]{:S(2)}) %collective-permute-start.50) | collective-permute-done | bytes 442400 | tf_op jit(solution)/shard_map/ppermute | solution.py:445
  403.1 2.4 collective-permute-done.49
  412.7 11.5 %collective-permute-start.45 = (bf16[512,768]{1,0:T(8,128)(2,1)}, bf16[512,768]{1,0:T(8,128)(2,1)}, u32[]{:S(2)}, u32[]{:S(2)}) collective-permute-start(bf16[512,768]{1,0:T(8,128)(2,1)} %select_select_fusion), channel_id=1, source_target_pairs={{0,1},{1,0},{2,3},{3,2},{4,5},{5,4},{6,7},{7,6},{8,9},{9,8},{10,11... | collective-permute-start | bytes 2359304 | tf_op jit(solution)/shard_map/ppermute | solution.py:447
  439.1 4.7 all-to-all-start.1
  445.3 2.7 copy.166
  452.2 3.0 multiply_reduce_fusion.12
  455.2 2.4 multiply_reduce_fusion.15
  458.9 7.6 %collective-permute-done.52 = bf16[2,6,96,192]{2,3,1,0:T(8,128)(2,1)} collective-permute-done((bf16[2,6,96,192]{2,3,1,0:T(8,128)(2,1)}, bf16[2,6,96,192]{2,3,1,0:T(8,128)(2,1)}, u32[]{:S(2)}, u32[]{:S(2)}) %collective-permute-start.52) | collective-permute-done | bytes 442400 | tf_op jit(solution)/shard_map/ppermute | solution.py:447
  468.2 3.0 collective-permute-start.53
  471.2 12.6 %collective-permute-done.53 = bf16[6,96,192]{1,2,0:T(8,128)(2,1)S(1)} collective-permute-done((bf16[6,96,192]{1,2,0:T(8,128)(2,1)S(1)}, bf16[6,96,192]{1,2,0:T(8,128)(2,1)S(1)}, u32[]{:S(2)}, u32[]{:S(2)}) %collective-permute-start.53) | collective-permute-done | bytes 221216 | tf_op jit(solution)/shard_map/ppermute | solution.py:447
  488.1 2.8 multiply_reduce_fusion.10
  503.7 2.8 collective-permute-done.55
  506.5 3.4 collective-permute-start.58
  511.5 2.6 collective-permute-start.59
  516.0 3.5 convert.51
  (602 shorter events, 196.9 us)
Async XLA Ops:
  7.2 23.9 %all-to-all-start = ((bf16[8,128,768]{2,1,0:T(8,128)(2,1)}), bf16[8,128,768]{2,1,0:T(8,128)(2,1)S(1)}, u32[]{:S(2)}, u32[]{:S(2)}) async-start(bf16[8,128,768]{2,1,0:T(8,128)(2,1)} %bitcast.435), calls=%async_computation | async-start | bytes 3145728 | tf_op jit(solution)/shard_map/all_to_all | solution.py:606
  11.6 105.7 %all-gather.3.cloned.1.call-start = ((), (), s32[]{:S(2)}) async-start(), calls=%async_computation.4 | async-start | bytes 6635520 | tf_op jit(solution)/shard_map/all_gather | solution.py:634
  13.2 19.9 %collective-permute-start.4 = (bf16[96,1536]{0,1:T(8,128)(2,1)}, bf16[96,1536]{0,1:T(8,128)(2,1)}, u32[]{:S(2)}, u32[]{:S(2)}) collective-permute-start(bf16[96,1536]{0,1:T(8,128)(2,1)} %pad_maximum_fusion.22), channel_id=1, source_target_pairs={{0,2},{1,3},{2,0},{3,1},{4,6},{5,7},{6,4},{7,5},{8,10},{9,11},{10,... | collective-permute-start | bytes 884744 | tf_op jit(solution)/shard_map/ppermute | solution.py:447
  34.4 13.9 %collective-permute-start.12 = (bf16[2,96,960]{1,2,0:T(8,128)(2,1)S(1)}, bf16[2,96,960]{1,2,0:T(8,128)(2,1)S(1)}, u32[]{:S(2)}, u32[]{:S(2)}) collective-permute-start(bf16[2,96,960]{1,2,0:T(8,128)(2,1)S(1)} %pad_maximum_fusion.19), channel_id=1, source_target_pairs={{0,1},{1,0},{2,3},{3,2},{4,5},{5,4},{6,7},{7,6},{8,9},{9,8},{10,11... | collective-permute-start | bytes 1105928 | tf_op jit(solution)/shard_map/ppermute | solution.py:447
  52.0 144.0 %all-gather.5.cloned.1.call-start = ((), (), s32[]{:S(2)}) async-start(), calls=%async_computation.5 | async-start | bytes 10616832 | tf_op jit(solution)/shard_map/all_gather | solution.py:684
  52.2 17.3 %collective-permute-start.2 = (bf16[1024,768]{1,0:T(8,128)(2,1)}, bf16[1024,768]{1,0:T(8,128)(2,1)}, u32[]{:S(2)}, u32[]{:S(2)}) collective-permute-start(bf16[1024,768]{1,0:T(8,128)(2,1)} %param.22), channel_id=1, source_target_pairs={{0,4},{4,0},{8,12},{12,8},{16,20},{20,16},{24,28},{28,24},{1,5},{5... | collective-permute-start | bytes 4718600 | tf_op jit(solution)/shard_map/ppermute | solution.py:445
  55.4 36.7 %collective-permute-start.3 = (bf16[2,512,768]{2,1,0:T(8,128)(2,1)S(1)}, bf16[2,512,768]{2,1,0:T(8,128)(2,1)}, u32[]{:S(2)}, u32[]{:S(2)}) collective-permute-start(bf16[2,512,768]{2,1,0:T(8,128)(2,1)S(1)} %bitcast.417), channel_id=1, source_target_pairs={{2,4},{3,5},{4,2},{5,3},{10,12},{11,13},{12,10},{13,11},{18,20},{1... | collective-permute-start | bytes 4718600 | tf_op jit(solution)/shard_map/ppermute | solution.py:604
  66.0 29.6 %collective-permute-start.8 = (bf16[192,640]{0,1:T(8,128)(2,1)S(1)}, bf16[192,640]{0,1:T(8,128)(2,1)S(1)}, u32[]{:S(2)}, u32[]{:S(2)}) collective-permute-start(bf16[192,640]{0,1:T(8,128)(2,1)S(1)} %maximum_select_fusion.9), channel_id=1, source_target_pairs={{0,8},{4,12},{8,0},{12,4},{16,24},{20,28},{24,16},{28,20},{1,9},{5... | collective-permute-start | bytes 737288 | tf_op jit(solution)/shard_map/ppermute | solution.py:445
  66.5 29.2 %collective-permute-start.7 = (bf16[192,640]{0,1:T(8,128)(2,1)S(1)}, bf16[192,640]{0,1:T(8,128)(2,1)S(1)}, u32[]{:S(2)}, u32[]{:S(2)}) collective-permute-start(bf16[192,640]{0,1:T(8,128)(2,1)S(1)} %maximum_select_fusion.9), channel_id=1, source_target_pairs={{0,16},{4,20},{8,24},{12,28},{16,0},{20,4},{24,8},{28,12},{1,17},{... | collective-permute-start | bytes 737288 | tf_op jit(solution)/shard_map/ppermute | solution.py:445
  68.1 27.5 %collective-permute-start.6 = (bf16[192,640]{0,1:T(8,128)(2,1)S(1)}, bf16[192,640]{0,1:T(8,128)(2,1)S(1)}, u32[]{:S(2)}, u32[]{:S(2)}) collective-permute-start(bf16[192,640]{0,1:T(8,128)(2,1)S(1)} %maximum_select_fusion.9), channel_id=1, source_target_pairs={{0,24},{4,28},{8,16},{12,20},{16,8},{20,12},{24,0},{28,4},{1,25},{... | collective-permute-start | bytes 737288 | tf_op jit(solution)/shard_map/ppermute | solution.py:445
  95.5 15.1 %collective-permute-start.20 = (bf16[96,3,512]{2,0,1:T(8,128)(2,1)S(1)}, bf16[96,3,512]{2,0,1:T(8,128)(2,1)S(1)}, u32[]{:S(2)}, u32[]{:S(2)}) collective-permute-start(bf16[96,3,512]{2,0,1:T(8,128)(2,1)S(1)} %broadcast_select_fusion.25), channel_id=1, source_target_pairs={{0,2},{1,3},{2,0},{3,1},{4,6},{5,7},{6,4},{7,5},{8,10},{9,11},{10,... | collective-permute-start | bytes 884744 | tf_op jit(solution)/shard_map/ppermute | solution.py:447
  106.1 9.9 %collective-permute-start.11 = (bf16[256,192]{1,0:T(8,128)(2,1)S(1)}, bf16[256,192]{1,0:T(8,128)(2,1)S(1)}, u32[]{:S(2)}, u32[]{:S(2)}) collective-permute-start(bf16[256,192]{1,0:T(8,128)(2,1)S(1)} %get-tuple-element.325), channel_id=1, source_target_pairs={{0,1},{1,0},{2,3},{3,2},{4,5},{5,4},{6,7},{7,6},{8,9},{9,8},{10,11... | collective-permute-start | bytes 294920 | tf_op jit(solution)/shard_map/ppermute | solution.py:447
  111.6 18.4 %collective-permute-start.21 = (bf16[2,96,3,512]{3,1,2,0:T(8,128)(2,1)}, bf16[2,96,3,512]{3,1,2,0:T(8,128)(2,1)}, u32[]{:S(2)}, u32[]{:S(2)}) collective-permute-start(bf16[2,96,3,512]{3,1,2,0:T(8,128)(2,1)} %pad_maximum_fusion.17), channel_id=1, source_target_pairs={{0,1},{1,0},{2,3},{3,2},{4,5},{5,4},{6,7},{7,6},{8,9},{9,8},{10,11... | collective-permute-start | bytes 1769480 | tf_op jit(solution)/shard_map/ppermute | solution.py:447
  136.2 171.0 %reduce-scatter.3.cloned.1.call-start = ((), (), s32[]{:S(2)}) async-start(), calls=%async_computation.6 | async-start | bytes 10616832 | tf_op jit(solution)/shard_map/reduce_scatter | solution.py:787
  138.1 43.6 %collective-permute-start = (bf16[256,768]{1,0:T(8,128)(2,1)}, bf16[256,768]{1,0:T(8,128)(2,1)S(1)}, u32[]{:S(2)}, u32[]{:S(2)}) collective-permute-start(bf16[256,768]{1,0:T(8,128)(2,1)} %dynamic-slice_bitcast_fusion.9), channel_id=1, source_target_pairs={{0,4},{4,0},{8,12},{12,8},{16,20},{20,16},{24,28},{28,24},{1,5},{5... | collective-permute-start | bytes 1179656 | tf_op jit(solution)/shard_map/ppermute | solution.py:445
  144.3 8.7 %collective-permute-start.15 = (bf16[256,384]{1,0:T(8,128)(2,1)S(1)}, bf16[256,384]{1,0:T(8,128)(2,1)S(1)}, u32[]{:S(2)}, u32[]{:S(2)}) collective-permute-start(bf16[256,384]{1,0:T(8,128)(2,1)S(1)} %get-tuple-element.340), channel_id=1, source_target_pairs={{0,4},{4,0},{8,12},{12,8},{16,20},{20,16},{24,28},{28,24},{1,5},{5... | collective-permute-start | bytes 589832 | tf_op jit(solution)/shard_map/ppermute | solution.py:445
  144.5 8.5 %collective-permute-start.13 = (bf16[256,384]{1,0:T(8,128)(2,1)S(1)}, bf16[256,384]{1,0:T(8,128)(2,1)S(1)}, u32[]{:S(2)}, u32[]{:S(2)}) collective-permute-start(bf16[256,384]{1,0:T(8,128)(2,1)S(1)} %get-tuple-element.340), channel_id=1, source_target_pairs={{0,5},{1,4},{2,7},{3,6},{4,1},{5,0},{6,3},{7,2},{8,13},{9,12},{10,... | collective-permute-start | bytes 589832 | tf_op jit(solution)/shard_map/ppermute | solution.py:453
  145.8 10.1 %collective-permute-start.14 = (bf16[256,384]{1,0:T(8,128)(2,1)S(1)}, bf16[256,384]{1,0:T(8,128)(2,1)S(1)}, u32[]{:S(2)}, u32[]{:S(2)}) collective-permute-start(bf16[256,384]{1,0:T(8,128)(2,1)S(1)} %get-tuple-element.341), channel_id=1, source_target_pairs={{0,1},{1,0},{2,3},{3,2},{4,5},{5,4},{6,7},{7,6},{8,9},{9,8},{10,11... | collective-permute-start | bytes 589832 | tf_op jit(solution)/shard_map/ppermute | solution.py:447
  183.5 8.8 %collective-permute-start.19 = (bf16[272,384]{1,0:T(8,128)(2,1)S(1)}, bf16[272,384]{1,0:T(8,128)(2,1)S(1)}, u32[]{:S(2)}, u32[]{:S(2)}) collective-permute-start(bf16[272,384]{1,0:T(8,128)(2,1)S(1)} %get-tuple-element.293), channel_id=1, source_target_pairs={{0,1},{1,0},{2,3},{3,2},{4,5},{5,4},{6,7},{7,6},{8,9},{9,8},{10,11... | collective-permute-start | bytes 626696 | tf_op jit(solution)/shard_map/ppermute | solution.py:447
  223.9 182.8 %reduce-scatter.5.cloned.1.call-start = ((), (), s32[]{:S(2)}) async-start(), calls=%async_computation.7 | async-start | bytes 1474560 | tf_op jit(solution)/shard_map/reduce_scatter | solution.py:840
  226.3 13.5 %collective-permute-start.25 = (bf16[288,384]{1,0:T(8,128)(2,1)}, bf16[288,384]{1,0:T(8,128)(2,1)S(1)}, u32[]{:S(2)}, u32[]{:S(2)}) collective-permute-start(bf16[288,384]{1,0:T(8,128)(2,1)} %copy-done.78), channel_id=1, source_target_pairs={{0,5},{1,4},{2,7},{3,6},{4,1},{5,0},{6,3},{7,2},{8,13},{9,12},{10,... | collective-permute-start | bytes 663560 | tf_op jit(solution)/shard_map/ppermute | solution.py:453
  231.5 11.5 %collective-permute-start.22 = (bf16[256,768]{1,0:T(8,128)(2,1)}, bf16[256,768]{1,0:T(8,128)(2,1)S(1)}, u32[]{:S(2)}, u32[]{:S(2)}) collective-permute-start(bf16[256,768]{1,0:T(8,128)(2,1)} %fusion.61), channel_id=1, source_target_pairs={{0,4},{4,0},{8,12},{12,8},{16,20},{20,16},{24,28},{28,24},{1,5},{5... | collective-permute-start | bytes 1179656 | tf_op jit(solution)/shard_map/ppermute | solution.py:445
  244.1 28.1 %collective-permute-start.23 = (bf16[512,768]{1,0:T(8,128)(2,1)S(1)}, bf16[512,768]{1,0:T(8,128)(2,1)S(1)}, u32[]{:S(2)}, u32[]{:S(2)}) collective-permute-start(bf16[512,768]{1,0:T(8,128)(2,1)S(1)} %pad_maximum_fusion.13), channel_id=1, source_target_pairs={{0,2},{1,3},{6,4},{7,5},{8,10},{9,11},{14,12},{15,13},{16,18},{17,... | collective-permute-start | bytes 2359304 | tf_op jit(solution)/shard_map/ppermute | solution.py:761
  277.5 9.7 %collective-permute-start.29 = (bf16[256,384]{1,0:T(8,128)(2,1)S(1)}, bf16[256,384]{1,0:T(8,128)(2,1)S(1)}, u32[]{:S(2)}, u32[]{:S(2)}) collective-permute-start(bf16[256,384]{1,0:T(8,128)(2,1)S(1)} %get-tuple-element.298), channel_id=1, source_target_pairs={{0,1},{1,0},{2,3},{3,2},{4,5},{5,4},{6,7},{7,6},{8,9},{9,8},{10,11... | collective-permute-start | bytes 589832 | tf_op jit(solution)/shard_map/ppermute | solution.py:447
  278.3 11.3 %collective-permute-start.28 = (bf16[256,384]{1,0:T(8,128)(2,1)S(1)}, bf16[256,384]{1,0:T(8,128)(2,1)S(1)}, u32[]{:S(2)}, u32[]{:S(2)}) collective-permute-start(bf16[256,384]{1,0:T(8,128)(2,1)S(1)} %get-tuple-element.299), channel_id=1, source_target_pairs={{0,5},{1,4},{2,7},{3,6},{4,1},{5,0},{6,3},{7,2},{8,13},{9,12},{10,... | collective-permute-start | bytes 589832 | tf_op jit(solution)/shard_map/ppermute | solution.py:453
  281.1 8.4 %collective-permute-start.27 = (bf16[256,384]{1,0:T(8,128)(2,1)S(1)}, bf16[256,384]{1,0:T(8,128)(2,1)S(1)}, u32[]{:S(2)}, u32[]{:S(2)}) collective-permute-start(bf16[256,384]{1,0:T(8,128)(2,1)S(1)} %get-tuple-element.300), channel_id=1, source_target_pairs={{0,4},{4,0},{8,12},{12,8},{16,20},{20,16},{24,28},{28,24},{1,5},{5... | collective-permute-start | bytes 589832 | tf_op jit(solution)/shard_map/ppermute | solution.py:445
  286.6 18.1 %collective-permute-start.38 = (bf16[1,4,96,768]{3,2,1,0:T(8,128)(2,1)S(1)}, bf16[1,4,96,768]{3,2,1,0:T(8,128)(2,1)S(1)}, u32[]{:S(2)}, u32[]{:S(2)}) collective-permute-start(bf16[1,4,96,768]{3,2,1,0:T(8,128)(2,1)S(1)} %dynamic-slice_bitcast_fusion.5), channel_id=1, source_target_pairs={{0,4},{4,0},{8,12},{12,8},{16,20},{20,16},{24,28},{28,24},{1,5},{5... | collective-permute-start | bytes 1769480 | tf_op jit(solution)/shard_map/ppermute | solution.py:445
  294.5 11.3 %collective-permute-start.37 = (bf16[2,4,96,768]{3,2,1,0:T(8,128)(2,1)S(1)}, bf16[2,4,96,768]{3,2,1,0:T(8,128)(2,1)S(1)}, u32[]{:S(2)}, u32[]{:S(2)}) collective-permute-start(bf16[2,4,96,768]{3,2,1,0:T(8,128)(2,1)S(1)} %fusion.66), channel_id=1, source_target_pairs={{0,4},{4,0},{8,12},{12,8},{16,20},{20,16},{24,28},{28,24},{1,5},{5... | collective-permute-start | bytes 3538952 | tf_op jit(solution)/shard_map/ppermute | solution.py:445
  300.0 42.8 %collective-permute-start.46 = (bf16[2,512,768]{2,1,0:T(8,128)(2,1)}, bf16[2,512,768]{2,1,0:T(8,128)(2,1)}, u32[]{:S(2)}, u32[]{:S(2)}) collective-permute-start(bf16[2,512,768]{2,1,0:T(8,128)(2,1)} %fusion.39), channel_id=1, source_target_pairs={{0,4},{4,0},{8,12},{12,8},{16,20},{20,16},{24,28},{28,24},{1,5},{5... | collective-permute-start | bytes 4718600 | tf_op jit(solution)/shard_map/ppermute | solution.py:445
  321.9 9.7 %collective-permute-start.34 = (bf16[2,256,768]{2,1,0:T(8,128)(2,1)}, bf16[2,256,768]{2,1,0:T(8,128)(2,1)}, u32[]{:S(2)}, u32[]{:S(2)}) collective-permute-start(bf16[2,256,768]{2,1,0:T(8,128)(2,1)} %fusion.88), channel_id=1, source_target_pairs={{0,4},{4,0},{8,12},{12,8},{16,20},{20,16},{24,28},{28,24},{1,5},{5... | collective-permute-start | bytes 2359304 | tf_op jit(solution)/shard_map/ppermute | solution.py:445
  335.0 22.3 %collective-permute-start.35 = (bf16[256,768]{1,0:T(8,128)(2,1)S(1)}, bf16[256,768]{1,0:T(8,128)(2,1)S(1)}, u32[]{:S(2)}, u32[]{:S(2)}) collective-permute-start(bf16[256,768]{1,0:T(8,128)(2,1)S(1)} %fusion.124), channel_id=1, source_target_pairs={{0,1},{1,0},{2,3},{3,2},{4,5},{5,4},{6,7},{7,6},{8,9},{9,8},{10,11... | collective-permute-start | bytes 1179656 | tf_op jit(solution)/shard_map/ppermute | solution.py:447
  339.3 31.5 %collective-permute-start.39 = (bf16[4,96,768]{2,1,0:T(8,128)(2,1)}, bf16[4,96,768]{2,1,0:T(8,128)(2,1)}, u32[]{:S(2)}, u32[]{:S(2)}) collective-permute-start(bf16[4,96,768]{2,1,0:T(8,128)(2,1)} %get-tuple-element.236), channel_id=1, source_target_pairs={{0,8},{4,12},{8,0},{12,4},{16,24},{20,28},{24,16},{28,20},{1,9},{5... | collective-permute-start | bytes 1769480 | tf_op jit(solution)/shard_map/ppermute | solution.py:445
  339.9 34.5 %collective-permute-start.41 = (bf16[4,96,768]{2,1,0:T(8,128)(2,1)}, bf16[4,96,768]{2,1,0:T(8,128)(2,1)}, u32[]{:S(2)}, u32[]{:S(2)}) collective-permute-start(bf16[4,96,768]{2,1,0:T(8,128)(2,1)} %get-tuple-element.237), channel_id=1, source_target_pairs={{0,24},{4,28},{8,16},{12,20},{16,8},{20,12},{24,0},{28,4},{1,25},{... | collective-permute-start | bytes 1769480 | tf_op jit(solution)/shard_map/ppermute | solution.py:445
  340.7 35.2 %collective-permute-start.40 = (bf16[4,96,768]{2,1,0:T(8,128)(2,1)}, bf16[4,96,768]{2,1,0:T(8,128)(2,1)}, u32[]{:S(2)}, u32[]{:S(2)}) collective-permute-start(bf16[4,96,768]{2,1,0:T(8,128)(2,1)} %get-tuple-element.238), channel_id=1, source_target_pairs={{0,16},{4,20},{8,24},{12,28},{16,0},{20,4},{24,8},{28,12},{1,17},{... | collective-permute-start | bytes 1769480 | tf_op jit(solution)/shard_map/ppermute | solution.py:445
  366.0 13.6 %collective-permute-start.42 = (bf16[1,4,96,768]{3,2,1,0:T(8,128)(2,1)S(1)}, bf16[1,4,96,768]{3,2,1,0:T(8,128)(2,1)S(1)}, u32[]{:S(2)}, u32[]{:S(2)}) collective-permute-start(bf16[1,4,96,768]{3,2,1,0:T(8,128)(2,1)S(1)} %dynamic-slice_bitcast_fusion.1), channel_id=1, source_target_pairs={{0,4},{4,0},{8,12},{12,8},{16,20},{20,16},{24,28},{28,24},{1,5},{5... | collective-permute-start | bytes 1769480 | tf_op jit(solution)/shard_map/ppermute | solution.py:445
  366.6 12.9 %collective-permute-start.43 = (bf16[4,96,768]{2,1,0:T(8,128)(2,1)S(1)}, bf16[4,96,768]{2,1,0:T(8,128)(2,1)S(1)}, u32[]{:S(2)}, u32[]{:S(2)}) collective-permute-start(bf16[4,96,768]{2,1,0:T(8,128)(2,1)S(1)} %dynamic-slice_bitcast_fusion), channel_id=1, source_target_pairs={{0,4},{4,0},{8,12},{12,8},{16,20},{20,16},{24,28},{28,24},{1,5},{5... | collective-permute-start | bytes 1769480 | tf_op jit(solution)/shard_map/ppermute | solution.py:445
  370.8 55.6 %collective-permute-start.47 = (bf16[2,512,768]{2,1,0:T(8,128)(2,1)}, bf16[2,512,768]{2,1,0:T(8,128)(2,1)}, u32[]{:S(2)}, u32[]{:S(2)}) collective-permute-start(bf16[2,512,768]{2,1,0:T(8,128)(2,1)} %fusion.9), channel_id=1, source_target_pairs={{2,4},{3,5},{4,2},{5,3},{10,12},{11,13},{12,10},{13,11},{18,20},{1... | collective-permute-start | bytes 4718600 | tf_op jit(solution)/shard_map/ppermute | solution.py:604
  374.4 34.8 %collective-permute-start.44 = (bf16[512,768]{1,0:T(8,128)(2,1)}, bf16[512,768]{1,0:T(8,128)(2,1)}, u32[]{:S(2)}, u32[]{:S(2)}) collective-permute-start(bf16[512,768]{1,0:T(8,128)(2,1)} %pad_maximum_fusion.14), channel_id=1, source_target_pairs={{0,2},{1,3},{6,4},{7,5},{8,10},{9,11},{14,12},{15,13},{16,18},{17,... | collective-permute-start | bytes 2359304 | tf_op jit(solution)/shard_map/ppermute | solution.py:761
  380.2 11.4 %collective-permute-start.48 = (bf16[3,96,768]{2,1,0:T(8,128)(2,1)S(1)}, bf16[3,96,768]{2,1,0:T(8,128)(2,1)S(1)}, u32[]{:S(2)}, u32[]{:S(2)}) collective-permute-start(bf16[3,96,768]{2,1,0:T(8,128)(2,1)S(1)} %get-tuple-element.250), channel_id=1, source_target_pairs={{0,8},{4,12},{8,0},{12,4},{16,24},{20,28},{24,16},{28,20},{1,9},{5... | collective-permute-start | bytes 1327112 | tf_op jit(solution)/shard_map/ppermute | solution.py:445
  380.8 22.4 %collective-permute-start.50 = (bf16[3,96,768]{2,1,0:T(8,128)(2,1)S(1)}, bf16[3,96,768]{2,1,0:T(8,128)(2,1)S(1)}, u32[]{:S(2)}, u32[]{:S(2)}) collective-permute-start(bf16[3,96,768]{2,1,0:T(8,128)(2,1)S(1)} %get-tuple-element.251), channel_id=1, source_target_pairs={{0,24},{4,28},{8,16},{12,20},{16,8},{20,12},{24,0},{28,4},{1,25},{... | collective-permute-start | bytes 1327112 | tf_op jit(solution)/shard_map/ppermute | solution.py:445
  383.2 22.4 %collective-permute-start.49 = (bf16[3,96,768]{2,1,0:T(8,128)(2,1)S(1)}, bf16[3,96,768]{2,1,0:T(8,128)(2,1)S(1)}, u32[]{:S(2)}, u32[]{:S(2)}) collective-permute-start(bf16[3,96,768]{2,1,0:T(8,128)(2,1)S(1)} %get-tuple-element.252), channel_id=1, source_target_pairs={{0,16},{4,20},{8,24},{12,28},{16,0},{20,4},{24,8},{28,12},{1,17},{... | collective-permute-start | bytes 1327112 | tf_op jit(solution)/shard_map/ppermute | solution.py:445
  391.6 118.4 %collective-permute-start.30 = (bf16[512,768]{1,0:T(8,128)(2,1)}, bf16[512,768]{1,0:T(8,128)(2,1)}, u32[]{:S(2)}, u32[]{:S(2)}) collective-permute-start(bf16[512,768]{1,0:T(8,128)(2,1)} %broadcast_select_fusion.3), channel_id=1, source_target_pairs={{0,1},{1,0},{2,3},{3,2},{4,5},{5,4},{6,7},{7,6},{8,9},{9,8},{10,11... | collective-permute-start | bytes 2359304 | tf_op jit(solution)/shard_map/ppermute | solution.py:447
  412.7 79.7 %collective-permute-start.45 = (bf16[512,768]{1,0:T(8,128)(2,1)}, bf16[512,768]{1,0:T(8,128)(2,1)}, u32[]{:S(2)}, u32[]{:S(2)}) collective-permute-start(bf16[512,768]{1,0:T(8,128)(2,1)} %select_select_fusion), channel_id=1, source_target_pairs={{0,1},{1,0},{2,3},{3,2},{4,5},{5,4},{6,7},{7,6},{8,9},{9,8},{10,11... | collective-permute-start | bytes 2359304 | tf_op jit(solution)/shard_map/ppermute | solution.py:447
  439.1 57.1 %all-to-all-start.1 = ((bf16[8,128,768]{2,1,0:T(8,128)(2,1)}), bf16[8,128,768]{2,1,0:T(8,128)(2,1)}, u32[]{:S(2)}, u32[]{:S(2)}) async-start(bf16[8,128,768]{2,1,0:T(8,128)(2,1)} %bitcast.418), calls=%async_computation.3 | async-start | bytes 3145728 | tf_op jit(solution)/shard_map/all_to_all | solution.py:886
  443.9 13.7 %collective-permute-start.51 = (bf16[96,768]{1,0:T(8,128)(2,1)}, bf16[96,768]{1,0:T(8,128)(2,1)}, u32[]{:S(2)}, u32[]{:S(2)}) collective-permute-start(bf16[96,768]{1,0:T(8,128)(2,1)} %fusion.162), channel_id=1, source_target_pairs={{0,2},{1,3},{2,0},{3,1},{4,6},{5,7},{6,4},{7,5},{8,10},{9,11},{10,... | collective-permute-start | bytes 442376 | tf_op jit(solution)/shard_map/ppermute | solution.py:447
  450.2 16.3 %collective-permute-start.52 = (bf16[2,6,96,192]{2,3,1,0:T(8,128)(2,1)}, bf16[2,6,96,192]{2,3,1,0:T(8,128)(2,1)}, u32[]{:S(2)}, u32[]{:S(2)}) collective-permute-start(bf16[2,6,96,192]{2,3,1,0:T(8,128)(2,1)} %bitcast.445), channel_id=1, source_target_pairs={{0,1},{1,0},{2,3},{3,2},{4,5},{5,4},{6,7},{7,6},{8,9},{9,8},{10,11... | collective-permute-start | bytes 1327112 | tf_op jit(solution)/shard_map/ppermute | solution.py:447
  468.2 15.6 %collective-permute-start.53 = (bf16[6,96,192]{1,2,0:T(8,128)(2,1)S(1)}, bf16[6,96,192]{1,2,0:T(8,128)(2,1)S(1)}, u32[]{:S(2)}, u32[]{:S(2)}) collective-permute-start(bf16[6,96,192]{1,2,0:T(8,128)(2,1)S(1)} %fusion.144), channel_id=1, source_target_pairs={{0,2},{1,3},{2,0},{3,1},{4,6},{5,7},{6,4},{7,5},{8,10},{9,11},{10,... | collective-permute-start | bytes 663560 | tf_op jit(solution)/shard_map/ppermute | solution.py:447
  511.5 8.1 %collective-permute-start.59 = (f32[2,2,14]{2,1,0:T(2,128)S(1)}, f32[2,2,14]{2,1,0:T(2,128)S(1)}, u32[]{:S(2)}, u32[]{:S(2)}) collective-permute-start(f32[2,2,14]{2,1,0:T(2,128)S(1)} %pad_maximum_fusion.36), channel_id=1, source_target_pairs={{0,1},{1,0},{2,3},{3,2},{4,5},{5,4},{6,7},{7,6},{8,9},{9,8},{10,11... | collective-permute-start | bytes 680 | tf_op jit(solution)/shard_map/ppermute | solution.py:447
  (132 other events, 932.5 us)
Sparse Core Ops, SparseCore 0:
  52.2 51.4 all-gather.2
  136.3 59.7 all-gather.4
  224.1 77.3 reduce-scatter.2
  325.2 35.6 reduce-scatter.4
